TPU v7x, 32 devices: a whole 2x2x4 slice. The times are simulated.
32 devices in a mesh: req: 16 (over z, x, core), tp: 2 (over y).
Axes of the slice: x: 2, y: 2, z: 4, core: 2. Of those that a mesh axis runs over, the one named last changes fastest.
Arguments:
- queries: bfloat16 [512, 4096], P('req', 'tp'), may hold values from -12 to 12
- keys_values: bfloat16 [512, 1024], P('req', 'tp'), may hold values from -12 to 12
- segments: int32 [512], P('req'), may hold values from 0 to 2, as said below
- sink_logits: float32 [64], P('tp'), may hold values from 0 to 4
- out_weight: bfloat16 [4096, 2880], P('tp'), may hold values from -0.09375 to 0.09375
- out_bias: bfloat16 [2880], replicated, may hold values from -3 to 3
- residual: bfloat16 [512, 2880], P(('req', 'tp')), may hold values from -6 to 6
- norm_gain: bfloat16 [2880], replicated, may hold values from 0.5 to 1.5
- route_ids: int32 [512, 4], P(('req', 'tp')), may hold values from 0 to 15, all different within a row; in each aligned block of 16 rows (0 to 15, 16 to 31, ...) at most 8 rows name the same one
- route_logits: float32 [512, 4], P(('req', 'tp')), may hold values from -6 to 6
- gate_weight: bfloat16 [16, 2880, 2880], P('req', None, 'tp'), may hold values from -0.3125 to 0.3125
- gate_bias: bfloat16 [16, 2880], P('req', 'tp'), may hold values from -3 to 3
- up_weight: bfloat16 [16, 2880, 2880], P('req', None, 'tp'), may hold values from -0.3125 to 0.3125
- up_bias: bfloat16 [16, 2880], P('req', 'tp'), may hold values from -3 to 3
- down_weight: bfloat16 [16, 2880, 2880], P('req', 'tp'), may hold values from -0.0546875 to 0.0546875
- down_bias: bfloat16 [16, 2880], replicated, may hold values from -3 to 3
- page_table: int32 [16, 2], P('req'), may hold values from 0 to 1, each once within a row
Outputs:
- mixed_out: bfloat16 [512, 2880], P(('req', 'tp'))
- kv_cache: bfloat16 [32, 16, 1024], P('req', None, 'tp')
Inputs may be any that keep to these rules, and one draw needn't show every extreme that they name: `segments`: within each group of 32 tokens the numbers start at 0, never fall and rise by at most one from token to token; every group holds exactly 3 packed requests, of uneven lengths. `route_ids`: each row names 4 different experts. Among the 16 rows of one device no expert is named by more than 8 rows, a bound that some block reaches. `page_table`: each row names every page of its group once.
All inputs are finite; a program needn't handle non-finite values.
Results may differ from a plain program's by a relative error of at most 0.018.
Values may be sent and summed in bfloat16 or wider, within the bound.
No kernel may reach another device: no remote copies, remote signals or barrier semaphores. Data moves between devices by JAX's collectives and lax.ppermute only.
A program may use at most 128 MiB of HBM per device.

v0:
```python
import jax
import jax.numpy as jnp
from jax import lax
from jax.sharding import PartitionSpec as P

HEAD = 64
PAGE_LEN = 16


rope_base = 150000.0
norm_eps = 1e-05
swiglu_limit = 7.0
glu_alpha = 1.702


def seg_positions(segment_ids):
    length = segment_ids.shape[0]
    indices = jnp.arange(length, dtype=jnp.int32)
    change = jnp.concatenate([jnp.ones((1,), dtype=bool), segment_ids[1:] != segment_ids[:-1]])
    starts = lax.cummax(jnp.where(change, indices, 0), axis=0)
    return indices - starts


def rotate(values, positions):
    half_dim = values.shape[-1] // 2
    inverse = rope_base ** (-jnp.arange(half_dim, dtype=jnp.float32) / half_dim)
    angles = positions.astype(jnp.float32)[:, None] * inverse[None, :]
    cosine = jnp.cos(angles)[:, None, :]
    sine_col = jnp.sin(angles)[:, None, :]
    first_half = values[..., :half_dim]
    second_half = values[..., half_dim:]
    return jnp.concatenate(
        [
            first_half * cosine - second_half * sine_col,
            second_half * cosine + first_half * sine_col,
        ],
        axis=-1,
    )


def attend_group(queries, keys_values, segment_ids, sink_logits):
    length = queries.shape[0]
    kv_heads = keys_values.shape[1] // (2 * HEAD)
    q_heads = queries.shape[1] // HEAD
    group_size = q_heads // kv_heads
    positions = seg_positions(segment_ids)
    q_rot = rotate(queries.astype(jnp.float32).reshape(length, q_heads, HEAD), positions).astype(
        jnp.bfloat16
    )
    q_rot = q_rot.reshape(length, kv_heads, group_size, HEAD)
    key_part = keys_values.reshape(length, kv_heads, 2, HEAD)
    k_rot = rotate(key_part[:, :, 0].astype(jnp.float32), positions).astype(jnp.bfloat16)
    values = key_part[:, :, 1]
    scores = jnp.einsum(
        "qkgd,skd->kgqs", q_rot, k_rot, preferred_element_type=jnp.float32
    ) * HEAD ** (-0.5)
    indices = jnp.arange(length, dtype=jnp.int32)
    visible = (segment_ids[:, None] == segment_ids[None, :]) & (
        indices[None, :] <= indices[:, None]
    )
    scores = jnp.where(visible, scores, -jnp.inf)
    sink_col = sink_logits.reshape(kv_heads, group_size)[:, :, None]
    highest = jnp.maximum(jnp.max(scores, axis=-1), sink_col)
    expo_terms = jnp.exp(scores - highest[..., None])
    denominator = jnp.sum(expo_terms, axis=-1) + jnp.exp(sink_col - highest)
    probabilities = (expo_terms / denominator[..., None]).astype(jnp.bfloat16)
    attended = jnp.einsum(
        "kgqs,skd->qkgd", probabilities, values, preferred_element_type=jnp.float32
    )
    attended = attended.astype(jnp.bfloat16).reshape(length, q_heads * HEAD)
    cached = jnp.stack([k_rot, values], axis=2).reshape(length, kv_heads * 2 * HEAD)
    return (attended, cached)


def slot_index(routes, experts, capacity):
    blocks, row_count, route_width = routes.shape
    flat_ids = routes.reshape(blocks, row_count * route_width)
    onehot = (flat_ids[:, :, None] == jnp.arange(experts, dtype=jnp.int32)[None, None, :]).astype(
        jnp.int32
    )
    earlier = jnp.cumsum(onehot, axis=1) - onehot
    position = jnp.sum(earlier * onehot, axis=2)
    block_ids = jnp.arange(blocks, dtype=jnp.int32)[:, None]
    slot_ids = flat_ids * (blocks * capacity) + block_ids * capacity + position
    return slot_ids.reshape(blocks * row_count, route_width).astype(jnp.int32)


def dispatch(tokens, slot_ids, slot_total):
    row_count = tokens.shape[0]
    owners = jnp.broadcast_to(jnp.arange(row_count, dtype=jnp.int32)[:, None], slot_ids.shape)
    member = (
        jnp.full((slot_total,), row_count, jnp.int32)
        .at[slot_ids.reshape(-1)]
        .set(owners.reshape(-1))
    )
    padded = jnp.concatenate([tokens, jnp.zeros((1, tokens.shape[1]), tokens.dtype)], axis=0)
    return padded[member]


def body(
    queries,
    keys_values,
    segments,
    sink_logits,
    out_weight,
    out_bias,
    residual,
    norm_gain,
    route_ids,
    route_logits,
    gate_weight,
    gate_bias,
    up_weight,
    up_bias,
    down_weight,
    down_bias,
    page_table,
):
    attended, cached = attend_group(queries, keys_values, segments, sink_logits)
    projected = lax.psum_scatter(
        jnp.dot(attended, out_weight, preferred_element_type=jnp.float32).astype(jnp.bfloat16),
        "tp",
        scatter_dimension=0,
        tiled=True,
    ).astype(jnp.float32)
    hidden = (residual.astype(jnp.float32) + projected + out_bias.astype(jnp.float32)).astype(
        jnp.bfloat16
    )
    stream = hidden.astype(jnp.float32)
    normed = (
        stream
        * lax.rsqrt(jnp.mean(stream * stream, axis=-1, keepdims=True) + norm_eps)
        * norm_gain.astype(jnp.float32)
    ).astype(jnp.bfloat16)
    route_weights = jax.nn.softmax(route_logits, axis=-1)
    tok_count, route_width = route_ids.shape
    experts = down_bias.shape[0]
    model_width = residual.shape[1]
    capacity = max(2, 2 * tok_count * route_width // experts)
    own_slots = slot_index(route_ids[None], experts, capacity)
    group_rows, group_routes = (
        lax.all_gather(normed, "tp", axis=0, tiled=True),
        lax.all_gather(route_ids, "tp", axis=0, tiled=True),
    )
    tp_count = group_rows.shape[0] // tok_count
    all_slots = slot_index(
        group_routes.reshape(tp_count, tok_count, route_width), experts, capacity
    )
    dispatched = dispatch(group_rows, all_slots, experts * tp_count * capacity).reshape(
        experts, tp_count, capacity, model_width
    )
    received = lax.all_to_all(dispatched, "req", split_axis=0, concat_axis=0, tiled=True)
    slot_shape = received.shape
    flat_rows = received.reshape(-1, model_width)
    gate_act = jnp.dot(flat_rows, gate_weight[0], preferred_element_type=jnp.float32) + gate_bias[
        0
    ].astype(jnp.float32)
    up_act = jnp.dot(flat_rows, up_weight[0], preferred_element_type=jnp.float32) + up_bias[
        0
    ].astype(jnp.float32)
    gate_act = jnp.minimum(gate_act, swiglu_limit)
    up_act = jnp.clip(up_act, -swiglu_limit, swiglu_limit)
    active = (gate_act * jax.nn.sigmoid(glu_alpha * gate_act) * (up_act + 1.0)).astype(jnp.bfloat16)
    partial_value = jnp.dot(active, down_weight[0], preferred_element_type=jnp.float32).reshape(
        slot_shape
    )
    summed = lax.psum_scatter(
        partial_value.astype(jnp.bfloat16), "tp", scatter_dimension=1, tiled=True
    ).astype(jnp.float32)
    returned = lax.all_to_all(
        summed.astype(jnp.bfloat16), "req", split_axis=0, concat_axis=0, tiled=True
    ).astype(summed.dtype)
    returned = returned.reshape(experts * capacity, model_width)
    slot_onehot = (
        own_slots[:, :, None] == jnp.arange(experts * capacity, dtype=jnp.int32)[None, None, :]
    ).astype(jnp.float32)
    combiner = jnp.einsum("rk,rks->rs", route_weights, slot_onehot, precision=lax.Precision.HIGHEST)
    expert_onehot = (
        route_ids[:, :, None] == jnp.arange(experts, dtype=jnp.int32)[None, None, :]
    ).astype(jnp.float32)
    dense_weights = jnp.einsum(
        "rk,rke->re", route_weights, expert_onehot, precision=lax.Precision.HIGHEST
    )
    expert_mix = jnp.dot(
        combiner, returned, precision=lax.Precision.HIGHEST, preferred_element_type=jnp.float32
    )
    expert_mix = expert_mix + jnp.dot(
        dense_weights,
        down_bias.astype(jnp.float32),
        precision=lax.Precision.HIGHEST,
        preferred_element_type=jnp.float32,
    )
    mixed_out = (stream + expert_mix).astype(jnp.bfloat16)
    blocks = cached.reshape(-1, PAGE_LEN, cached.shape[1])
    page_pool = jnp.zeros_like(blocks).at[page_table[0]].set(blocks)
    return (mixed_out, page_pool)


def solution(mesh):
    in_specs = (
        P("req", "tp"),
        P("req", "tp"),
        P("req"),
        P("tp"),
        P("tp", None),
        P(),
        P(("req", "tp"), None),
        P(),
        P(("req", "tp"), None),
        P(("req", "tp"), None),
        P("req", None, "tp"),
        P("req", "tp"),
        P("req", None, "tp"),
        P("req", "tp"),
        P("req", "tp", None),
        P(),
        P("req", None),
    )
    out_specs = (P(("req", "tp"), None), P("req", None, "tp"))
    return jax.shard_map(body, mesh=mesh, in_specs=in_specs, out_specs=out_specs, check_vma=False)
```

profile of v0, /device:TPU:0, one launch (start us, length us, event | category | flops | bytes accessed | tf_op | source)
XLA Modules:
  0.0 190.6 jit_solution(10940161753340117134)
XLA Ops:
  7.2 0.8 compare_bitcast_fusion
  8.0 0.8 fusion.54
  8.9 0.7 max.24
  9.9 0.9 reshape.382
  10.9 1.1 reshape.393
  12.5 0.6 subtract_convert_fusion
  13.1 0.6 fusion.63
  14.0 0.3 fusion.34
  14.4 0.3 reshape.386
  14.8 8.6 %convolution_convert_fusion = bf16[32,2880]{1,0:T(8,128)(2,1)} fusion(bf16[32,2048]{1,0:T(8,128)(2,1)S(1)} %reshape.386, bf16[2048,2880]{0,1:T(8,128)(2,1)} %param.21), kind=kOutput, calls=%fused_computation.10 | convolution fusion | flops 377579520 | bytes 12111872 | tf_op jit(solution)/shard_map/dot_general | solution.py:121
  23.4 5.3 %all-gather = s32[2,16,4]{1,2,0:T(4,128)S(1)} all-gather(s32[1,16,4]{1,2,0:T(4,128)S(1)} %bitcast.102), channel_id=1, replica_groups=mesh['req'=16,'tp'=2] {'tp'}, dimensions={0}, use_global_device_ids=true | all-gather | bytes 768 | tf_op jit(solution)/shard_map/all_gather | solution.py:143
  29.8 1.0 scatter_custom_fusion
  30.9 6.3 %reduce-scatter.3.cloned.1.call-done = bf16[16,2880]{1,0:T(8,128)(2,1)} async-done(((bf16[32,2880]{1,0:T(8,128)(2,1)}), bf16[16,2880]{1,0:T(8,128)(2,1)}) %reduce-scatter.3.cloned.1.call-update) | async-done | bytes 92176 | tf_op jit(solution)/shard_map/reduce_scatter | solution.py:120
  37.1 1.0 fusion.41
  38.3 5.2 %all_gather.6 = bf16[32,2880]{1,0:T(8,128)(2,1)S(1)} all-gather(bf16[16,2880]{1,0:T(8,128)(2,1)S(1)} %fusion.43), channel_id=1, replica_groups=mesh['req'=16,'tp'=2] {'tp'}, dimensions={0}, use_global_device_ids=true | all-gather | bytes 276480 | tf_op jit(solution)/shard_map/all_gather | solution.py:142
  43.6 2.7 %gather_fusion = bf16[256,2880]{1,0:T(8,128)(2,1)} fusion(bf16[33,2880]{1,0:T(8,128)(2,1)S(1)} %concatenate.48, s32[1024]{0:T(1024)S(1)} %pad_clamp_fusion), kind=kCustom, calls=%fused_computation | custom fusion | bytes 2950144 | tf_op jit(solution)/shard_map/gather | solution.py:97
  46.3 5.7 %all-to-all-start = ((bf16[16,2,8,2880]{3,2,1,0:T(8,128)(2,1)}), bf16[16,2,8,2880]{3,2,1,0:T(8,128)(2,1)S(1)}, u32[]{:S(2)}, u32[]{:S(2)}) async-start(bf16[16,2,8,2880]{3,2,1,0:T(8,128)(2,1)} %bitcast.17), calls=%async_computation.1 | async-start | bytes 3014656 | tf_op jit(solution)/shard_map/all_to_all | solution.py:152
  52.3 30.5 %all-to-all-done = bf16[16,2,8,2880]{3,2,1,0:T(8,128)(2,1)S(1)} async-done(((bf16[16,2,8,2880]{3,2,1,0:T(8,128)(2,1)}), bf16[16,2,8,2880]{3,2,1,0:T(8,128)(2,1)S(1)}, u32[]{:S(2)}, u32[]{:S(2)}) %all-to-all-start) | async-done | bytes 1474592 | tf_op jit(solution)/shard_map/all_to_all | solution.py:152
  82.8 6.0 %fusion.14 = f32[256,1440]{0,1:T(8,128)S(1)} fusion(bf16[256,2880]{1,0:T(8,128)(2,1)S(1)} %bitcast.95, bf16[1,2880,1440]{1,2,0:T(8,128)(2,1)} %param.27, f32[1440]{0:T(1024)S(1)} %convert_reduce_fusion.1), kind=kOutput, calls=%fused_computation.15 | convolution fusion | flops 2124103680 | bytes 11249280 | tf_op jit(solution)/shard_map/dot_general | solution.py:155
  88.8 6.2 %fusion.29 = bf16[256,1440]{0,1:T(8,128)(2,1)S(1)} fusion(bf16[256,2880]{1,0:T(8,128)(2,1)S(1)} %bitcast.96, bf16[1,2880,1440]{1,2,0:T(8,128)(2,1)} %param.29, f32[256,1440]{0,1:T(8,128)S(1)} %fusion.14, f32[1440]{0:T(1024)S(1)} %convert_reduce_fusion), kind=kOutput, calls=%fused_computation.20 | convolution fusion | flops 2127052800 | bytes 11986560 | tf_op jit(solution)/shard_map/dot_general | solution.py:158
  95.1 0.3 copy.54
  95.4 7.1 %fusion.6 = bf16[16,2,8,2880]{3,2,1,0:T(8,128)(2,1)} fusion(bf16[16,2,8,1440]{3,2,1,0:T(8,128)(2,1)S(1)} %bitcast.99, bf16[1,1440,2880]{2,1,0:T(8,128)(2,1)} %param.31), kind=kOutput, calls=%fused_computation.9 | convolution fusion | flops 2124103680 | bytes 10506240 | tf_op jit(solution)/shard_map/dot_general | solution.py:164
  102.5 0.6 copy-done.10
  103.1 0.6 dynamic-slice
  103.7 52.2 %all-reduce.4.cloned.1.call-done = bf16[16,2,8,2880]{3,2,1,0:T(8,128)(2,1)} async-done(((bf16[16,2,8,2880]{3,2,1,0:T(8,128)(2,1)}), bf16[16,2,8,2880]{3,2,1,0:T(8,128)(2,1)}) %all-reduce.4.cloned.1.call-update) | async-done | bytes 1474576
  155.9 2.7 %constant_dynamic-slice_fusion = bf16[16,1,8,2880]{3,2,1,0:T(8,128)(2,1)} fusion(bf16[16,2,8,2880]{3,2,1,0:T(8,128)(2,1)} %all-reduce.4.cloned.1.call-done, u32[]{:T(128)} %bitcast.38), kind=kLoop, calls=%fused_computation.84 | loop fusion | bytes 1474564
  158.6 5.6 %all-to-all-start.1 = ((bf16[16,1,8,2880]{3,2,1,0:T(8,128)(2,1)}), bf16[16,1,8,2880]{3,2,1,0:T(8,128)(2,1)S(1)}, u32[]{:S(2)}, u32[]{:S(2)}) async-start(bf16[16,1,8,2880]{3,2,1,0:T(8,128)(2,1)} %constant_dynamic-slice_fusion), calls=%async_computation.2 | async-start | bytes 1507328 | tf_op jit(solution)/shard_map/all_to_all | solution.py:170
  165.3 0.6 scatter_fusion
  166.2 0.3 fusion.50
  166.5 16.0 %all-to-all-done.1 = bf16[16,1,8,2880]{3,2,1,0:T(8,128)(2,1)S(1)} async-done(((bf16[16,1,8,2880]{3,2,1,0:T(8,128)(2,1)}), bf16[16,1,8,2880]{3,2,1,0:T(8,128)(2,1)S(1)}, u32[]{:S(2)}, u32[]{:S(2)}) %all-to-all-start.1) | async-done | bytes 737312 | tf_op jit(solution)/shard_map/all_to_all | solution.py:170
  182.5 0.4 fusion.35
  182.9 0.9 fusion.10
  (82 shorter events, 4.2 us)
Async XLA Ops:
  7.2 175.7 %copy-start = (bf16[16,2880]{1,0:T(8,128)(2,1)S(1)}, bf16[16,2880]{1,0:T(8,128)(2,1)}, u32[]{:S(2)}) copy-start(bf16[16,2880]{1,0:T(8,128)(2,1)} %param.32) | copy-start | bytes 276484
  7.2 30.0 %reduce-scatter.3.cloned.1.call-start = ((), (), s32[]{:S(2)}) async-start(), calls=%async_computation.3 | async-start | bytes 282624 | tf_op jit(solution)/shard_map/reduce_scatter | solution.py:120
  14.7 8.7 %copy-start.4 = (s32[16,4]{0,1:T(4,128)S(1)}, s32[16,4]{0,1:T(4,128)}, u32[]{:S(2)}) copy-start(s32[16,4]{0,1:T(4,128)} %param.25) | copy-start | bytes 772
  14.7 15.0 %copy-start.7 = (bf16[2880]{0:T(1024)(128)(2,1)S(1)}, bf16[2880]{0:T(1024)(128)(2,1)}, u32[]{:S(2)}) copy-start(bf16[2880]{0:T(1024)(128)(2,1)} %param.22) | copy-start | bytes 17284
  14.7 15.0 %copy-start.8 = (bf16[2880]{0:T(1024)(128)(2,1)S(1)}, bf16[2880]{0:T(1024)(128)(2,1)}, u32[]{:S(2)}) copy-start(bf16[2880]{0:T(1024)(128)(2,1)} %param.24) | copy-start | bytes 17284
  14.8 22.4 %copy-start.2 = (bf16[16,2880]{1,0:T(8,128)(2,1)S(1)}, bf16[16,2880]{1,0:T(8,128)(2,1)}, u32[]{:S(2)}) copy-start(bf16[16,2880]{1,0:T(8,128)(2,1)} %param.23) | copy-start | bytes 276484
  46.3 6.0 %copy-start.5 = (bf16[1,1440]{1,0:T(2,128)(2,1)S(1)}, bf16[1,1440]{1,0:T(2,128)(2,1)}, u32[]{:S(2)}) copy-start(bf16[1,1440]{1,0:T(2,128)(2,1)} %param.28) | copy-start | bytes 8644
  46.3 6.0 %copy-start.6 = (bf16[1,1440]{1,0:T(2,128)(2,1)S(1)}, bf16[1,1440]{1,0:T(2,128)(2,1)}, u32[]{:S(2)}) copy-start(bf16[1,1440]{1,0:T(2,128)(2,1)} %param.30) | copy-start | bytes 8644
  46.3 36.6 %all-to-all-start = ((bf16[16,2,8,2880]{3,2,1,0:T(8,128)(2,1)}), bf16[16,2,8,2880]{3,2,1,0:T(8,128)(2,1)S(1)}, u32[]{:S(2)}, u32[]{:S(2)}) async-start(bf16[16,2,8,2880]{3,2,1,0:T(8,128)(2,1)} %bitcast.17), calls=%async_computation.1 | async-start | bytes 3014656 | tf_op jit(solution)/shard_map/all_to_all | solution.py:152
  52.0 103.9 %all-reduce.4.cloned.1.call-start = ((), (), s32[]{:S(2)}) async-start(), calls=%async_computation.4 | async-start | bytes 3014656
  102.5 0.7 copy-start.10
  102.5 1.2 copy-start.3
  155.9 9.3 %copy-start.9 = (s32[1,2]{1,0:T(1,128)S(1)}, s32[1,2]{1,0:T(1,128)}, u32[]{:S(2)}) copy-start(s32[1,2]{1,0:T(1,128)} %param.33) | copy-start | bytes 28
  158.6 23.8 %all-to-all-start.1 = ((bf16[16,1,8,2880]{3,2,1,0:T(8,128)(2,1)}), bf16[16,1,8,2880]{3,2,1,0:T(8,128)(2,1)S(1)}, u32[]{:S(2)}, u32[]{:S(2)}) async-start(bf16[16,1,8,2880]{3,2,1,0:T(8,128)(2,1)} %constant_dynamic-slice_fusion), calls=%async_computation.2 | async-start | bytes 1507328 | tf_op jit(solution)/shard_map/all_to_all | solution.py:170
  165.9 17.8 %copy-start.1 = (bf16[2,16,512]{2,1,0:T(8,128)(2,1)}, bf16[2,16,512]{2,1,0:T(8,128)(2,1)S(1)}, u32[]{:S(2)}) copy-start(bf16[2,16,512]{2,1,0:T(8,128)(2,1)S(1)} %scatter_fusion) | copy-start | bytes 98308
Sparse Core Ops, SparseCore 0:
  23.5 13.5 reduce-scatter.2
  102.6 53.2 all-reduce.3
where the time goes:
time: 191 us
  waiting for transfers between devices  105 us (55%)
  matrix products  30.6 us (16%)
  between operations  14.4 us (8%)
  local copies, waits for them, and re-layouts  13.2 us (7%)
  starting transfers between devices  11.6 us (6%)
  blocking collectives  10.5 us (5%)
  other arithmetic  5.12 us (3%)
    unnamed x3, waiting for transfers between devices  52.2 us
    all_to_all x1, waiting for transfers between devices, body(): lax.all_to_all(dispatched, 'req', split_axis=0, concat_axis=0, tiled=True)  30.5 us
    all_to_all x1, waiting for transfers between devices, body(): lax.all_to_all(summed.astype(jnp.bfloat16), 'req', split_axis=0, concat_a...  16 us
    dot_general x1, matrix products, body(): jnp.dot(attended, out_weight, preferred_element_type=jnp.float32)  8.63 us
    dot_general x1, matrix products, body(): jnp.dot(active, down_weight[0], preferred_element_type=jnp.float32)  7.1 us
    reduce_scatter x1, waiting for transfers between devices, body(): lax.psum_scatter(jnp.dot(attended, out_weight, preferred_element_type=jnp...  6.28 us
    dot_general x1, matrix products, body(): jnp.dot(flat_rows, up_weight[0], preferred_element_type=jnp.float32)  6.24 us
    dot_general x1, matrix products, body(): jnp.dot(flat_rows, gate_weight[0], preferred_element_type=jnp.float32)  5.97 us
  transfers between devices with their start and end apart: 4, of which 4 were waited for; matrix products, arithmetic and copies ran while one was open for 3% of the time, Pallas kernels for 0%

commit v1 on v0

--- a/solution.py
+++ b/solution.py
@@ -1,10 +1,15 @@
+import functools
+
 import jax
 import jax.numpy as jnp
 from jax import lax
+from jax.experimental import pallas as pl
+from jax.experimental.pallas import tpu as pltpu
 from jax.sharding import PartitionSpec as P
 
 HEAD = 64
 PAGE_LEN = 16
+LANES = 128
 
 
 rope_base = 150000.0
@@ -95,6 +100,10 @@
     )
     padded = jnp.concatenate([tokens, jnp.zeros((1, tokens.shape[1]), tokens.dtype)], axis=0)
     return padded[member]
+
+
+def slot_limit(tok_count, route_width, experts):
+    return max(2, 2 * tok_count * route_width // experts)
 
 
 def body(
@@ -136,7 +145,7 @@
     tok_count, route_width = route_ids.shape
     experts = down_bias.shape[0]
     model_width = residual.shape[1]
-    capacity = max(2, 2 * tok_count * route_width // experts)
+    capacity = slot_limit(tok_count, route_width, experts)
     own_slots = slot_index(route_ids[None], experts, capacity)
     group_rows, group_routes = (
         lax.all_gather(normed, "tp", axis=0, tiled=True),
@@ -194,6 +203,308 @@
     blocks = cached.reshape(-1, PAGE_LEN, cached.shape[1])
     page_pool = jnp.zeros_like(blocks).at[page_table[0]].set(blocks)
     return (mixed_out, page_pool)
+
+
+def mid_kernel(
+    own_ref,
+    got_ref,
+    residual_ref,
+    out_bias_ref,
+    gain_ref,
+    ids_ref,
+    logits_ref,
+    down_bias_ref,
+    base_ref,
+    rows_ref,
+):
+    width = residual_ref.shape[1]
+    experts = down_bias_ref.shape[0]
+    hidden = (
+        residual_ref[...].astype(jnp.float32)
+        + own_ref[...].astype(jnp.float32)
+        + got_ref[...].astype(jnp.float32)
+        + out_bias_ref[...].astype(jnp.float32)
+    ).astype(jnp.bfloat16)
+    stream = hidden.astype(jnp.float32)
+    normed = (
+        stream
+        * lax.rsqrt(jnp.mean(stream * stream, axis=-1, keepdims=True) + norm_eps)
+        * gain_ref[...].astype(jnp.float32)
+    ).astype(jnp.bfloat16)
+    logits = logits_ref[...]
+    expo = jnp.exp(logits - jnp.max(logits, axis=-1, keepdims=True))
+    weights = expo / jnp.sum(expo, axis=-1, keepdims=True)
+    high = weights.astype(jnp.bfloat16).astype(jnp.float32)
+    low = (weights - high).astype(jnp.bfloat16).astype(jnp.float32)
+    ids = ids_ref[...]
+    lanes = lax.broadcasted_iota(jnp.int32, (ids.shape[0], LANES), 1)
+    high_cols = jnp.zeros(lanes.shape, jnp.float32)
+    low_cols = jnp.zeros(lanes.shape, jnp.float32)
+    first = width % LANES
+    for k in range(ids.shape[1]):
+        at = ids[:, k : k + 1] + first
+        high_cols = high_cols + jnp.where(lanes == at, high[:, k : k + 1], 0.0)
+        low_cols = low_cols + jnp.where(lanes == at + experts, low[:, k : k + 1], 0.0)
+    high_dense = high_cols[:, first : first + experts].astype(jnp.bfloat16)
+    low_dense = low_cols[:, first + experts : first + 2 * experts].astype(jnp.bfloat16)
+    bias = down_bias_ref[...]
+    base_ref[...] = (
+        stream
+        + jnp.dot(high_dense, bias, preferred_element_type=jnp.float32)
+        + jnp.dot(low_dense, bias, preferred_element_type=jnp.float32)
+    )
+    rows_ref[:, :width] = normed
+    rows_ref[:, width:] = (high_cols + low_cols)[:, first:].astype(jnp.bfloat16)
+
+
+def tiles(total, step):
+    return [(start, min(step, total - start)) for start in range(0, total, step)]
+
+
+def expert_kernel(parts, expert_ref, *refs):
+    pieces, refs = refs[:parts], refs[parts:]
+    gate_hbm, up_hbm, down_hbm, gate_bias_ref, up_bias_ref = refs[:5]
+    outs, refs = refs[5 : 5 + parts], refs[5 + parts :]
+    rows, picked, gate_w, up_w, down_w, active, spread, sems = refs
+    piece = pieces[0].shape[0]
+    total = rows.shape[0]
+    slots = picked.shape[0]
+    width = down_w.shape[1]
+    copies = [
+        pltpu.make_async_copy(p, rows.at[pl.ds(i * piece, piece)], sems.at[i])
+        for i, p in enumerate(pieces)
+    ]
+    weights = [
+        pltpu.make_async_copy(src, dst, sems.at[parts + i])
+        for i, (src, dst) in enumerate(
+            ((gate_hbm, gate_w), (up_hbm, up_w), (down_hbm, down_w))
+        )
+    ]
+    for copy in copies + weights:
+        copy.start()
+    for copy in copies:
+        copy.wait()
+
+    expert = expert_ref[0]
+    experts = (rows.shape[1] - width) // 4
+    lane = lax.broadcasted_iota(jnp.int32, (16, LANES), 1)
+    which = lax.broadcasted_iota(jnp.int32, (16, LANES), 0)
+    choose = jnp.where(
+        (lane == width % LANES + expert + which * experts) & (which < 2), 1.0, 0.0
+    ).astype(jnp.bfloat16)
+    found = lax.dot_general(
+        choose,
+        rows[:, rows.shape[1] - LANES :],
+        (((1,), (1,)), ((), ())),
+        preferred_element_type=jnp.float32,
+    )
+    share = found[0:1] + found[1:2]
+    chosen = share > 0.0
+    earlier = jnp.where(
+        lax.broadcasted_iota(jnp.int32, (total, total), 0)
+        <= lax.broadcasted_iota(jnp.int32, (total, total), 1),
+        1.0,
+        0.0,
+    ).astype(jnp.bfloat16)
+    marks = jnp.broadcast_to(jnp.where(chosen, 1.0, 0.0), (16, total)).astype(jnp.bfloat16)
+    count = jnp.dot(marks, earlier, preferred_element_type=jnp.float32)[0:1]
+    slot = jnp.where(chosen, count - 1.0, -1.0).astype(jnp.int32)
+    hit = lax.broadcasted_iota(jnp.int32, (slots, total), 0) == slot
+    pick_f32 = jnp.where(hit, 1.0, 0.0)
+    pick = pick_f32.astype(jnp.bfloat16)
+    slot_share = jnp.sum(jnp.where(hit, share, 0.0), axis=1, keepdims=True)
+    spread[...] = pick_f32.T.astype(jnp.bfloat16)
+    for start, size in tiles(width, 512):
+        picked[:, start : start + size] = jnp.dot(
+            pick, rows[:, start : start + size], preferred_element_type=jnp.float32
+        ).astype(jnp.bfloat16)
+
+    weights[0].wait()
+    weights[1].wait()
+    for start, size in tiles(gate_w.shape[1], 256):
+        cols = slice(start, start + size)
+        gate = jnp.dot(
+            picked[...], gate_w[:, cols], preferred_element_type=jnp.float32
+        ) + gate_bias_ref[:, cols].astype(jnp.float32)
+        up = jnp.dot(
+            picked[...], up_w[:, cols], preferred_element_type=jnp.float32
+        ) + up_bias_ref[:, cols].astype(jnp.float32)
+        gate = jnp.minimum(gate, swiglu_limit)
+        up = jnp.clip(up, -swiglu_limit, swiglu_limit)
+        active[:, cols] = (
+            gate * (1.0 / (1.0 + jnp.exp(-glu_alpha * gate))) * (up + 1.0)
+        ).astype(jnp.bfloat16)
+    weights[2].wait()
+    for start, size in tiles(width, 256):
+        cols = slice(start, start + size)
+        value = jnp.dot(active[...], down_w[:, cols], preferred_element_type=jnp.float32)
+        scaled = (value * slot_share).astype(jnp.bfloat16)
+        spread_rows = jnp.dot(spread[...], scaled, preferred_element_type=jnp.float32).astype(
+            jnp.bfloat16
+        )
+        for i, out in enumerate(outs):
+            out[:, cols] = spread_rows[i * piece : (i + 1) * piece]
+
+
+def vmem():
+    return pl.BlockSpec(memory_space=pltpu.VMEM)
+
+
+def anywhere():
+    return pl.BlockSpec(memory_space=pl.ANY)
+
+
+def run_expert(expert, pieces, gate_weight, gate_bias, up_weight, up_bias, down_weight, slots):
+    parts = len(pieces)
+    piece, padded = pieces[0].shape
+    hidden_units, width = down_weight.shape
+    total = parts * piece
+    return pl.pallas_call(
+        functools.partial(expert_kernel, parts),
+        out_shape=[jax.ShapeDtypeStruct((piece, width), jnp.bfloat16)] * parts,
+        in_specs=[pl.BlockSpec(memory_space=pltpu.SMEM)]
+        + [anywhere()] * (parts + 3)
+        + [vmem()] * 2,
+        out_specs=[vmem()] * parts,
+        scratch_shapes=[
+            pltpu.VMEM((total, padded), jnp.bfloat16),
+            pltpu.VMEM((slots, width), jnp.bfloat16),
+            pltpu.VMEM(gate_weight.shape, jnp.bfloat16),
+            pltpu.VMEM(up_weight.shape, jnp.bfloat16),
+            pltpu.VMEM(down_weight.shape, jnp.bfloat16),
+            pltpu.VMEM((slots, hidden_units), jnp.bfloat16),
+            pltpu.VMEM((total, slots), jnp.bfloat16),
+            pltpu.SemaphoreType.DMA((parts + 3,)),
+        ],
+        compiler_params=pltpu.CompilerParams(vmem_limit_bytes=52 * 2**20),
+        cost_estimate=pl.CostEstimate(
+            flops=2 * slots * width * (3 * hidden_units + 2 * total),
+            bytes_accessed=6 * width * hidden_units,
+            transcendentals=slots * hidden_units,
+        ),
+        name="expert",
+    )(expert, *pieces, gate_weight, up_weight, down_weight, gate_bias, up_bias)
+
+
+AXES = ("req", "tp")
+
+
+def moved(array, n_req, step):
+    outer, mid, core, tp = step
+    pairs = []
+    for source in range(2 * n_req):
+        req, side = divmod(source, 2)
+        place = (req // 4 ^ outer) * 4 + (req // 2 % 2 ^ mid) * 2 + (req % 2 ^ core)
+        pairs.append((source, place * 2 + (side ^ tp)))
+    return lax.ppermute(array, AXES, pairs)
+
+
+def crossed(array, n_req, by_core):
+    pairs = []
+    for source in range(2 * n_req):
+        req, side = divmod(source, 2)
+        if req % 2 == by_core:
+            pairs.append((source, (req ^ 2) * 2 + side))
+        else:
+            pairs.append((source, req * 2 + (side ^ 1)))
+    return lax.ppermute(array, AXES, pairs)
+
+
+def gather_rows(rows, n_req):
+    outer = n_req // 4
+    line = jnp.concatenate([rows] + [moved(rows, n_req, (k, 0, 0, 0)) for k in range(1, outer)])
+    first = crossed(line, n_req, 0)
+    second = crossed(line, n_req, 1)
+    both = crossed(first, n_req, 1)
+    own = [line, first, second, both]
+    return own + [moved(piece, n_req, (0, 0, 1, 0)) for piece in own]
+
+
+def add_rows(left, right):
+    return (left.astype(jnp.float32) + right.astype(jnp.float32)).astype(jnp.bfloat16)
+
+
+def scatter_rows(sums, n_req):
+    own, other = sums[:4], sums[4:]
+    line, first, second, both = [
+        add_rows(mine, moved(theirs, n_req, (0, 0, 1, 0))) for mine, theirs in zip(own, other)
+    ]
+    first = add_rows(first, crossed(both, n_req, 1))
+    line = add_rows(line, crossed(second, n_req, 1))
+    line = add_rows(line, crossed(first, n_req, 0))
+    outer = n_req // 4
+    count = line.shape[0] // outer
+    blocks = [line[k * count : (k + 1) * count] for k in range(outer)]
+    return [blocks[0]] + [
+        moved(block, n_req, (k, 0, 0, 0)) for k, block in enumerate(blocks) if k > 0
+    ]
+
+
+def gathered_body(
+    n_req,
+    queries,
+    keys_values,
+    segments,
+    sink_logits,
+    out_weight,
+    out_bias,
+    residual,
+    norm_gain,
+    route_ids,
+    route_logits,
+    gate_weight,
+    gate_bias,
+    up_weight,
+    up_bias,
+    down_weight,
+    down_bias,
+    page_table,
+):
+    attended, cached = attend_group(queries, keys_values, segments, sink_logits)
+    tok_count, width = residual.shape
+    partial = jnp.dot(attended, out_weight, preferred_element_type=jnp.float32).astype(jnp.bfloat16)
+    side = lax.axis_index("tp")
+    own = lax.dynamic_slice_in_dim(partial, side * tok_count, tok_count)
+    other = lax.dynamic_slice_in_dim(partial, (1 - side) * tok_count, tok_count)
+    got = moved(other, n_req, (0, 0, 0, 1))
+    experts = down_bias.shape[0]
+    base, rows = pl.pallas_call(
+        mid_kernel,
+        out_shape=[
+            jax.ShapeDtypeStruct((tok_count, width), jnp.float32),
+            jax.ShapeDtypeStruct((tok_count, width + 4 * experts), jnp.bfloat16),
+        ],
+        in_specs=[vmem()] * 8,
+        out_specs=[vmem()] * 2,
+        name="norm_rows",
+    )(
+        own,
+        got,
+        residual,
+        out_bias[None],
+        norm_gain[None],
+        route_ids,
+        route_logits,
+        down_bias,
+    )
+    pieces = gather_rows(rows, n_req)
+    slots = 2 * n_req * slot_limit(tok_count, route_ids.shape[1], experts)
+    sums = run_expert(
+        lax.axis_index("req")[None],
+        pieces,
+        gate_weight[0],
+        gate_bias,
+        up_weight[0],
+        up_bias,
+        down_weight[0],
+        slots,
+    )
+    mixed = base
+    for part in scatter_rows(sums, n_req):
+        mixed = mixed + part.astype(jnp.float32)
+    blocks = cached.reshape(-1, PAGE_LEN, cached.shape[1])
+    page_pool = jnp.zeros_like(blocks).at[page_table[0]].set(blocks)
+    return (mixed.astype(jnp.bfloat16), page_pool)
 
 
 def solution(mesh):
@@ -217,4 +528,6 @@
         P("req", None),
     )
     out_specs = (P(("req", "tp"), None), P("req", None, "tp"))
-    return jax.shard_map(body, mesh=mesh, in_specs=in_specs, out_specs=out_specs, check_vma=False)
+    n_req, n_tp = mesh.shape["req"], mesh.shape["tp"]
+    chosen = functools.partial(gathered_body, n_req) if (n_req, n_tp) == (16, 2) else body
+    return jax.shard_map(chosen, mesh=mesh, in_specs=in_specs, out_specs=out_specs, check_vma=False)

time: 191 us -> 133 us (0.70)
  waiting for transfers between devices: 105 us -> 41.1 us
  Pallas kernels: 0 us -> 23.5 us
  matrix products: 30.6 us -> 8.81 us
  local copies, waits for them, and re-layouts: 13.2 us -> 33.9 us
  between operations: 14.4 us -> 0.96 us
  blocking collectives: 10.5 us -> 0 us
  starting transfers between devices: 11.6 us -> 19.8 us
    unnamed x3 -> x0, waiting for transfers between devices: 52.2 us -> none
    all_to_all x2 -> x0, waiting for transfers between devices: 46.5 us -> none  [the longest x1 30.5 us: body(): lax.all_to_all(dispatched, 'req', split_axis=0, concat_axis=0, tiled=True)]
    ppermute x0 -> x21, waiting for transfers between devices: none -> 41.1 us  [the longest x6 26.6 us: crossed(): return lax.ppermute(array, AXES, pairs)]
    unnamed x26 -> x44, local copies, waits for them, and re-layouts: 4.06 us -> 27.7 us
    pallas_call x0 -> x2, Pallas kernels: none -> 23.5 us  [the longest x1 21.2 us: run_expert(): pl.pallas_call(functools.partial(expert_kernel, parts), out_shape=[jax.Sh...]
    dot_general x8 -> x1, matrix products: 29.7 us -> 7.91 us  [gathered_body(): jnp.dot(attended, out_weight, preferred_element_type=jnp.float32)]
    ppermute x0 -> x21, starting transfers between devices: none -> 19.8 us  [the longest x15 12.7 us: moved(): return lax.ppermute(array, AXES, pairs)]
    all_to_all x2 -> x0, starting transfers between devices: 11.4 us -> none  [the longest x1 5.75 us: body(): lax.all_to_all(dispatched, 'req', split_axis=0, concat_axis=0, tiled=True)]
  transfers between devices with their start and end apart: 4 -> 21, of which waited for: 4 -> 13; matrix products, arithmetic and copies ran while one was open for 3% -> 21% of each run, Pallas kernels for 0% -> 0%
where the time goes in v1:
time: 133 us; the launch traced here: 132 us
  waiting for transfers between devices  41.1 us (31%)
  local copies, waits for them, and re-layouts  33.9 us (25%)
  Pallas kernels  23.5 us (18%)
  starting transfers between devices  19.8 us (15%)
  matrix products  8.81 us (7%)
  other arithmetic  4.32 us (3%)
    unnamed x44, local copies, waits for them, and re-layouts  27.7 us
    ppermute x6, waiting for transfers between devices, crossed(): return lax.ppermute(array, AXES, pairs)  26.6 us
    pallas_call x1, Pallas kernels, run_expert(): pl.pallas_call(functools.partial(expert_kernel, parts), out_shape=[jax.Sh...  21.2 us
    ppermute x15, waiting for transfers between devices, moved(): return lax.ppermute(array, AXES, pairs)  14.5 us
    ppermute x15, starting transfers between devices, moved(): return lax.ppermute(array, AXES, pairs)  12.7 us
    dot_general x1, matrix products, gathered_body(): jnp.dot(attended, out_weight, preferred_element_type=jnp.float32)  7.91 us
    ppermute x6, starting transfers between devices, crossed(): return lax.ppermute(array, AXES, pairs)  7.09 us
  transfers between devices with their start and end apart: 21, of which 13 were waited for; matrix products, arithmetic and copies ran while one was open for 21% of the time, Pallas kernels for 0%

profile of v1, /device:TPU:0, one launch (start us, length us, event | category | flops | bytes accessed | tf_op | source)
XLA Modules:
  0.0 132.4 jit_solution(6753440507881920806)
XLA Ops:
  0.7 0.8 compare_bitcast_fusion
  1.5 0.8 fusion.11
  2.3 0.7 max.17
  3.3 0.9 reshape.201
  4.4 1.1 reshape.208
  8.2 7.9 %convolution_convert_fusion = bf16[32,2880]{1,0:T(8,128)(2,1)S(1)} fusion(bf16[32,2048]{1,0:T(8,128)(2,1)S(1)} %reshape.205, bf16[2048,2880]{0,1:T(8,128)(2,1)} %param.21), kind=kOutput, calls=%fused_computation.1 | convolution fusion | flops 377579520 | bytes 12111872 | tf_op jit(solution)/shard_map/dot_general | solution.py:465
  16.8 3.0 %collective-permute-start = (bf16[16,2880]{1,0:T(8,128)(2,1)S(1)}, bf16[16,2880]{1,0:T(8,128)(2,1)S(1)}, u32[]{:S(2)}, u32[]{:S(2)}) collective-permute-start(bf16[16,2880]{1,0:T(8,128)(2,1)S(1)} %get-tuple-element.29), channel_id=1, source_target_pairs={{0,1},{1,0},{2,3},{3,2},{4,5},{5,4},{6,7},{7,6},{8,9},{9,8},{10,11... | collective-permute-start | bytes 276488 | tf_op jit(solution)/shard_map/ppermute | solution.py:399
  23.1 2.3 %norm_rows.1 = (f32[16,2880]{1,0:T(8,128)}, bf16[16,2944]{1,0:T(8,128)(2,1)}) custom-call(bf16[16,2880]{1,0:T(8,128)(2,1)} %get-tuple-element.30.own_ref, bf16[16,2880]{1,0:T(8,128)(2,1)} %copy-done.12, bf16[16,2880]{1,0:T(8,128)(2,1)} %residual_ref.1, bf16[1,2880]{1,0:T(2,128)(2,1)} %broadcast_in_dim.23.out_bias_ref, ...), custom_call_target="tpu_custom_call" | custom-call | tf_op jit(solution)/shard_map/norm_rows/pallas_call | solution.py:471
  25.4 4.0 %collective-permute-start.3 = (bf16[16,2944]{1,0:T(8,128)(2,1)}, bf16[16,2944]{1,0:T(8,128)(2,1)S(1)}, u32[]{:S(2)}, u32[]{:S(2)}) collective-permute-start(bf16[16,2944]{1,0:T(8,128)(2,1)} %get-tuple-element.13), channel_id=1, source_target_pairs={{0,24},{1,25},{2,26},{3,27},{4,28},{5,29},{6,30},{7,31},{8,16},{9,... | collective-permute-start | bytes 282632 | tf_op jit(solution)/shard_map/ppermute | solution.py:399
  29.9 0.9 constant_dynamic-update-slice_fusion.3
  30.8 4.1 %collective-permute-done.1 = bf16[16,2944]{1,0:T(8,128)(2,1)S(1)} collective-permute-done((bf16[16,2944]{1,0:T(8,128)(2,1)}, bf16[16,2944]{1,0:T(8,128)(2,1)S(1)}, u32[]{:S(2)}, u32[]{:S(2)}) %collective-permute-start.1) | collective-permute-done | bytes 94240 | tf_op jit(solution)/shard_map/ppermute | solution.py:399
  35.0 1.7 %collective-permute-done.2 = bf16[16,2944]{1,0:T(8,128)(2,1)S(1)} collective-permute-done((bf16[16,2944]{1,0:T(8,128)(2,1)}, bf16[16,2944]{1,0:T(8,128)(2,1)S(1)}, u32[]{:S(2)}, u32[]{:S(2)}) %collective-permute-start.2) | collective-permute-done | bytes 94240 | tf_op jit(solution)/shard_map/ppermute | solution.py:399
  36.7 1.6 %collective-permute-start.4 = (bf16[64,2944]{1,0:T(8,128)(2,1)S(1)}, bf16[64,2944]{1,0:T(8,128)(2,1)S(1)}, u32[]{:S(2)}, u32[]{:S(2)}) collective-permute-start(bf16[64,2944]{1,0:T(8,128)(2,1)S(1)} %constant_dynamic-update-slice_fusion.refs_0_), channel_id=1, source_target_pairs={{0,4},{1,5},{2,3},{3,2},{4,0},{5,1},{6,7},{7,6},{8,12},{9,13},{10,... | collective-permute-start | bytes 1130504 | tf_op jit(solution)/shard_map/ppermute | solution.py:410
  38.3 1.3 collective-permute-start.5
  39.6 8.6 %collective-permute-done.4.refs_1_ = bf16[64,2944]{1,0:T(8,128)(2,1)S(1)} collective-permute-done((bf16[64,2944]{1,0:T(8,128)(2,1)S(1)}, bf16[64,2944]{1,0:T(8,128)(2,1)S(1)}, u32[]{:S(2)}, u32[]{:S(2)}) %collective-permute-start.4) | collective-permute-done | bytes 376864 | tf_op jit(solution)/shard_map/ppermute | solution.py:410
  48.2 0.9 collective-permute-start.6
  49.7 6.2 %collective-permute-done.6.refs_3_ = bf16[64,2944]{1,0:T(8,128)(2,1)S(1)} collective-permute-done((bf16[64,2944]{1,0:T(8,128)(2,1)S(1)}, bf16[64,2944]{1,0:T(8,128)(2,1)S(1)}, u32[]{:S(2)}, u32[]{:S(2)}) %collective-permute-start.6) | collective-permute-done | bytes 376864 | tf_op jit(solution)/shard_map/ppermute | solution.py:410
  55.8 11.8 %copy.36 = bf16[1,2880,1440]{2,1,0:T(8,128)(2,1)} copy(bf16[1,2880,1440]{1,2,0:T(8,128)(2,1)} %param.27) | data formatting | bytes 16588800 | tf_op args[10]
  67.6 11.8 %copy.37 = bf16[1,2880,1440]{2,1,0:T(8,128)(2,1)} copy(bf16[1,2880,1440]{1,2,0:T(8,128)(2,1)} %param.29) | data formatting | bytes 16588800 | tf_op args[12]
  80.7 21.2 %expert.1 = (bf16[64,2880]{1,0:T(8,128)(2,1)S(1)}, bf16[64,2880]{1,0:T(8,128)(2,1)S(1)}, bf16[64,2880]{1,0:T(8,128)(2,1)S(1)}, bf16[64,2880]{1,0:T(8,128)(2,1)S(...) custom-call(s32[1]{0:T(128)} %bitcast.12.expert_ref, ...), custom_call_target="tpu_custom_call" | custom-call | flops 7880048640 | bytes 24883200 | tf_op jit(solution)/shard_map/expert/pallas_call | solution.py:362
  103.0 0.9 collective-permute-done.15
  104.0 0.9 collective-permute-start.16
  105.0 1.2 collective-permute-start.13
  106.2 5.4 %collective-permute-done.16 = bf16[64,2880]{1,0:T(8,128)(2,1)S(1)} collective-permute-done((bf16[64,2880]{1,0:T(8,128)(2,1)S(1)}, bf16[64,2880]{1,0:T(8,128)(2,1)S(1)}, u32[]{:S(2)}, u32[]{:S(2)}) %collective-permute-start.16) | collective-permute-done | bytes 368672 | tf_op jit(solution)/shard_map/ppermute | solution.py:410
  111.8 1.3 collective-permute-start.17
  113.1 4.2 %collective-permute-done.13 = bf16[64,2880]{1,0:T(8,128)(2,1)S(1)} collective-permute-done((bf16[64,2880]{1,0:T(8,128)(2,1)S(1)}, bf16[64,2880]{1,0:T(8,128)(2,1)S(1)}, u32[]{:S(2)}, u32[]{:S(2)}) %collective-permute-start.13) | collective-permute-done | bytes 368672 | tf_op jit(solution)/shard_map/ppermute | solution.py:410
  117.3 2.1 %collective-permute-done.17 = bf16[64,2880]{1,0:T(8,128)(2,1)S(1)} collective-permute-done((bf16[64,2880]{1,0:T(8,128)(2,1)S(1)}, bf16[64,2880]{1,0:T(8,128)(2,1)S(1)}, u32[]{:S(2)}, u32[]{:S(2)}) %collective-permute-start.17) | collective-permute-done | bytes 368672 | tf_op jit(solution)/shard_map/ppermute | solution.py:410
  119.8 1.9 %collective-permute-start.20 = (bf16[16,2880]{1,0:T(8,128)(2,1)S(1)}, bf16[16,2880]{1,0:T(8,128)(2,1)S(1)}, u32[]{:S(2)}, u32[]{:S(2)}) collective-permute-start(bf16[16,2880]{1,0:T(8,128)(2,1)S(1)} %get-tuple-element.27), channel_id=1, source_target_pairs={{0,24},{1,25},{2,26},{3,27},{4,28},{5,29},{6,30},{7,31},{8,16},{9,... | collective-permute-start | bytes 276488 | tf_op jit(solution)/shard_map/ppermute | solution.py:399
  121.7 1.5 %collective-permute-start.19 = (bf16[16,2880]{1,0:T(8,128)(2,1)S(1)}, bf16[16,2880]{1,0:T(8,128)(2,1)S(1)}, u32[]{:S(2)}, u32[]{:S(2)}) collective-permute-start(bf16[16,2880]{1,0:T(8,128)(2,1)S(1)} %get-tuple-element.28), channel_id=1, source_target_pairs={{0,16},{1,17},{2,18},{3,19},{4,20},{5,21},{6,22},{7,23},{8,24},{9,... | collective-permute-start | bytes 276488 | tf_op jit(solution)/shard_map/ppermute | solution.py:399
  124.5 2.7 %collective-permute-done.20 = bf16[16,2880]{1,0:T(8,128)(2,1)S(1)} collective-permute-done((bf16[16,2880]{1,0:T(8,128)(2,1)S(1)}, bf16[16,2880]{1,0:T(8,128)(2,1)S(1)}, u32[]{:S(2)}, u32[]{:S(2)}) %collective-permute-start.20) | collective-permute-done | bytes 92192 | tf_op jit(solution)/shard_map/ppermute | solution.py:399
  127.3 4.4 %collective-permute-done.19 = bf16[16,2880]{1,0:T(8,128)(2,1)S(1)} collective-permute-done((bf16[16,2880]{1,0:T(8,128)(2,1)S(1)}, bf16[16,2880]{1,0:T(8,128)(2,1)S(1)}, u32[]{:S(2)}, u32[]{:S(2)}) %collective-permute-start.19) | collective-permute-done | bytes 92192 | tf_op jit(solution)/shard_map/ppermute | solution.py:399
  131.7 0.7 add_convert_fusion.8
  (97 shorter events, 12.5 us)
Async XLA Ops:
  6.6 13.2 %copy-start.15 = (s32[16,4]{0,1:T(4,128)S(1)}, s32[16,4]{0,1:T(4,128)}, u32[]{:S(2)}) copy-start(s32[16,4]{0,1:T(4,128)} %param.25) | copy-start | bytes 772
  6.6 13.9 %copy-start.16 = (f32[16,4]{0,1:T(4,128)S(1)}, f32[16,4]{0,1:T(4,128)}, u32[]{:S(2)}) copy-start(f32[16,4]{0,1:T(4,128)} %param.26) | copy-start | bytes 772
  6.6 14.5 %copy-start.13 = (bf16[2880]{0:T(1024)(128)(2,1)S(1)}, bf16[2880]{0:T(1024)(128)(2,1)}, u32[]{:S(2)}) copy-start(bf16[2880]{0:T(1024)(128)(2,1)} %param.22) | copy-start | bytes 17284
  6.6 15.1 %copy-start.14 = (bf16[2880]{0:T(1024)(128)(2,1)S(1)}, bf16[2880]{0:T(1024)(128)(2,1)}, u32[]{:S(2)}) copy-start(bf16[2880]{0:T(1024)(128)(2,1)} %param.24) | copy-start | bytes 17284
  16.8 5.7 %collective-permute-start = (bf16[16,2880]{1,0:T(8,128)(2,1)S(1)}, bf16[16,2880]{1,0:T(8,128)(2,1)S(1)}, u32[]{:S(2)}, u32[]{:S(2)}) collective-permute-start(bf16[16,2880]{1,0:T(8,128)(2,1)S(1)} %get-tuple-element.29), channel_id=1, source_target_pairs={{0,1},{1,0},{2,3},{3,2},{4,5},{5,4},{6,7},{7,6},{8,9},{9,8},{10,11... | collective-permute-start | bytes 276488 | tf_op jit(solution)/shard_map/ppermute | solution.py:399
  25.4 11.3 %collective-permute-start.3 = (bf16[16,2944]{1,0:T(8,128)(2,1)}, bf16[16,2944]{1,0:T(8,128)(2,1)S(1)}, u32[]{:S(2)}, u32[]{:S(2)}) collective-permute-start(bf16[16,2944]{1,0:T(8,128)(2,1)} %get-tuple-element.13), channel_id=1, source_target_pairs={{0,24},{1,25},{2,26},{3,27},{4,28},{5,29},{6,30},{7,31},{8,16},{9,... | collective-permute-start | bytes 282632 | tf_op jit(solution)/shard_map/ppermute | solution.py:399
  29.3 7.4 %collective-permute-start.2 = (bf16[16,2944]{1,0:T(8,128)(2,1)}, bf16[16,2944]{1,0:T(8,128)(2,1)S(1)}, u32[]{:S(2)}, u32[]{:S(2)}) collective-permute-start(bf16[16,2944]{1,0:T(8,128)(2,1)} %get-tuple-element.13), channel_id=1, source_target_pairs={{0,16},{1,17},{2,18},{3,19},{4,20},{5,21},{6,22},{7,23},{8,24},{9,... | collective-permute-start | bytes 282632 | tf_op jit(solution)/shard_map/ppermute | solution.py:399
  29.3 5.6 %collective-permute-start.1 = (bf16[16,2944]{1,0:T(8,128)(2,1)}, bf16[16,2944]{1,0:T(8,128)(2,1)S(1)}, u32[]{:S(2)}, u32[]{:S(2)}) collective-permute-start(bf16[16,2944]{1,0:T(8,128)(2,1)} %get-tuple-element.13), channel_id=1, source_target_pairs={{0,8},{1,9},{2,10},{3,11},{4,12},{5,13},{6,14},{7,15},{8,0},{9,1},... | collective-permute-start | bytes 282632 | tf_op jit(solution)/shard_map/ppermute | solution.py:399
  36.7 42.7 %copy-start.2 = (bf16[64,2944]{1,0:T(8,128)(2,1)}, bf16[64,2944]{1,0:T(8,128)(2,1)S(1)}, u32[]{:S(2)}) copy-start(bf16[64,2944]{1,0:T(8,128)(2,1)S(1)} %constant_dynamic-update-slice_fusion.refs_0_) | copy-start | bytes 1130500
  36.7 11.5 %collective-permute-start.4 = (bf16[64,2944]{1,0:T(8,128)(2,1)S(1)}, bf16[64,2944]{1,0:T(8,128)(2,1)S(1)}, u32[]{:S(2)}, u32[]{:S(2)}) collective-permute-start(bf16[64,2944]{1,0:T(8,128)(2,1)S(1)} %constant_dynamic-update-slice_fusion.refs_0_), channel_id=1, source_target_pairs={{0,4},{1,5},{2,3},{3,2},{4,0},{5,1},{6,7},{7,6},{8,12},{9,13},{10,... | collective-permute-start | bytes 1130504 | tf_op jit(solution)/shard_map/ppermute | solution.py:410
  38.3 11.3 %collective-permute-start.5 = (bf16[64,2944]{1,0:T(8,128)(2,1)S(1)}, bf16[64,2944]{1,0:T(8,128)(2,1)S(1)}, u32[]{:S(2)}, u32[]{:S(2)}) collective-permute-start(bf16[64,2944]{1,0:T(8,128)(2,1)S(1)} %constant_dynamic-update-slice_fusion.refs_0_), channel_id=1, source_target_pairs={{0,1},{1,0},{2,6},{3,7},{4,5},{5,4},{6,2},{7,3},{8,9},{9,8},{10,14... | collective-permute-start | bytes 1130504 | tf_op jit(solution)/shard_map/ppermute | solution.py:410
  48.2 31.2 %copy-start.3 = (bf16[64,2944]{1,0:T(8,128)(2,1)}, bf16[64,2944]{1,0:T(8,128)(2,1)S(1)}, u32[]{:S(2)}) copy-start(bf16[64,2944]{1,0:T(8,128)(2,1)S(1)} %collective-permute-done.4.refs_1_) | copy-start | bytes 1130500
  48.2 7.6 %collective-permute-start.6 = (bf16[64,2944]{1,0:T(8,128)(2,1)S(1)}, bf16[64,2944]{1,0:T(8,128)(2,1)S(1)}, u32[]{:S(2)}, u32[]{:S(2)}) collective-permute-start(bf16[64,2944]{1,0:T(8,128)(2,1)S(1)} %collective-permute-done.4.refs_1_), channel_id=1, source_target_pairs={{0,1},{1,0},{2,6},{3,7},{4,5},{5,4},{6,2},{7,3},{8,9},{9,8},{10,14... | collective-permute-start | bytes 1130504 | tf_op jit(solution)/shard_map/ppermute | solution.py:410
  49.1 30.4 %collective-permute-start.7 = (bf16[64,2944]{1,0:T(8,128)(2,1)S(1)}, bf16[64,2944]{1,0:T(8,128)(2,1)S(1)}, u32[]{:S(2)}, u32[]{:S(2)}) collective-permute-start(bf16[64,2944]{1,0:T(8,128)(2,1)S(1)} %constant_dynamic-update-slice_fusion.refs_0_), channel_id=1, source_target_pairs={{0,2},{1,3},{2,0},{3,1},{4,6},{5,7},{6,4},{7,5},{8,10},{9,11},{10,... | collective-permute-start | bytes 1130504 | tf_op jit(solution)/shard_map/ppermute | solution.py:399
  49.1 30.4 %collective-permute-start.8 = (bf16[64,2944]{1,0:T(8,128)(2,1)S(1)}, bf16[64,2944]{1,0:T(8,128)(2,1)S(1)}, u32[]{:S(2)}, u32[]{:S(2)}) collective-permute-start(bf16[64,2944]{1,0:T(8,128)(2,1)S(1)} %collective-permute-done.4.refs_1_), channel_id=1, source_target_pairs={{0,2},{1,3},{2,0},{3,1},{4,6},{5,7},{6,4},{7,5},{8,10},{9,11},{10,... | collective-permute-start | bytes 1130504 | tf_op jit(solution)/shard_map/ppermute | solution.py:399
  49.6 29.9 %copy-start.4 = (bf16[64,2944]{1,0:T(8,128)(2,1)}, bf16[64,2944]{1,0:T(8,128)(2,1)S(1)}, u32[]{:S(2)}) copy-start(bf16[64,2944]{1,0:T(8,128)(2,1)S(1)} %collective-permute-done.5.refs_2_) | copy-start | bytes 1130500
  49.6 29.9 %collective-permute-start.9 = (bf16[64,2944]{1,0:T(8,128)(2,1)S(1)}, bf16[64,2944]{1,0:T(8,128)(2,1)S(1)}, u32[]{:S(2)}, u32[]{:S(2)}) collective-permute-start(bf16[64,2944]{1,0:T(8,128)(2,1)S(1)} %collective-permute-done.5.refs_2_), channel_id=1, source_target_pairs={{0,2},{1,3},{2,0},{3,1},{4,6},{5,7},{6,4},{7,5},{8,10},{9,11},{10,... | collective-permute-start | bytes 1130504 | tf_op jit(solution)/shard_map/ppermute | solution.py:399
  55.8 23.7 %copy-start.5 = (bf16[64,2944]{1,0:T(8,128)(2,1)}, bf16[64,2944]{1,0:T(8,128)(2,1)S(1)}, u32[]{:S(2)}) copy-start(bf16[64,2944]{1,0:T(8,128)(2,1)S(1)} %collective-permute-done.6.refs_3_) | copy-start | bytes 1130500
  55.8 23.7 %collective-permute-start.10 = (bf16[64,2944]{1,0:T(8,128)(2,1)S(1)}, bf16[64,2944]{1,0:T(8,128)(2,1)S(1)}, u32[]{:S(2)}, u32[]{:S(2)}) collective-permute-start(bf16[64,2944]{1,0:T(8,128)(2,1)S(1)} %collective-permute-done.6.refs_3_), channel_id=1, source_target_pairs={{0,2},{1,3},{2,0},{3,1},{4,6},{5,7},{6,4},{7,5},{8,10},{9,11},{10,... | collective-permute-start | bytes 1130504 | tf_op jit(solution)/shard_map/ppermute | solution.py:399
  67.6 13.0 %copy-start.1 = (bf16[1,1440]{1,0:T(2,128)(2,1)S(1)}, bf16[1,1440]{1,0:T(2,128)(2,1)}, u32[]{:S(2)}) copy-start(bf16[1,1440]{1,0:T(2,128)(2,1)} %refs_12_.1) | copy-start | bytes 8644
  80.6 32.4 %copy-start.17 = (s32[1,2]{1,0:T(1,128)S(1)}, s32[1,2]{1,0:T(1,128)}, u32[]{:S(2)}) copy-start(s32[1,2]{1,0:T(1,128)} %param.33) | copy-start | bytes 28
  80.6 51.0 %copy-start.10 = (f32[16,2880]{1,0:T(8,128)S(1)}, f32[16,2880]{1,0:T(8,128)}, u32[]{:S(2)}) copy-start(f32[16,2880]{1,0:T(8,128)} %get-tuple-element.12) | copy-start | bytes 552964
  101.9 2.0 %collective-permute-start.15 = (bf16[64,2880]{1,0:T(8,128)(2,1)}, bf16[64,2880]{1,0:T(8,128)(2,1)S(1)}, u32[]{:S(2)}, u32[]{:S(2)}) collective-permute-start(bf16[64,2880]{1,0:T(8,128)(2,1)} %get-tuple-element.21), channel_id=1, source_target_pairs={{0,2},{1,3},{2,0},{3,1},{4,6},{5,7},{6,4},{7,5},{8,10},{9,11},{10,... | collective-permute-start | bytes 1105928 | tf_op jit(solution)/shard_map/ppermute | solution.py:399
  102.3 10.7 %collective-permute-start.11 = (bf16[64,2880]{1,0:T(8,128)(2,1)S(1)}, bf16[64,2880]{1,0:T(8,128)(2,1)S(1)}, u32[]{:S(2)}, u32[]{:S(2)}) collective-permute-start(bf16[64,2880]{1,0:T(8,128)(2,1)S(1)} %get-tuple-element.15), channel_id=1, source_target_pairs={{0,2},{1,3},{2,0},{3,1},{4,6},{5,7},{6,4},{7,5},{8,10},{9,11},{10,... | collective-permute-start | bytes 1105928 | tf_op jit(solution)/shard_map/ppermute | solution.py:399
  102.5 2.5 %collective-permute-start.12 = (bf16[64,2880]{1,0:T(8,128)(2,1)}, bf16[64,2880]{1,0:T(8,128)(2,1)S(1)}, u32[]{:S(2)}, u32[]{:S(2)}) collective-permute-start(bf16[64,2880]{1,0:T(8,128)(2,1)} %get-tuple-element.17), channel_id=1, source_target_pairs={{0,2},{1,3},{2,0},{3,1},{4,6},{5,7},{6,4},{7,5},{8,10},{9,11},{10,... | collective-permute-start | bytes 1105928 | tf_op jit(solution)/shard_map/ppermute | solution.py:399
  102.8 3.4 %collective-permute-start.14 = (bf16[64,2880]{1,0:T(8,128)(2,1)}, bf16[64,2880]{1,0:T(8,128)(2,1)S(1)}, u32[]{:S(2)}, u32[]{:S(2)}) collective-permute-start(bf16[64,2880]{1,0:T(8,128)(2,1)} %get-tuple-element.19), channel_id=1, source_target_pairs={{0,2},{1,3},{2,0},{3,1},{4,6},{5,7},{6,4},{7,5},{8,10},{9,11},{10,... | collective-permute-start | bytes 1105928 | tf_op jit(solution)/shard_map/ppermute | solution.py:399
  104.0 7.7 %collective-permute-start.16 = (bf16[64,2880]{1,0:T(8,128)(2,1)S(1)}, bf16[64,2880]{1,0:T(8,128)(2,1)S(1)}, u32[]{:S(2)}, u32[]{:S(2)}) collective-permute-start(bf16[64,2880]{1,0:T(8,128)(2,1)S(1)} %add_convert_fusion.2), channel_id=1, source_target_pairs={{0,1},{1,0},{2,6},{3,7},{4,5},{5,4},{6,2},{7,3},{8,9},{9,8},{10,14... | collective-permute-start | bytes 1105928 | tf_op jit(solution)/shard_map/ppermute | solution.py:410
  105.0 12.3 %collective-permute-start.13 = (bf16[64,2880]{1,0:T(8,128)(2,1)S(1)}, bf16[64,2880]{1,0:T(8,128)(2,1)S(1)}, u32[]{:S(2)}, u32[]{:S(2)}) collective-permute-start(bf16[64,2880]{1,0:T(8,128)(2,1)S(1)} %add_convert_fusion.5), channel_id=1, source_target_pairs={{0,1},{1,0},{2,6},{3,7},{4,5},{5,4},{6,2},{7,3},{8,9},{9,8},{10,14... | collective-permute-start | bytes 1105928 | tf_op jit(solution)/shard_map/ppermute | solution.py:410
  111.8 7.7 %collective-permute-start.17 = (bf16[64,2880]{1,0:T(8,128)(2,1)S(1)}, bf16[64,2880]{1,0:T(8,128)(2,1)S(1)}, u32[]{:S(2)}, u32[]{:S(2)}) collective-permute-start(bf16[64,2880]{1,0:T(8,128)(2,1)S(1)} %add_convert_fusion.1), channel_id=1, source_target_pairs={{0,4},{1,5},{2,3},{3,2},{4,0},{5,1},{6,7},{7,6},{8,12},{9,13},{10,... | collective-permute-start | bytes 1105928 | tf_op jit(solution)/shard_map/ppermute | solution.py:410
  119.6 4.9 %collective-permute-start.18 = (bf16[16,2880]{1,0:T(8,128)(2,1)S(1)}, bf16[16,2880]{1,0:T(8,128)(2,1)S(1)}, u32[]{:S(2)}, u32[]{:S(2)}) collective-permute-start(bf16[16,2880]{1,0:T(8,128)(2,1)S(1)} %get-tuple-element.26), channel_id=1, source_target_pairs={{0,8},{1,9},{2,10},{3,11},{4,12},{5,13},{6,14},{7,15},{8,0},{9,1},... | collective-permute-start | bytes 276488 | tf_op jit(solution)/shard_map/ppermute | solution.py:399
  119.8 7.5 %collective-permute-start.20 = (bf16[16,2880]{1,0:T(8,128)(2,1)S(1)}, bf16[16,2880]{1,0:T(8,128)(2,1)S(1)}, u32[]{:S(2)}, u32[]{:S(2)}) collective-permute-start(bf16[16,2880]{1,0:T(8,128)(2,1)S(1)} %get-tuple-element.27), channel_id=1, source_target_pairs={{0,24},{1,25},{2,26},{3,27},{4,28},{5,29},{6,30},{7,31},{8,16},{9,... | collective-permute-start | bytes 276488 | tf_op jit(solution)/shard_map/ppermute | solution.py:399
  121.7 10.0 %collective-permute-start.19 = (bf16[16,2880]{1,0:T(8,128)(2,1)S(1)}, bf16[16,2880]{1,0:T(8,128)(2,1)S(1)}, u32[]{:S(2)}, u32[]{:S(2)}) collective-permute-start(bf16[16,2880]{1,0:T(8,128)(2,1)S(1)} %get-tuple-element.28), channel_id=1, source_target_pairs={{0,16},{1,17},{2,18},{3,19},{4,20},{5,21},{6,22},{7,23},{8,24},{9,... | collective-permute-start | bytes 276488 | tf_op jit(solution)/shard_map/ppermute | solution.py:399
  (7 other events, 25.6 us)

commit v2 on v1

--- a/solution.py
+++ b/solution.py
@@ -2,6 +2,7 @@
 
 import jax
 import jax.numpy as jnp
+import numpy as np
 from jax import lax
 from jax.experimental import pallas as pl
 from jax.experimental.pallas import tpu as pltpu
@@ -261,28 +262,50 @@
     return [(start, min(step, total - start)) for start in range(0, total, step)]
 
 
-def expert_kernel(parts, expert_ref, *refs):
+def expert_kernel(parts, step, expert_ref, *refs):
     pieces, refs = refs[:parts], refs[parts:]
     gate_hbm, up_hbm, down_hbm, gate_bias_ref, up_bias_ref = refs[:5]
     outs, refs = refs[5 : 5 + parts], refs[5 + parts :]
-    rows, picked, gate_w, up_w, down_w, active, spread, sems = refs
+    rows, picked, gate_up, down_w, active, spread, sems = refs
     piece = pieces[0].shape[0]
     total = rows.shape[0]
     slots = picked.shape[0]
-    width = down_w.shape[1]
-    copies = [
+    units, width = down_w.shape
+    row_copies = [
         pltpu.make_async_copy(p, rows.at[pl.ds(i * piece, piece)], sems.at[i])
         for i, p in enumerate(pieces)
     ]
-    weights = [
-        pltpu.make_async_copy(src, dst, sems.at[parts + i])
-        for i, (src, dst) in enumerate(
-            ((gate_hbm, gate_w), (up_hbm, up_w), (down_hbm, down_w))
+    chunks = tiles(units, step)
+    up_copies = []
+    for i, (start, size) in enumerate(chunks):
+        for side, source in enumerate((gate_hbm, up_hbm)):
+            up_copies.append(
+                pltpu.make_async_copy(
+                    source.at[pl.ds(start, size)],
+                    gate_up.at[pl.ds(2 * start + side * size, size)],
+                    sems.at[parts + 2 * i + side],
+                )
+            )
+    blocks = tiles(width, 2 * step)
+    down_copies = [
+        pltpu.make_async_copy(
+            down_hbm.at[:, pl.ds(start, size)],
+            down_w.at[:, pl.ds(start, size)],
+            sems.at[parts + 2 * len(chunks) + i],
         )
+        for i, (start, size) in enumerate(blocks)
     ]
-    for copy in copies + weights:
+    for copy in row_copies + up_copies + down_copies:
         copy.start()
-    for copy in copies:
+    up_bias = jnp.broadcast_to(up_bias_ref[...].astype(jnp.float32), (8, units)).T
+    gate_bias = jnp.broadcast_to(gate_bias_ref[...].astype(jnp.float32), (8, units)).T
+    earlier = jnp.where(
+        lax.broadcasted_iota(jnp.int32, (total, total), 0)
+        <= lax.broadcasted_iota(jnp.int32, (total, total), 1),
+        1.0,
+        0.0,
+    ).astype(jnp.bfloat16)
+    for copy in row_copies:
         copy.wait()
 
     expert = expert_ref[0]
@@ -300,12 +323,6 @@
     )
     share = found[0:1] + found[1:2]
     chosen = share > 0.0
-    earlier = jnp.where(
-        lax.broadcasted_iota(jnp.int32, (total, total), 0)
-        <= lax.broadcasted_iota(jnp.int32, (total, total), 1),
-        1.0,
-        0.0,
-    ).astype(jnp.bfloat16)
     marks = jnp.broadcast_to(jnp.where(chosen, 1.0, 0.0), (16, total)).astype(jnp.bfloat16)
     count = jnp.dot(marks, earlier, preferred_element_type=jnp.float32)[0:1]
     slot = jnp.where(chosen, count - 1.0, -1.0).astype(jnp.int32)
@@ -319,31 +336,167 @@
             pick, rows[:, start : start + size], preferred_element_type=jnp.float32
         ).astype(jnp.bfloat16)
 
-    weights[0].wait()
-    weights[1].wait()
-    for start, size in tiles(gate_w.shape[1], 256):
-        cols = slice(start, start + size)
-        gate = jnp.dot(
-            picked[...], gate_w[:, cols], preferred_element_type=jnp.float32
-        ) + gate_bias_ref[:, cols].astype(jnp.float32)
-        up = jnp.dot(
-            picked[...], up_w[:, cols], preferred_element_type=jnp.float32
-        ) + up_bias_ref[:, cols].astype(jnp.float32)
-        gate = jnp.minimum(gate, swiglu_limit)
-        up = jnp.clip(up, -swiglu_limit, swiglu_limit)
-        active[:, cols] = (
-            gate * (1.0 / (1.0 + jnp.exp(-glu_alpha * gate))) * (up + 1.0)
-        ).astype(jnp.bfloat16)
-    weights[2].wait()
-    for start, size in tiles(width, 256):
+    for i, (start, size) in enumerate(chunks):
+        up_copies[2 * i].wait()
+        up_copies[2 * i + 1].wait()
+        both = lax.dot_general(
+            gate_up[2 * start : 2 * (start + size)],
+            picked[...],
+            (((1,), (1,)), ((), ())),
+            preferred_element_type=jnp.float32,
+        )
+        gate = jnp.minimum(both[:size] + gate_bias[start : start + size, 0:1], swiglu_limit)
+        up = jnp.clip(both[size:] + up_bias[start : start + size, 0:1], -swiglu_limit, swiglu_limit)
+        value = gate * (1.0 / (1.0 + jnp.exp(-glu_alpha * gate))) * (up + 1.0)
+        active[:, start : start + size] = value.T.astype(jnp.bfloat16)
+    for i, (start, size) in enumerate(blocks):
+        down_copies[i].wait()
         cols = slice(start, start + size)
         value = jnp.dot(active[...], down_w[:, cols], preferred_element_type=jnp.float32)
         scaled = (value * slot_share).astype(jnp.bfloat16)
         spread_rows = jnp.dot(spread[...], scaled, preferred_element_type=jnp.float32).astype(
             jnp.bfloat16
         )
-        for i, out in enumerate(outs):
-            out[:, cols] = spread_rows[i * piece : (i + 1) * piece]
+        for k, out in enumerate(outs):
+            out[:, cols] = spread_rows[k * piece : (k + 1) * piece]
+
+
+def attention_kernel(
+    side_ref,
+    pages_ref,
+    sink_ref,
+    queries_ref,
+    keys_values_ref,
+    segments_ref,
+    inverse_ref,
+    weight_hbm,
+    own_ref,
+    other_ref,
+    cache_ref,
+    weight,
+    attended,
+    sems,
+):
+    length, query_width = queries_ref.shape
+    width = weight.shape[0]
+    kv_heads = keys_values_ref.shape[1] // LANES
+    group_tiles = query_width // LANES // kv_heads
+    chunks = tiles(width, 512)
+    copies = [
+        pltpu.make_async_copy(
+            weight_hbm.at[pl.ds(start, size)], weight.at[pl.ds(start, size)], sems.at[i]
+        )
+        for i, (start, size) in enumerate(chunks)
+    ]
+    for copy in copies:
+        copy.start()
+    named = jnp.broadcast_to(segments_ref[...].astype(jnp.float32), (length, length))
+    visible = (named == named.T) & (
+        lax.broadcasted_iota(jnp.int32, (length, length), 1)
+        <= lax.broadcasted_iota(jnp.int32, (length, length), 0)
+    )
+    positions = jnp.sum(jnp.where(visible, 1.0, 0.0), axis=1, keepdims=True) - 1.0
+    angles = positions * inverse_ref[...]
+    lane = lax.broadcasted_iota(jnp.int32, (length, LANES), 1)
+    lower = lane % HEAD < HEAD // 2
+    cosine = jnp.cos(angles)
+    sine = jnp.sin(angles)
+    sine = jnp.where(lower, -sine, sine)
+    left = lane < HEAD
+
+    def turned(tile):
+        swapped = jnp.where(
+            lower, pltpu.roll(tile, LANES - HEAD // 2, 1), pltpu.roll(tile, HEAD // 2, 1)
+        )
+        return tile * cosine + swapped * sine
+
+    seen = jnp.concatenate([visible] * (2 * group_tiles), axis=0)
+    for k in range(kv_heads):
+        raw = keys_values_ref[:, k * LANES : (k + 1) * LANES].astype(jnp.float32)
+        pair = jnp.where(left, turned(raw), raw).astype(jnp.bfloat16)
+        for b in range(cache_ref.shape[0]):
+            cache_ref[pages_ref[0, b], :, k * LANES : (k + 1) * LANES] = pair[
+                b * PAGE_LEN : (b + 1) * PAGE_LEN
+            ]
+        heads = []
+        sinks = []
+        for t in range(k * group_tiles, (k + 1) * group_tiles):
+            tile = turned(queries_ref[:, t * LANES : (t + 1) * LANES].astype(jnp.float32))
+            heads.append(jnp.where(left, tile, 0.0))
+            heads.append(jnp.where(left, pltpu.roll(tile, HEAD, 1), 0.0))
+            sinks.append(jnp.full((length, 1), sink_ref[2 * t], jnp.float32))
+            sinks.append(jnp.full((length, 1), sink_ref[2 * t + 1], jnp.float32))
+        sink = jnp.concatenate(sinks, axis=0)
+        scores = lax.dot_general(
+            jnp.concatenate(heads, axis=0).astype(jnp.bfloat16),
+            pair,
+            (((1,), (1,)), ((), ())),
+            preferred_element_type=jnp.float32,
+        ) * HEAD ** (-0.5)
+        scores = jnp.where(seen, scores, -1e30)
+        highest = jnp.maximum(jnp.max(scores, axis=-1, keepdims=True), sink)
+        expo = jnp.where(seen, jnp.exp(scores - highest), 0.0)
+        denominator = jnp.sum(expo, axis=-1, keepdims=True) + jnp.exp(sink - highest)
+        probabilities = (expo / denominator).astype(jnp.bfloat16)
+        mixed = jnp.dot(probabilities, pair, preferred_element_type=jnp.float32)
+        for t in range(group_tiles):
+            even = mixed[2 * t * length : (2 * t + 1) * length]
+            odd = mixed[(2 * t + 1) * length : (2 * t + 2) * length]
+            start = (k * group_tiles + t) * LANES
+            attended[:, start : start + LANES] = jnp.where(
+                left, pltpu.roll(even, HEAD, 1), odd
+            ).astype(jnp.bfloat16)
+    first_side = side_ref[0] == 0
+    half = own_ref.shape[0]
+    for i, (start, size) in enumerate(chunks):
+        copies[i].wait()
+        projected = lax.dot_general(
+            attended[...],
+            weight[start : start + size],
+            (((1,), (1,)), ((), ())),
+            preferred_element_type=jnp.float32,
+        )
+        top, bottom = projected[:half], projected[half:]
+        own_ref[:, start : start + size] = jnp.where(first_side, top, bottom)
+        other_ref[:, start : start + size] = jnp.where(first_side, bottom, top).astype(jnp.bfloat16)
+
+
+def run_attention(side, page_table, sink_logits, queries, keys_values, segments, out_weight):
+    length, query_width = queries.shape
+    width = out_weight.shape[1]
+    half = length // 2
+    inverse = np.float32(rope_base) ** (
+        -(np.arange(LANES) % (HEAD // 2)).astype(np.float32) / np.float32(HEAD // 2)
+    )
+    smem = pl.BlockSpec(memory_space=pltpu.SMEM)
+    return pl.pallas_call(
+        attention_kernel,
+        out_shape=[
+            jax.ShapeDtypeStruct((half, width), jnp.float32),
+            jax.ShapeDtypeStruct((half, width), jnp.bfloat16),
+            jax.ShapeDtypeStruct(
+                (length // PAGE_LEN, PAGE_LEN, keys_values.shape[1]), jnp.bfloat16
+            ),
+        ],
+        in_specs=[smem] * 3 + [vmem()] * 4 + [anywhere()],
+        out_specs=[vmem()] * 3,
+        scratch_shapes=[
+            pltpu.VMEM((width, query_width), jnp.bfloat16),
+            pltpu.VMEM((length, query_width), jnp.bfloat16),
+            pltpu.SemaphoreType.DMA((len(tiles(width, 512)),)),
+        ],
+        compiler_params=pltpu.CompilerParams(vmem_limit_bytes=24 * 2**20),
+        name="attention",
+    )(
+        side,
+        page_table,
+        sink_logits,
+        queries,
+        keys_values,
+        segments[None],
+        jnp.asarray(inverse.astype(np.float32))[None],
+        out_weight.T,
+    )
 
 
 def vmem():
@@ -359,8 +512,10 @@
     piece, padded = pieces[0].shape
     hidden_units, width = down_weight.shape
     total = parts * piece
+    step = 256
+    copies = parts + 2 * len(tiles(hidden_units, step)) + len(tiles(width, 2 * step))
     return pl.pallas_call(
-        functools.partial(expert_kernel, parts),
+        functools.partial(expert_kernel, parts, step),
         out_shape=[jax.ShapeDtypeStruct((piece, width), jnp.bfloat16)] * parts,
         in_specs=[pl.BlockSpec(memory_space=pltpu.SMEM)]
         + [anywhere()] * (parts + 3)
@@ -369,12 +524,11 @@
         scratch_shapes=[
             pltpu.VMEM((total, padded), jnp.bfloat16),
             pltpu.VMEM((slots, width), jnp.bfloat16),
-            pltpu.VMEM(gate_weight.shape, jnp.bfloat16),
-            pltpu.VMEM(up_weight.shape, jnp.bfloat16),
+            pltpu.VMEM((2 * hidden_units, width), jnp.bfloat16),
             pltpu.VMEM(down_weight.shape, jnp.bfloat16),
             pltpu.VMEM((slots, hidden_units), jnp.bfloat16),
             pltpu.VMEM((total, slots), jnp.bfloat16),
-            pltpu.SemaphoreType.DMA((parts + 3,)),
+            pltpu.SemaphoreType.DMA((copies,)),
         ],
         compiler_params=pltpu.CompilerParams(vmem_limit_bytes=52 * 2**20),
         cost_estimate=pl.CostEstimate(
@@ -383,7 +537,7 @@
             transcendentals=slots * hidden_units,
         ),
         name="expert",
-    )(expert, *pieces, gate_weight, up_weight, down_weight, gate_bias, up_bias)
+    )(expert, *pieces, gate_weight.T, up_weight.T, down_weight, gate_bias, up_bias)
 
 
 AXES = ("req", "tp")
@@ -460,12 +614,11 @@
     down_bias,
     page_table,
 ):
-    attended, cached = attend_group(queries, keys_values, segments, sink_logits)
     tok_count, width = residual.shape
-    partial = jnp.dot(attended, out_weight, preferred_element_type=jnp.float32).astype(jnp.bfloat16)
-    side = lax.axis_index("tp")
-    own = lax.dynamic_slice_in_dim(partial, side * tok_count, tok_count)
-    other = lax.dynamic_slice_in_dim(partial, (1 - side) * tok_count, tok_count)
+    side = lax.axis_index("tp")[None]
+    own, other, page_pool = run_attention(
+        side, page_table, sink_logits, queries, keys_values, segments, out_weight
+    )
     got = moved(other, n_req, (0, 0, 0, 1))
     experts = down_bias.shape[0]
     base, rows = pl.pallas_call(
@@ -502,8 +655,6 @@
     mixed = base
     for part in scatter_rows(sums, n_req):
         mixed = mixed + part.astype(jnp.float32)
-    blocks = cached.reshape(-1, PAGE_LEN, cached.shape[1])
-    page_pool = jnp.zeros_like(blocks).at[page_table[0]].set(blocks)
     return (mixed.astype(jnp.bfloat16), page_pool)
 
 

time: 133 us -> 112 us (0.84)
  local copies, waits for them, and re-layouts: 33.9 us -> 14.3 us
  matrix products: 8.81 us -> 0 us
  Pallas kernels: 23.5 us -> 31.5 us
  other arithmetic: 4.32 us -> 1.22 us
  waiting for transfers between devices: 41.1 us -> 43.6 us
    unnamed x44 -> x53, local copies, waits for them, and re-layouts: 27.7 us -> 13 us
    dot_general x3 -> x0, matrix products: 8.81 us -> none  [the longest x1 7.91 us: gathered_body(): jnp.dot(attended, out_weight, preferred_element_type=jnp.float32)]
    pallas_call x1 -> x2, Pallas kernels: 21.2 us -> 29.2 us  [the longest x1 20.9 us: run_expert(): pl.pallas_call(functools.partial(expert_kernel, parts, step), out_shape=[...]
    ppermute x15, waiting for transfers between devices: 14.5 us -> 17.1 us  [moved(): return lax.ppermute(array, AXES, pairs)]
    reshape x3 -> x0, local copies, waits for them, and re-layouts: 2.25 us -> none  [the longest x1 1.11 us: attend_group(): queries.astype(jnp.float32).reshape(length, q_heads, HEAD)]
  transfers between devices with their start and end apart: 21 -> 21, of which waited for: 13 -> 14; matrix products, arithmetic and copies ran while one was open for 21% -> 3% of each run, Pallas kernels for 0% -> 0%
where the time goes in v2:
time: 112 us; the launch traced here: 111 us
  waiting for transfers between devices  43.6 us (39%)
  Pallas kernels  31.5 us (28%)
  starting transfers between devices  19.8 us (18%)
  local copies, waits for them, and re-layouts  14.3 us (13%)
  other arithmetic  1.22 us (1%)
    ppermute x6, waiting for transfers between devices, crossed(): return lax.ppermute(array, AXES, pairs)  26.5 us
    pallas_call x1, Pallas kernels, run_expert(): pl.pallas_call(functools.partial(expert_kernel, parts, step), out_shape=[...  20.9 us
    ppermute x15, waiting for transfers between devices, moved(): return lax.ppermute(array, AXES, pairs)  17.1 us
    unnamed x53, local copies, waits for them, and re-layouts  13 us
    ppermute x15, starting transfers between devices, moved(): return lax.ppermute(array, AXES, pairs)  12.7 us
    pallas_call x1, Pallas kernels, run_attention(): pl.pallas_call(attention_kernel, out_shape=[jax.ShapeDtypeStruct((half, w...  8.25 us
    ppermute x6, starting transfers between devices, crossed(): return lax.ppermute(array, AXES, pairs)  7.13 us
    pallas_call x1, Pallas kernels, gathered_body(): pl.pallas_call(mid_kernel, out_shape=[jax.ShapeDtypeStruct((tok_count, wi...  2.33 us
  transfers between devices with their start and end apart: 21, of which 14 were waited for; matrix products, arithmetic and copies ran while one was open for 3% of the time, Pallas kernels for 0%

profile of v2, /device:TPU:0, one launch (start us, length us, event | category | flops | bytes accessed | tf_op | source)
XLA Modules:
  0.0 111.3 jit_solution(17729062481759833405)
XLA Ops:
  0.7 4.4 %copy-done = bf16[2048,2880]{0,1:T(8,128)(2,1)S(1)} copy-done((bf16[2048,2880]{0,1:T(8,128)(2,1)S(1)}, bf16[2048,2880]{0,1:T(8,128)(2,1)}, u32[]{:S(2)}) %copy-start) | copy-done | bytes 11796504
  5.0 0.9 copy-done.2
  5.9 0.8 copy-done.3
  9.3 8.2 %attention.1 = (f32[16,2880]{1,0:T(8,128)S(1)}, bf16[16,2880]{1,0:T(8,128)(2,1)S(1)}, bf16[2,16,512]{2,1,0:T(8,128)(2,1)}) custom-call(s32[1]{0:T(128)} %bitcast.side_ref, s32[1,2]{1,0:T(1,128)S(1)} %copy-done.4, f32[32]{0:T(128)S(1)} %copy-done.5, bf16[32,2048]{1,0:T(8,128)(2,1)S(1)} %copy-done.2, bf16[32,512]{1,0:T(8,128)(2,1)S(1)} %copy-done.3, ...), custom_call_target="tpu_custom_call" | custom-call | tf_op jit(solution)/shard_map/attention/pallas_call | solution.py:472
  18.3 3.0 %collective-permute-start = (bf16[16,2880]{1,0:T(8,128)(2,1)S(1)}, bf16[16,2880]{1,0:T(8,128)(2,1)S(1)}, u32[]{:S(2)}, u32[]{:S(2)}) collective-permute-start(bf16[16,2880]{1,0:T(8,128)(2,1)S(1)} %get-tuple-element.16), channel_id=1, source_target_pairs={{0,1},{1,0},{2,3},{3,2},{4,5},{5,4},{6,7},{7,6},{8,9},{9,8},{10,11... | collective-permute-start | bytes 276488 | tf_op jit(solution)/shard_map/ppermute | solution.py:553
  21.2 0.7 copy.20.ids_ref
  24.6 2.3 %norm_rows.1 = (f32[16,2880]{1,0:T(8,128)}, bf16[16,2944]{1,0:T(8,128)(2,1)}) custom-call(f32[16,2880]{1,0:T(8,128)} %copy-done.1, bf16[16,2880]{1,0:T(8,128)(2,1)} %copy-done.11, bf16[16,2880]{1,0:T(8,128)(2,1)} %residual_ref.1, bf16[1,2880]{1,0:T(2,128)(2,1)} %broadcast_in_dim.21.out_bias_ref, bf16[1,2880]{1,0:T(2,128)(2,1)} %broadcast_in_dim.22.gain_ref, ...), custom_call_target="tpu_custom_call" | custom-call | tf_op jit(solution)/shard_map/norm_rows/pallas_call | solution.py:624
  26.9 4.0 %collective-permute-start.3 = (bf16[16,2944]{1,0:T(8,128)(2,1)}, bf16[16,2944]{1,0:T(8,128)(2,1)S(1)}, u32[]{:S(2)}, u32[]{:S(2)}) collective-permute-start(bf16[16,2944]{1,0:T(8,128)(2,1)} %get-tuple-element.18), channel_id=1, source_target_pairs={{0,24},{1,25},{2,26},{3,27},{4,28},{5,29},{6,30},{7,31},{8,16},{9,... | collective-permute-start | bytes 282632 | tf_op jit(solution)/shard_map/ppermute | solution.py:553
  31.4 0.9 constant_dynamic-update-slice_fusion.3
  32.3 4.1 %collective-permute-done.1 = bf16[16,2944]{1,0:T(8,128)(2,1)S(1)} collective-permute-done((bf16[16,2944]{1,0:T(8,128)(2,1)}, bf16[16,2944]{1,0:T(8,128)(2,1)S(1)}, u32[]{:S(2)}, u32[]{:S(2)}) %collective-permute-start.1) | collective-permute-done | bytes 94240 | tf_op jit(solution)/shard_map/ppermute | solution.py:553
  36.5 1.7 %collective-permute-done.2 = bf16[16,2944]{1,0:T(8,128)(2,1)S(1)} collective-permute-done((bf16[16,2944]{1,0:T(8,128)(2,1)}, bf16[16,2944]{1,0:T(8,128)(2,1)S(1)}, u32[]{:S(2)}, u32[]{:S(2)}) %collective-permute-start.2) | collective-permute-done | bytes 94240 | tf_op jit(solution)/shard_map/ppermute | solution.py:553
  38.3 1.6 %collective-permute-start.4 = (bf16[64,2944]{1,0:T(8,128)(2,1)S(1)}, bf16[64,2944]{1,0:T(8,128)(2,1)S(1)}, u32[]{:S(2)}, u32[]{:S(2)}) collective-permute-start(bf16[64,2944]{1,0:T(8,128)(2,1)S(1)} %constant_dynamic-update-slice_fusion.refs_0_), channel_id=1, source_target_pairs={{0,4},{1,5},{2,3},{3,2},{4,0},{5,1},{6,7},{7,6},{8,12},{9,13},{10,... | collective-permute-start | bytes 1130504 | tf_op jit(solution)/shard_map/ppermute | solution.py:564
  39.8 1.3 %collective-permute-start.5 = (bf16[64,2944]{1,0:T(8,128)(2,1)S(1)}, bf16[64,2944]{1,0:T(8,128)(2,1)S(1)}, u32[]{:S(2)}, u32[]{:S(2)}) collective-permute-start(bf16[64,2944]{1,0:T(8,128)(2,1)S(1)} %constant_dynamic-update-slice_fusion.refs_0_), channel_id=1, source_target_pairs={{0,1},{1,0},{2,6},{3,7},{4,5},{5,4},{6,2},{7,3},{8,9},{9,8},{10,14... | collective-permute-start | bytes 1130504 | tf_op jit(solution)/shard_map/ppermute | solution.py:564
  41.1 8.6 %collective-permute-done.4.refs_1_ = bf16[64,2944]{1,0:T(8,128)(2,1)S(1)} collective-permute-done((bf16[64,2944]{1,0:T(8,128)(2,1)S(1)}, bf16[64,2944]{1,0:T(8,128)(2,1)S(1)}, u32[]{:S(2)}, u32[]{:S(2)}) %collective-permute-start.4) | collective-permute-done | bytes 376864 | tf_op jit(solution)/shard_map/ppermute | solution.py:564
  49.7 0.9 collective-permute-start.6
  51.2 6.2 %collective-permute-done.6.refs_3_ = bf16[64,2944]{1,0:T(8,128)(2,1)S(1)} collective-permute-done((bf16[64,2944]{1,0:T(8,128)(2,1)S(1)}, bf16[64,2944]{1,0:T(8,128)(2,1)S(1)}, u32[]{:S(2)}, u32[]{:S(2)}) %collective-permute-start.6) | collective-permute-done | bytes 376864 | tf_op jit(solution)/shard_map/ppermute | solution.py:564
  57.4 1.6 %collective-permute-done.10.refs_7_ = bf16[64,2944]{1,0:T(8,128)(2,1)S(1)} collective-permute-done((bf16[64,2944]{1,0:T(8,128)(2,1)S(1)}, bf16[64,2944]{1,0:T(8,128)(2,1)S(1)}, u32[]{:S(2)}, u32[]{:S(2)}) %collective-permute-start.10) | collective-permute-done | bytes 376864 | tf_op jit(solution)/shard_map/ppermute | solution.py:553
  59.1 0.7 copy-done.23
  59.8 20.9 %expert.1 = (bf16[64,2880]{1,0:T(8,128)(2,1)S(1)}, bf16[64,2880]{1,0:T(8,128)(2,1)S(1)}, bf16[64,2880]{1,0:T(8,128)(2,1)S(1)}, bf16[64,2880]{1,0:T(8,128)(2,1)S(...) custom-call(s32[1]{0:T(128)} %bitcast.3.expert_ref, ...), custom_call_target="tpu_custom_call" | custom-call | flops 7880048640 | bytes 24883200 | tf_op jit(solution)/shard_map/expert/pallas_call | solution.py:517
  81.8 0.9 collective-permute-done.15
  82.8 0.9 collective-permute-start.16
  83.9 1.2 %collective-permute-start.13 = (bf16[64,2880]{1,0:T(8,128)(2,1)S(1)}, bf16[64,2880]{1,0:T(8,128)(2,1)S(1)}, u32[]{:S(2)}, u32[]{:S(2)}) collective-permute-start(bf16[64,2880]{1,0:T(8,128)(2,1)S(1)} %add_convert_fusion.5), channel_id=1, source_target_pairs={{0,1},{1,0},{2,6},{3,7},{4,5},{5,4},{6,2},{7,3},{8,9},{9,8},{10,14... | collective-permute-start | bytes 1105928 | tf_op jit(solution)/shard_map/ppermute | solution.py:564
  85.1 5.4 %collective-permute-done.16 = bf16[64,2880]{1,0:T(8,128)(2,1)S(1)} collective-permute-done((bf16[64,2880]{1,0:T(8,128)(2,1)S(1)}, bf16[64,2880]{1,0:T(8,128)(2,1)S(1)}, u32[]{:S(2)}, u32[]{:S(2)}) %collective-permute-start.16) | collective-permute-done | bytes 368672 | tf_op jit(solution)/shard_map/ppermute | solution.py:564
  90.6 1.3 %collective-permute-start.17 = (bf16[64,2880]{1,0:T(8,128)(2,1)S(1)}, bf16[64,2880]{1,0:T(8,128)(2,1)S(1)}, u32[]{:S(2)}, u32[]{:S(2)}) collective-permute-start(bf16[64,2880]{1,0:T(8,128)(2,1)S(1)} %add_convert_fusion.1), channel_id=1, source_target_pairs={{0,4},{1,5},{2,3},{3,2},{4,0},{5,1},{6,7},{7,6},{8,12},{9,13},{10,... | collective-permute-start | bytes 1105928 | tf_op jit(solution)/shard_map/ppermute | solution.py:564
  92.0 4.4 %collective-permute-done.13 = bf16[64,2880]{1,0:T(8,128)(2,1)S(1)} collective-permute-done((bf16[64,2880]{1,0:T(8,128)(2,1)S(1)}, bf16[64,2880]{1,0:T(8,128)(2,1)S(1)}, u32[]{:S(2)}, u32[]{:S(2)}) %collective-permute-start.13) | collective-permute-done | bytes 368672 | tf_op jit(solution)/shard_map/ppermute | solution.py:564
  96.4 1.9 %collective-permute-done.17 = bf16[64,2880]{1,0:T(8,128)(2,1)S(1)} collective-permute-done((bf16[64,2880]{1,0:T(8,128)(2,1)S(1)}, bf16[64,2880]{1,0:T(8,128)(2,1)S(1)}, u32[]{:S(2)}, u32[]{:S(2)}) %collective-permute-start.17) | collective-permute-done | bytes 368672 | tf_op jit(solution)/shard_map/ppermute | solution.py:564
  98.6 1.9 %collective-permute-start.20 = (bf16[16,2880]{1,0:T(8,128)(2,1)S(1)}, bf16[16,2880]{1,0:T(8,128)(2,1)S(1)}, u32[]{:S(2)}, u32[]{:S(2)}) collective-permute-start(bf16[16,2880]{1,0:T(8,128)(2,1)S(1)} %get-tuple-element.29), channel_id=1, source_target_pairs={{0,24},{1,25},{2,26},{3,27},{4,28},{5,29},{6,30},{7,31},{8,16},{9,... | collective-permute-start | bytes 276488 | tf_op jit(solution)/shard_map/ppermute | solution.py:553
  100.5 1.5 %collective-permute-start.19 = (bf16[16,2880]{1,0:T(8,128)(2,1)S(1)}, bf16[16,2880]{1,0:T(8,128)(2,1)S(1)}, u32[]{:S(2)}, u32[]{:S(2)}) collective-permute-start(bf16[16,2880]{1,0:T(8,128)(2,1)S(1)} %get-tuple-element.30), channel_id=1, source_target_pairs={{0,16},{1,17},{2,18},{3,19},{4,20},{5,21},{6,22},{7,23},{8,24},{9,... | collective-permute-start | bytes 276488 | tf_op jit(solution)/shard_map/ppermute | solution.py:553
  102.1 1.3 %collective-permute-done.18 = bf16[16,2880]{1,0:T(8,128)(2,1)S(1)} collective-permute-done((bf16[16,2880]{1,0:T(8,128)(2,1)S(1)}, bf16[16,2880]{1,0:T(8,128)(2,1)S(1)}, u32[]{:S(2)}, u32[]{:S(2)}) %collective-permute-start.18) | collective-permute-done | bytes 92192 | tf_op jit(solution)/shard_map/ppermute | solution.py:553
  103.4 2.7 %collective-permute-done.20 = bf16[16,2880]{1,0:T(8,128)(2,1)S(1)} collective-permute-done((bf16[16,2880]{1,0:T(8,128)(2,1)S(1)}, bf16[16,2880]{1,0:T(8,128)(2,1)S(1)}, u32[]{:S(2)}, u32[]{:S(2)}) %collective-permute-start.20) | collective-permute-done | bytes 92192 | tf_op jit(solution)/shard_map/ppermute | solution.py:553
  106.1 4.4 %collective-permute-done.19 = bf16[16,2880]{1,0:T(8,128)(2,1)S(1)} collective-permute-done((bf16[16,2880]{1,0:T(8,128)(2,1)S(1)}, bf16[16,2880]{1,0:T(8,128)(2,1)S(1)}, u32[]{:S(2)}, u32[]{:S(2)}) %collective-permute-start.19) | collective-permute-done | bytes 92192 | tf_op jit(solution)/shard_map/ppermute | solution.py:553
  110.6 0.7 add_convert_fusion.7
  (75 shorter events, 9.0 us)
Async XLA Ops:
  0.6 20.6 %copy-start.15 = (s32[16,4]{0,1:T(4,128)S(1)}, s32[16,4]{0,1:T(4,128)}, u32[]{:S(2)}) copy-start(s32[16,4]{0,1:T(4,128)} %param.26) | copy-start | bytes 772
  0.6 21.3 %copy-start.16 = (f32[16,4]{0,1:T(4,128)S(1)}, f32[16,4]{0,1:T(4,128)}, u32[]{:S(2)}) copy-start(f32[16,4]{0,1:T(4,128)} %param.27) | copy-start | bytes 772
  0.7 59.1 %copy-start.8 = (bf16[1,1440]{1,0:T(2,128)(2,1)S(1)}, bf16[1,1440]{1,0:T(2,128)(2,1)}, u32[]{:S(2)}) copy-start(bf16[1,1440]{1,0:T(2,128)(2,1)} %refs_11_.1) | copy-start | bytes 8644
  0.7 4.4 %copy-start = (bf16[2048,2880]{0,1:T(8,128)(2,1)S(1)}, bf16[2048,2880]{0,1:T(8,128)(2,1)}, u32[]{:S(2)}) copy-start(bf16[2048,2880]{0,1:T(8,128)(2,1)} %param.22) | copy-start | bytes 35389444
  9.3 13.3 %copy-start.13 = (bf16[2880]{0:T(1024)(128)(2,1)S(1)}, bf16[2880]{0:T(1024)(128)(2,1)}, u32[]{:S(2)}) copy-start(bf16[2880]{0:T(1024)(128)(2,1)} %param.23) | copy-start | bytes 17284
  9.3 13.9 %copy-start.14 = (bf16[2880]{0:T(1024)(128)(2,1)S(1)}, bf16[2880]{0:T(1024)(128)(2,1)}, u32[]{:S(2)}) copy-start(bf16[2880]{0:T(1024)(128)(2,1)} %param.25) | copy-start | bytes 17284
  9.3 50.5 %copy-start.9 = (bf16[1,1440]{1,0:T(2,128)(2,1)S(1)}, bf16[1,1440]{1,0:T(2,128)(2,1)}, u32[]{:S(2)}) copy-start(bf16[1,1440]{1,0:T(2,128)(2,1)} %refs_12_.1) | copy-start | bytes 8644
  18.3 5.7 %collective-permute-start = (bf16[16,2880]{1,0:T(8,128)(2,1)S(1)}, bf16[16,2880]{1,0:T(8,128)(2,1)S(1)}, u32[]{:S(2)}, u32[]{:S(2)}) collective-permute-start(bf16[16,2880]{1,0:T(8,128)(2,1)S(1)} %get-tuple-element.16), channel_id=1, source_target_pairs={{0,1},{1,0},{2,3},{3,2},{4,5},{5,4},{6,7},{7,6},{8,9},{9,8},{10,11... | collective-permute-start | bytes 276488 | tf_op jit(solution)/shard_map/ppermute | solution.py:553
  26.9 11.3 %collective-permute-start.3 = (bf16[16,2944]{1,0:T(8,128)(2,1)}, bf16[16,2944]{1,0:T(8,128)(2,1)S(1)}, u32[]{:S(2)}, u32[]{:S(2)}) collective-permute-start(bf16[16,2944]{1,0:T(8,128)(2,1)} %get-tuple-element.18), channel_id=1, source_target_pairs={{0,24},{1,25},{2,26},{3,27},{4,28},{5,29},{6,30},{7,31},{8,16},{9,... | collective-permute-start | bytes 282632 | tf_op jit(solution)/shard_map/ppermute | solution.py:553
  30.8 7.4 %collective-permute-start.2 = (bf16[16,2944]{1,0:T(8,128)(2,1)}, bf16[16,2944]{1,0:T(8,128)(2,1)S(1)}, u32[]{:S(2)}, u32[]{:S(2)}) collective-permute-start(bf16[16,2944]{1,0:T(8,128)(2,1)} %get-tuple-element.18), channel_id=1, source_target_pairs={{0,16},{1,17},{2,18},{3,19},{4,20},{5,21},{6,22},{7,23},{8,24},{9,... | collective-permute-start | bytes 282632 | tf_op jit(solution)/shard_map/ppermute | solution.py:553
  30.8 5.6 %collective-permute-start.1 = (bf16[16,2944]{1,0:T(8,128)(2,1)}, bf16[16,2944]{1,0:T(8,128)(2,1)S(1)}, u32[]{:S(2)}, u32[]{:S(2)}) collective-permute-start(bf16[16,2944]{1,0:T(8,128)(2,1)} %get-tuple-element.18), channel_id=1, source_target_pairs={{0,8},{1,9},{2,10},{3,11},{4,12},{5,13},{6,14},{7,15},{8,0},{9,1},... | collective-permute-start | bytes 282632 | tf_op jit(solution)/shard_map/ppermute | solution.py:553
  38.3 20.8 %copy-start.12 = (bf16[64,2944]{1,0:T(8,128)(2,1)}, bf16[64,2944]{1,0:T(8,128)(2,1)S(1)}, u32[]{:S(2)}) copy-start(bf16[64,2944]{1,0:T(8,128)(2,1)S(1)} %constant_dynamic-update-slice_fusion.refs_0_) | copy-start | bytes 1130500
  38.3 11.5 %collective-permute-start.4 = (bf16[64,2944]{1,0:T(8,128)(2,1)S(1)}, bf16[64,2944]{1,0:T(8,128)(2,1)S(1)}, u32[]{:S(2)}, u32[]{:S(2)}) collective-permute-start(bf16[64,2944]{1,0:T(8,128)(2,1)S(1)} %constant_dynamic-update-slice_fusion.refs_0_), channel_id=1, source_target_pairs={{0,4},{1,5},{2,3},{3,2},{4,0},{5,1},{6,7},{7,6},{8,12},{9,13},{10,... | collective-permute-start | bytes 1130504 | tf_op jit(solution)/shard_map/ppermute | solution.py:564
  39.8 11.3 %collective-permute-start.5 = (bf16[64,2944]{1,0:T(8,128)(2,1)S(1)}, bf16[64,2944]{1,0:T(8,128)(2,1)S(1)}, u32[]{:S(2)}, u32[]{:S(2)}) collective-permute-start(bf16[64,2944]{1,0:T(8,128)(2,1)S(1)} %constant_dynamic-update-slice_fusion.refs_0_), channel_id=1, source_target_pairs={{0,1},{1,0},{2,6},{3,7},{4,5},{5,4},{6,2},{7,3},{8,9},{9,8},{10,14... | collective-permute-start | bytes 1130504 | tf_op jit(solution)/shard_map/ppermute | solution.py:564
  49.7 9.3 %copy-start.17 = (bf16[64,2944]{1,0:T(8,128)(2,1)}, bf16[64,2944]{1,0:T(8,128)(2,1)S(1)}, u32[]{:S(2)}) copy-start(bf16[64,2944]{1,0:T(8,128)(2,1)S(1)} %collective-permute-done.4.refs_1_) | copy-start | bytes 1130500
  49.7 7.6 %collective-permute-start.6 = (bf16[64,2944]{1,0:T(8,128)(2,1)S(1)}, bf16[64,2944]{1,0:T(8,128)(2,1)S(1)}, u32[]{:S(2)}, u32[]{:S(2)}) collective-permute-start(bf16[64,2944]{1,0:T(8,128)(2,1)S(1)} %collective-permute-done.4.refs_1_), channel_id=1, source_target_pairs={{0,1},{1,0},{2,6},{3,7},{4,5},{5,4},{6,2},{7,3},{8,9},{9,8},{10,14... | collective-permute-start | bytes 1130504 | tf_op jit(solution)/shard_map/ppermute | solution.py:564
  50.6 6.8 %collective-permute-start.7 = (bf16[64,2944]{1,0:T(8,128)(2,1)S(1)}, bf16[64,2944]{1,0:T(8,128)(2,1)S(1)}, u32[]{:S(2)}, u32[]{:S(2)}) collective-permute-start(bf16[64,2944]{1,0:T(8,128)(2,1)S(1)} %constant_dynamic-update-slice_fusion.refs_0_), channel_id=1, source_target_pairs={{0,2},{1,3},{2,0},{3,1},{4,6},{5,7},{6,4},{7,5},{8,10},{9,11},{10,... | collective-permute-start | bytes 1130504 | tf_op jit(solution)/shard_map/ppermute | solution.py:553
  50.6 6.8 %collective-permute-start.8 = (bf16[64,2944]{1,0:T(8,128)(2,1)S(1)}, bf16[64,2944]{1,0:T(8,128)(2,1)S(1)}, u32[]{:S(2)}, u32[]{:S(2)}) collective-permute-start(bf16[64,2944]{1,0:T(8,128)(2,1)S(1)} %collective-permute-done.4.refs_1_), channel_id=1, source_target_pairs={{0,2},{1,3},{2,0},{3,1},{4,6},{5,7},{6,4},{7,5},{8,10},{9,11},{10,... | collective-permute-start | bytes 1130504 | tf_op jit(solution)/shard_map/ppermute | solution.py:553
  51.1 7.9 %copy-start.18 = (bf16[64,2944]{1,0:T(8,128)(2,1)}, bf16[64,2944]{1,0:T(8,128)(2,1)S(1)}, u32[]{:S(2)}) copy-start(bf16[64,2944]{1,0:T(8,128)(2,1)S(1)} %collective-permute-done.5.refs_2_) | copy-start | bytes 1130500
  51.1 6.3 %collective-permute-start.9 = (bf16[64,2944]{1,0:T(8,128)(2,1)S(1)}, bf16[64,2944]{1,0:T(8,128)(2,1)S(1)}, u32[]{:S(2)}, u32[]{:S(2)}) collective-permute-start(bf16[64,2944]{1,0:T(8,128)(2,1)S(1)} %collective-permute-done.5.refs_2_), channel_id=1, source_target_pairs={{0,2},{1,3},{2,0},{3,1},{4,6},{5,7},{6,4},{7,5},{8,10},{9,11},{10,... | collective-permute-start | bytes 1130504 | tf_op jit(solution)/shard_map/ppermute | solution.py:553
  57.3 1.7 %collective-permute-start.10 = (bf16[64,2944]{1,0:T(8,128)(2,1)S(1)}, bf16[64,2944]{1,0:T(8,128)(2,1)S(1)}, u32[]{:S(2)}, u32[]{:S(2)}) collective-permute-start(bf16[64,2944]{1,0:T(8,128)(2,1)S(1)} %collective-permute-done.6.refs_3_), channel_id=1, source_target_pairs={{0,2},{1,3},{2,0},{3,1},{4,6},{5,7},{6,4},{7,5},{8,10},{9,11},{10,... | collective-permute-start | bytes 1130504 | tf_op jit(solution)/shard_map/ppermute | solution.py:553
  59.8 50.7 %copy-start.10 = (f32[16,2880]{1,0:T(8,128)S(1)}, f32[16,2880]{1,0:T(8,128)}, u32[]{:S(2)}) copy-start(f32[16,2880]{1,0:T(8,128)} %get-tuple-element.17) | copy-start | bytes 552964
  80.7 2.0 %collective-permute-start.15 = (bf16[64,2880]{1,0:T(8,128)(2,1)}, bf16[64,2880]{1,0:T(8,128)(2,1)S(1)}, u32[]{:S(2)}, u32[]{:S(2)}) collective-permute-start(bf16[64,2880]{1,0:T(8,128)(2,1)} %get-tuple-element.26), channel_id=1, source_target_pairs={{0,2},{1,3},{2,0},{3,1},{4,6},{5,7},{6,4},{7,5},{8,10},{9,11},{10,... | collective-permute-start | bytes 1105928 | tf_op jit(solution)/shard_map/ppermute | solution.py:553
  80.9 11.0 %collective-permute-start.11 = (bf16[64,2880]{1,0:T(8,128)(2,1)S(1)}, bf16[64,2880]{1,0:T(8,128)(2,1)S(1)}, u32[]{:S(2)}, u32[]{:S(2)}) collective-permute-start(bf16[64,2880]{1,0:T(8,128)(2,1)S(1)} %get-tuple-element.20), channel_id=1, source_target_pairs={{0,2},{1,3},{2,0},{3,1},{4,6},{5,7},{6,4},{7,5},{8,10},{9,11},{10,... | collective-permute-start | bytes 1105928 | tf_op jit(solution)/shard_map/ppermute | solution.py:553
  81.3 2.5 %collective-permute-start.12 = (bf16[64,2880]{1,0:T(8,128)(2,1)}, bf16[64,2880]{1,0:T(8,128)(2,1)S(1)}, u32[]{:S(2)}, u32[]{:S(2)}) collective-permute-start(bf16[64,2880]{1,0:T(8,128)(2,1)} %get-tuple-element.22), channel_id=1, source_target_pairs={{0,2},{1,3},{2,0},{3,1},{4,6},{5,7},{6,4},{7,5},{8,10},{9,11},{10,... | collective-permute-start | bytes 1105928 | tf_op jit(solution)/shard_map/ppermute | solution.py:553
  81.5 3.6 %collective-permute-start.14 = (bf16[64,2880]{1,0:T(8,128)(2,1)}, bf16[64,2880]{1,0:T(8,128)(2,1)S(1)}, u32[]{:S(2)}, u32[]{:S(2)}) collective-permute-start(bf16[64,2880]{1,0:T(8,128)(2,1)} %get-tuple-element.24), channel_id=1, source_target_pairs={{0,2},{1,3},{2,0},{3,1},{4,6},{5,7},{6,4},{7,5},{8,10},{9,11},{10,... | collective-permute-start | bytes 1105928 | tf_op jit(solution)/shard_map/ppermute | solution.py:553
  82.8 7.7 %collective-permute-start.16 = (bf16[64,2880]{1,0:T(8,128)(2,1)S(1)}, bf16[64,2880]{1,0:T(8,128)(2,1)S(1)}, u32[]{:S(2)}, u32[]{:S(2)}) collective-permute-start(bf16[64,2880]{1,0:T(8,128)(2,1)S(1)} %add_convert_fusion.2), channel_id=1, source_target_pairs={{0,1},{1,0},{2,6},{3,7},{4,5},{5,4},{6,2},{7,3},{8,9},{9,8},{10,14... | collective-permute-start | bytes 1105928 | tf_op jit(solution)/shard_map/ppermute | solution.py:564
  83.9 12.5 %collective-permute-start.13 = (bf16[64,2880]{1,0:T(8,128)(2,1)S(1)}, bf16[64,2880]{1,0:T(8,128)(2,1)S(1)}, u32[]{:S(2)}, u32[]{:S(2)}) collective-permute-start(bf16[64,2880]{1,0:T(8,128)(2,1)S(1)} %add_convert_fusion.5), channel_id=1, source_target_pairs={{0,1},{1,0},{2,6},{3,7},{4,5},{5,4},{6,2},{7,3},{8,9},{9,8},{10,14... | collective-permute-start | bytes 1105928 | tf_op jit(solution)/shard_map/ppermute | solution.py:564
  90.6 7.7 %collective-permute-start.17 = (bf16[64,2880]{1,0:T(8,128)(2,1)S(1)}, bf16[64,2880]{1,0:T(8,128)(2,1)S(1)}, u32[]{:S(2)}, u32[]{:S(2)}) collective-permute-start(bf16[64,2880]{1,0:T(8,128)(2,1)S(1)} %add_convert_fusion.1), channel_id=1, source_target_pairs={{0,4},{1,5},{2,3},{3,2},{4,0},{5,1},{6,7},{7,6},{8,12},{9,13},{10,... | collective-permute-start | bytes 1105928 | tf_op jit(solution)/shard_map/ppermute | solution.py:564
  98.5 4.9 %collective-permute-start.18 = (bf16[16,2880]{1,0:T(8,128)(2,1)S(1)}, bf16[16,2880]{1,0:T(8,128)(2,1)S(1)}, u32[]{:S(2)}, u32[]{:S(2)}) collective-permute-start(bf16[16,2880]{1,0:T(8,128)(2,1)S(1)} %get-tuple-element.28), channel_id=1, source_target_pairs={{0,8},{1,9},{2,10},{3,11},{4,12},{5,13},{6,14},{7,15},{8,0},{9,1},... | collective-permute-start | bytes 276488 | tf_op jit(solution)/shard_map/ppermute | solution.py:553
  98.6 7.5 %collective-permute-start.20 = (bf16[16,2880]{1,0:T(8,128)(2,1)S(1)}, bf16[16,2880]{1,0:T(8,128)(2,1)S(1)}, u32[]{:S(2)}, u32[]{:S(2)}) collective-permute-start(bf16[16,2880]{1,0:T(8,128)(2,1)S(1)} %get-tuple-element.29), channel_id=1, source_target_pairs={{0,24},{1,25},{2,26},{3,27},{4,28},{5,29},{6,30},{7,31},{8,16},{9,... | collective-permute-start | bytes 276488 | tf_op jit(solution)/shard_map/ppermute | solution.py:553
  100.5 10.0 %collective-permute-start.19 = (bf16[16,2880]{1,0:T(8,128)(2,1)S(1)}, bf16[16,2880]{1,0:T(8,128)(2,1)S(1)}, u32[]{:S(2)}, u32[]{:S(2)}) collective-permute-start(bf16[16,2880]{1,0:T(8,128)(2,1)S(1)} %get-tuple-element.30), channel_id=1, source_target_pairs={{0,16},{1,17},{2,18},{3,19},{4,20},{5,21},{6,22},{7,23},{8,24},{9,... | collective-permute-start | bytes 276488 | tf_op jit(solution)/shard_map/ppermute | solution.py:553
  (13 other events, 13.2 us)

commit v3 on v2

--- a/solution.py
+++ b/solution.py
@@ -11,6 +11,8 @@
 HEAD = 64
 PAGE_LEN = 16
 LANES = 128
+VMEM_LIMIT = 60 * 2**20
+LOAD_ROWS = 480
 
 
 rope_base = 150000.0
@@ -233,19 +235,21 @@
         * gain_ref[...].astype(jnp.float32)
     ).astype(jnp.bfloat16)
     logits = logits_ref[...]
-    expo = jnp.exp(logits - jnp.max(logits, axis=-1, keepdims=True))
-    weights = expo / jnp.sum(expo, axis=-1, keepdims=True)
+    expo = jnp.exp(logits - jnp.max(logits, axis=0, keepdims=True))
+    weights = expo / jnp.sum(expo, axis=0, keepdims=True)
     high = weights.astype(jnp.bfloat16).astype(jnp.float32)
     low = (weights - high).astype(jnp.bfloat16).astype(jnp.float32)
     ids = ids_ref[...]
-    lanes = lax.broadcasted_iota(jnp.int32, (ids.shape[0], LANES), 1)
-    high_cols = jnp.zeros(lanes.shape, jnp.float32)
-    low_cols = jnp.zeros(lanes.shape, jnp.float32)
+    column = lax.broadcasted_iota(jnp.int32, (LANES, ids.shape[1]), 0)
+    high_cols = jnp.zeros(column.shape, jnp.float32)
+    low_cols = jnp.zeros(column.shape, jnp.float32)
     first = width % LANES
-    for k in range(ids.shape[1]):
-        at = ids[:, k : k + 1] + first
-        high_cols = high_cols + jnp.where(lanes == at, high[:, k : k + 1], 0.0)
-        low_cols = low_cols + jnp.where(lanes == at + experts, low[:, k : k + 1], 0.0)
+    for k in range(ids.shape[0]):
+        at = ids[k : k + 1] + first
+        high_cols = high_cols + jnp.where(column == at, high[k : k + 1], 0.0)
+        low_cols = low_cols + jnp.where(column == at + experts, low[k : k + 1], 0.0)
+    high_cols = high_cols.T
+    low_cols = low_cols.T
     high_dense = high_cols[:, first : first + experts].astype(jnp.bfloat16)
     low_dense = low_cols[:, first + experts : first + 2 * experts].astype(jnp.bfloat16)
     bias = down_bias_ref[...]
@@ -262,107 +266,121 @@
     return [(start, min(step, total - start)) for start in range(0, total, step)]
 
 
-def expert_kernel(parts, step, expert_ref, *refs):
+def by_rows(left, right):
+    return lax.dot_general(
+        left, right, (((1,), (1,)), ((), ())), preferred_element_type=jnp.float32
+    )
+
+
+def load_kernel(parts, *refs):
+    sources, targets, sign, sems = refs[:parts], refs[parts : 2 * parts], refs[-2], refs[-1]
+    copies = []
+    for source, target in zip(sources, targets):
+        for start, size in tiles(source.shape[0], LOAD_ROWS):
+            here = pl.ds(start, size)
+            copies.append(
+                pltpu.make_async_copy(source.at[here], target.at[here], sems.at[len(copies)])
+            )
+    for copy in copies:
+        copy.start()
+    for copy in copies:
+        copy.wait()
+    sign[...] = targets[0][: sign.shape[0], : sign.shape[1]]
+
+
+def load(weights, reserve):
+    parts = len(weights)
+    copies = sum(len(tiles(weight.shape[0], LOAD_ROWS)) for weight in weights)
+    return pl.pallas_call(
+        functools.partial(load_kernel, parts),
+        out_shape=[jax.ShapeDtypeStruct(weight.shape, weight.dtype) for weight in weights]
+        + [jax.ShapeDtypeStruct((16, LANES), weights[0].dtype)],
+        in_specs=[anywhere()] * parts,
+        out_specs=[vmem()] * (parts + 1),
+        scratch_shapes=[pltpu.SemaphoreType.DMA((copies,))],
+        compiler_params=pltpu.CompilerParams(vmem_limit_bytes=reserve),
+        cost_estimate=pl.CostEstimate(
+            flops=0, bytes_accessed=4 * sum(w.size for w in weights), transcendentals=0
+        ),
+        name="load",
+    )(*weights)
+
+
+def expert_kernel(parts, block, limit, step, expert_ref, *refs):
     pieces, refs = refs[:parts], refs[parts:]
-    gate_hbm, up_hbm, down_hbm, gate_bias_ref, up_bias_ref = refs[:5]
-    outs, refs = refs[5 : 5 + parts], refs[5 + parts :]
-    rows, picked, gate_up, down_w, active, spread, sems = refs
-    piece = pieces[0].shape[0]
-    total = rows.shape[0]
-    slots = picked.shape[0]
+    gate_w, up_w, down_w, gate_bias_ref, up_bias_ref = refs[:5]
+    outs, (picked, active) = refs[7 : 7 + parts], refs[7 + parts :]
+    piece, padded = pieces[0].shape
+    total = parts * piece
     units, width = down_w.shape
-    row_copies = [
-        pltpu.make_async_copy(p, rows.at[pl.ds(i * piece, piece)], sems.at[i])
-        for i, p in enumerate(pieces)
-    ]
-    chunks = tiles(units, step)
-    up_copies = []
-    for i, (start, size) in enumerate(chunks):
-        for side, source in enumerate((gate_hbm, up_hbm)):
-            up_copies.append(
-                pltpu.make_async_copy(
-                    source.at[pl.ds(start, size)],
-                    gate_up.at[pl.ds(2 * start + side * size, size)],
-                    sems.at[parts + 2 * i + side],
-                )
-            )
-    blocks = tiles(width, 2 * step)
-    down_copies = [
-        pltpu.make_async_copy(
-            down_hbm.at[:, pl.ds(start, size)],
-            down_w.at[:, pl.ds(start, size)],
-            sems.at[parts + 2 * len(chunks) + i],
-        )
-        for i, (start, size) in enumerate(blocks)
-    ]
-    for copy in row_copies + up_copies + down_copies:
-        copy.start()
+    group = 2 * piece
+    group_slots = group // block * limit
     up_bias = jnp.broadcast_to(up_bias_ref[...].astype(jnp.float32), (8, units)).T
     gate_bias = jnp.broadcast_to(gate_bias_ref[...].astype(jnp.float32), (8, units)).T
-    earlier = jnp.where(
-        lax.broadcasted_iota(jnp.int32, (total, total), 0)
-        <= lax.broadcasted_iota(jnp.int32, (total, total), 1),
-        1.0,
-        0.0,
-    ).astype(jnp.bfloat16)
-    for copy in row_copies:
-        copy.wait()
 
     expert = expert_ref[0]
-    experts = (rows.shape[1] - width) // 4
+    experts = (padded - width) // 4
     lane = lax.broadcasted_iota(jnp.int32, (16, LANES), 1)
     which = lax.broadcasted_iota(jnp.int32, (16, LANES), 0)
     choose = jnp.where(
         (lane == width % LANES + expert + which * experts) & (which < 2), 1.0, 0.0
     ).astype(jnp.bfloat16)
-    found = lax.dot_general(
-        choose,
-        rows[:, rows.shape[1] - LANES :],
-        (((1,), (1,)), ((), ())),
-        preferred_element_type=jnp.float32,
-    )
-    share = found[0:1] + found[1:2]
+    found = by_rows(
+        choose, jnp.concatenate([p[:, padded - LANES :] for p in pieces], axis=0)
+    )
+    share = jnp.broadcast_to(found[0:1] + found[1:2], (8, total))
     chosen = share > 0.0
-    marks = jnp.broadcast_to(jnp.where(chosen, 1.0, 0.0), (16, total)).astype(jnp.bfloat16)
-    count = jnp.dot(marks, earlier, preferred_element_type=jnp.float32)[0:1]
-    slot = jnp.where(chosen, count - 1.0, -1.0).astype(jnp.int32)
-    hit = lax.broadcasted_iota(jnp.int32, (slots, total), 0) == slot
-    pick_f32 = jnp.where(hit, 1.0, 0.0)
-    pick = pick_f32.astype(jnp.bfloat16)
-    slot_share = jnp.sum(jnp.where(hit, share, 0.0), axis=1, keepdims=True)
-    spread[...] = pick_f32.T.astype(jnp.bfloat16)
-    for start, size in tiles(width, 512):
-        picked[:, start : start + size] = jnp.dot(
-            pick, rows[:, start : start + size], preferred_element_type=jnp.float32
-        ).astype(jnp.bfloat16)
-
-    for i, (start, size) in enumerate(chunks):
-        up_copies[2 * i].wait()
-        up_copies[2 * i + 1].wait()
-        both = lax.dot_general(
-            gate_up[2 * start : 2 * (start + size)],
-            picked[...],
-            (((1,), (1,)), ((), ())),
-            preferred_element_type=jnp.float32,
+    token = lax.broadcasted_iota(jnp.int32, (8, total), 1)
+    count = jnp.where(chosen, 1, 0)
+    reach = 1
+    while reach < block:
+        count = count + jnp.where(token % block >= reach, pltpu.roll(count, reach, 1), 0)
+        reach *= 2
+    slot = jnp.where(chosen, token // block * limit + count - 1, -1)
+    spreads, shares = [], []
+    for g in range(total // group):
+        here = slice(g * group, (g + 1) * group)
+        hit = (
+            lax.broadcasted_iota(jnp.int32, (group_slots, group), 0) + g * group_slots
+            == slot[0:1, here]
         )
-        gate = jnp.minimum(both[:size] + gate_bias[start : start + size, 0:1], swiglu_limit)
-        up = jnp.clip(both[size:] + up_bias[start : start + size, 0:1], -swiglu_limit, swiglu_limit)
+        shares.append(jnp.sum(jnp.where(hit, share[0:1, here], 0.0), axis=1, keepdims=True))
+        pick = jnp.where(hit, 1.0, 0.0)
+        spreads.append(pick.T.astype(jnp.bfloat16))
+        pick = pick.astype(jnp.bfloat16)
+        for start, size in tiles(width, 2 * step):
+            cols = slice(start, start + size)
+            both = jnp.concatenate([pieces[2 * g][:, cols], pieces[2 * g + 1][:, cols]], axis=0)
+            picked[g * group_slots : (g + 1) * group_slots, cols] = jnp.dot(
+                pick, both, preferred_element_type=jnp.float32
+            ).astype(jnp.bfloat16)
+    slot_share = jnp.concatenate(shares, axis=0)
+
+    for start, size in tiles(units, step):
+        here = slice(start, start + size)
+        gate = by_rows(gate_w[here], picked[...])
+        up = by_rows(up_w[here], picked[...])
+        gate = jnp.minimum(gate + gate_bias[here, 0:1], swiglu_limit)
+        up = jnp.clip(up + up_bias[here, 0:1], -swiglu_limit, swiglu_limit)
         value = gate * (1.0 / (1.0 + jnp.exp(-glu_alpha * gate))) * (up + 1.0)
-        active[:, start : start + size] = value.T.astype(jnp.bfloat16)
-    for i, (start, size) in enumerate(blocks):
-        down_copies[i].wait()
+        active[:, here] = value.T.astype(jnp.bfloat16)
+    for start, size in tiles(width, 2 * step):
         cols = slice(start, start + size)
         value = jnp.dot(active[...], down_w[:, cols], preferred_element_type=jnp.float32)
         scaled = (value * slot_share).astype(jnp.bfloat16)
-        spread_rows = jnp.dot(spread[...], scaled, preferred_element_type=jnp.float32).astype(
-            jnp.bfloat16
-        )
-        for k, out in enumerate(outs):
-            out[:, cols] = spread_rows[k * piece : (k + 1) * piece]
+        for g, spread in enumerate(spreads):
+            sums = jnp.dot(
+                spread,
+                scaled[g * group_slots : (g + 1) * group_slots],
+                preferred_element_type=jnp.float32,
+            ).astype(jnp.bfloat16)
+            outs[2 * g][:, cols] = sums[:piece]
+            outs[2 * g + 1][:, cols] = sums[piece:]
 
 
 def attention_kernel(
     side_ref,
+    expert_in_ref,
     pages_ref,
     sink_ref,
     queries_ref,
@@ -373,10 +391,12 @@
     own_ref,
     other_ref,
     cache_ref,
+    expert_ref,
     weight,
     attended,
     sems,
 ):
+    expert_ref[0] = expert_in_ref[0]
     length, query_width = queries_ref.shape
     width = weight.shape[0]
     kv_heads = keys_values_ref.shape[1] // LANES
@@ -388,7 +408,7 @@
         )
         for i, (start, size) in enumerate(chunks)
     ]
-    for copy in copies:
+    for copy in copies[:2]:
         copy.start()
     named = jnp.broadcast_to(segments_ref[...].astype(jnp.float32), (length, length))
     visible = (named == named.T) & (
@@ -450,18 +470,15 @@
     half = own_ref.shape[0]
     for i, (start, size) in enumerate(chunks):
         copies[i].wait()
-        projected = lax.dot_general(
-            attended[...],
-            weight[start : start + size],
-            (((1,), (1,)), ((), ())),
-            preferred_element_type=jnp.float32,
-        )
+        if i + 2 < len(copies):
+            copies[i + 2].start()
+        projected = by_rows(attended[...], weight[start : start + size])
         top, bottom = projected[:half], projected[half:]
         own_ref[:, start : start + size] = jnp.where(first_side, top, bottom)
         other_ref[:, start : start + size] = jnp.where(first_side, bottom, top).astype(jnp.bfloat16)
 
 
-def run_attention(side, page_table, sink_logits, queries, keys_values, segments, out_weight):
+def run_attention(side, expert, page_table, sink_logits, queries, keys_values, segments, out_weight):
     length, query_width = queries.shape
     width = out_weight.shape[1]
     half = length // 2
@@ -477,18 +494,20 @@
             jax.ShapeDtypeStruct(
                 (length // PAGE_LEN, PAGE_LEN, keys_values.shape[1]), jnp.bfloat16
             ),
+            jax.ShapeDtypeStruct((1,), jnp.int32),
         ],
-        in_specs=[smem] * 3 + [vmem()] * 4 + [anywhere()],
-        out_specs=[vmem()] * 3,
+        in_specs=[smem] * 4 + [vmem()] * 4 + [anywhere()],
+        out_specs=[vmem()] * 3 + [smem],
         scratch_shapes=[
             pltpu.VMEM((width, query_width), jnp.bfloat16),
             pltpu.VMEM((length, query_width), jnp.bfloat16),
             pltpu.SemaphoreType.DMA((len(tiles(width, 512)),)),
         ],
-        compiler_params=pltpu.CompilerParams(vmem_limit_bytes=24 * 2**20),
+        compiler_params=pltpu.CompilerParams(vmem_limit_bytes=VMEM_LIMIT),
         name="attention",
     )(
         side,
+        expert,
         page_table,
         sink_logits,
         queries,
@@ -507,37 +526,31 @@
     return pl.BlockSpec(memory_space=pl.ANY)
 
 
-def run_expert(expert, pieces, gate_weight, gate_bias, up_weight, up_bias, down_weight, slots):
+def run_expert(
+    expert, pieces, gate_rows, gate_bias, up_rows, up_bias, down_weight, sign, late_sign, block, limit
+):
     parts = len(pieces)
     piece, padded = pieces[0].shape
     hidden_units, width = down_weight.shape
-    total = parts * piece
-    step = 256
-    copies = parts + 2 * len(tiles(hidden_units, step)) + len(tiles(width, 2 * step))
+    slots = parts * piece // block * limit
     return pl.pallas_call(
-        functools.partial(expert_kernel, parts, step),
+        functools.partial(expert_kernel, parts, block, limit, 256),
         out_shape=[jax.ShapeDtypeStruct((piece, width), jnp.bfloat16)] * parts,
-        in_specs=[pl.BlockSpec(memory_space=pltpu.SMEM)]
-        + [anywhere()] * (parts + 3)
-        + [vmem()] * 2,
+        in_specs=[pl.BlockSpec(memory_space=pltpu.SMEM)] + [vmem()] * (parts + 5)
+        + [anywhere()] * 2,
         out_specs=[vmem()] * parts,
         scratch_shapes=[
-            pltpu.VMEM((total, padded), jnp.bfloat16),
             pltpu.VMEM((slots, width), jnp.bfloat16),
-            pltpu.VMEM((2 * hidden_units, width), jnp.bfloat16),
-            pltpu.VMEM(down_weight.shape, jnp.bfloat16),
             pltpu.VMEM((slots, hidden_units), jnp.bfloat16),
-            pltpu.VMEM((total, slots), jnp.bfloat16),
-            pltpu.SemaphoreType.DMA((copies,)),
         ],
-        compiler_params=pltpu.CompilerParams(vmem_limit_bytes=52 * 2**20),
+        compiler_params=pltpu.CompilerParams(vmem_limit_bytes=8 * 2**20),
         cost_estimate=pl.CostEstimate(
-            flops=2 * slots * width * (3 * hidden_units + 2 * total),
+            flops=6 * slots * width * hidden_units,
             bytes_accessed=6 * width * hidden_units,
             transcendentals=slots * hidden_units,
         ),
         name="expert",
-    )(expert, *pieces, gate_weight.T, up_weight.T, down_weight, gate_bias, up_bias)
+    )(expert, *pieces, gate_rows, up_rows, down_weight, gate_bias, up_bias, sign, late_sign)
 
 
 AXES = ("req", "tp")
@@ -564,14 +577,17 @@
     return lax.ppermute(array, AXES, pairs)
 
 
-def gather_rows(rows, n_req):
+def gather_rows(rows, n_req, sign, late_sign):
     outer = n_req // 4
     line = jnp.concatenate([rows] + [moved(rows, n_req, (k, 0, 0, 0)) for k in range(1, outer)])
     first = crossed(line, n_req, 0)
     second = crossed(line, n_req, 1)
-    both = crossed(first, n_req, 1)
+    sent, sign = lax.optimization_barrier((first, sign))
+    both = crossed(sent, n_req, 1)
     own = [line, first, second, both]
-    return own + [moved(piece, n_req, (0, 0, 1, 0)) for piece in own]
+    sent, late_sign = lax.optimization_barrier((both, late_sign))
+    pieces = own + [moved(piece, n_req, (0, 0, 1, 0)) for piece in (line, first, second, sent)]
+    return pieces, sign, late_sign
 
 
 def add_rows(left, right):
@@ -616,8 +632,9 @@
 ):
     tok_count, width = residual.shape
     side = lax.axis_index("tp")[None]
-    own, other, page_pool = run_attention(
-        side, page_table, sink_logits, queries, keys_values, segments, out_weight
+    expert = lax.axis_index("req")[None]
+    own, other, page_pool, expert = run_attention(
+        side, expert, page_table, sink_logits, queries, keys_values, segments, out_weight
     )
     got = moved(other, n_req, (0, 0, 0, 1))
     experts = down_bias.shape[0]
@@ -636,21 +653,25 @@
         residual,
         out_bias[None],
         norm_gain[None],
-        route_ids,
-        route_logits,
+        route_ids.T,
+        route_logits.T,
         down_bias,
     )
-    pieces = gather_rows(rows, n_req)
-    slots = 2 * n_req * slot_limit(tok_count, route_ids.shape[1], experts)
+    gate, up, sign = load([gate_weight[0].T, up_weight[0].T], 36 * 2**20)
+    down, late_sign = load([down_weight[0]], 2 * 2**20)
+    pieces, sign, late_sign = gather_rows(rows, n_req, sign, late_sign)
     sums = run_expert(
-        lax.axis_index("req")[None],
+        expert,
         pieces,
-        gate_weight[0],
+        gate,
         gate_bias,
-        up_weight[0],
+        up,
         up_bias,
-        down_weight[0],
-        slots,
+        down,
+        sign,
+        late_sign,
+        tok_count,
+        slot_limit(tok_count, route_ids.shape[1], experts),
     )
     mixed = base
     for part in scatter_rows(sums, n_req):

time: 112 us -> 96 us (0.86)
  local copies, waits for them, and re-layouts: 14.3 us -> 6.3 us
  waiting for transfers between devices: 43.6 us -> 37.5 us
  Pallas kernels: 31.5 us -> 30.2 us
    unnamed x53 -> x25, local copies, waits for them, and re-layouts: 13 us -> 5.04 us
    ppermute x6, waiting for transfers between devices: 26.5 us -> 19.4 us  [crossed(): return lax.ppermute(array, AXES, pairs)]
    pallas_call x1 -> x3, Pallas kernels: 20.9 us -> 18.5 us  [the longest x1 10.8 us: run_expert(): pl.pallas_call(functools.partial(expert_kernel, parts, block, limit, 256)...]
    pallas_call x1, Pallas kernels: 8.25 us -> 9.43 us  [run_attention(): pl.pallas_call(attention_kernel, out_shape=[jax.ShapeDtypeStruct((half, w...]
    ppermute x15, waiting for transfers between devices: 17.1 us -> 18.2 us  [moved(): return lax.ppermute(array, AXES, pairs)]
  transfers between devices with their start and end apart: 21 -> 21, of which waited for: 14 -> 13; matrix products, arithmetic and copies ran while one was open for 3% -> 3% of each run, Pallas kernels for 0% -> 8%
where the time goes in v3:
time: 96 us; the launch traced here: 95.7 us
  waiting for transfers between devices  37.5 us (39%)
  Pallas kernels  30.2 us (31%)
  starting transfers between devices  19.7 us (21%)
  local copies, waits for them, and re-layouts  6.3 us (7%)
  other arithmetic  1.21 us (1%)
    ppermute x6, waiting for transfers between devices, crossed(): return lax.ppermute(array, AXES, pairs)  19.4 us
    ppermute x15, waiting for transfers between devices, moved(): return lax.ppermute(array, AXES, pairs)  18.2 us
    ppermute x15, starting transfers between devices, moved(): return lax.ppermute(array, AXES, pairs)  12.8 us
    pallas_call x1, Pallas kernels, run_expert(): pl.pallas_call(functools.partial(expert_kernel, parts, block, limit, 256)...  10.8 us
    pallas_call x1, Pallas kernels, run_attention(): pl.pallas_call(attention_kernel, out_shape=[jax.ShapeDtypeStruct((half, w...  9.43 us
    pallas_call x2, Pallas kernels, load(): pl.pallas_call(functools.partial(load_kernel, parts), out_shape=[jax.Shap...  7.63 us
    ppermute x6, starting transfers between devices, crossed(): return lax.ppermute(array, AXES, pairs)  6.97 us
    unnamed x25, local copies, waits for them, and re-layouts  5.04 us
  transfers between devices with their start and end apart: 21, of which 13 were waited for; matrix products, arithmetic and copies ran while one was open for 3% of the time, Pallas kernels for 8%

profile of v3, /device:TPU:0, one launch (start us, length us, event | category | flops | bytes accessed | tf_op | source)
XLA Modules:
  0.0 95.7 jit_solution(8208011543393968767)
XLA Ops:
  0.7 9.4 %attention.1 = (f32[16,2880]{1,0:T(8,128)}, bf16[16,2880]{1,0:T(8,128)(2,1)}, bf16[2,16,512]{2,1,0:T(8,128)(2,1)}, s32[1]{0:T(128)}) custom-call(s32[1]{0:T(128)} %bitcast.side_ref, s32[1]{0:T(128)} %bitcast.1.expert_in_ref, s32[1,2]{1,0:T(1,128)} %pages_ref.1, f32[32]{0:T(128)} %sink_ref.1, bf16[32,2048]{1,0:T(8,128)(2,1)} %queries_ref.1, ...), custom_call_target="tpu_custom_call" | custom-call | tf_op jit(solution)/shard_map/attention/pallas_call | solution.py:489
  10.1 3.0 %collective-permute-start = (bf16[16,2880]{1,0:T(8,128)(2,1)}, bf16[16,2880]{1,0:T(8,128)(2,1)S(1)}, u32[]{:S(2)}, u32[]{:S(2)}) collective-permute-start(bf16[16,2880]{1,0:T(8,128)(2,1)} %get-tuple-element.26), channel_id=1, source_target_pairs={{0,1},{1,0},{2,3},{3,2},{4,5},{5,4},{6,7},{7,6},{8,9},{9,8},{10,11... | collective-permute-start | bytes 276488 | tf_op jit(solution)/shard_map/ppermute | solution.py:566
  13.1 0.6 broadcast_in_dim.22.out_bias_ref
  14.3 1.7 %collective-permute-done.got_ref = bf16[16,2880]{1,0:T(8,128)(2,1)S(1)} collective-permute-done((bf16[16,2880]{1,0:T(8,128)(2,1)}, bf16[16,2880]{1,0:T(8,128)(2,1)S(1)}, u32[]{:S(2)}, u32[]{:S(2)}) %collective-permute-start) | collective-permute-done | bytes 92192 | tf_op jit(solution)/shard_map/ppermute | solution.py:566
  16.0 0.6 copy-done.5
  16.7 2.3 %norm_rows.1 = (f32[16,2880]{1,0:T(8,128)}, bf16[16,2944]{1,0:T(8,128)(2,1)}) custom-call(f32[16,2880]{1,0:T(8,128)} %get-tuple-element.25.own_ref, bf16[16,2880]{1,0:T(8,128)(2,1)} %copy-done.5, bf16[16,2880]{1,0:T(8,128)(2,1)} %residual_ref.1, bf16[1,2880]{1,0:T(2,128)(2,1)} %broadcast_in_dim.22.out_bias_ref, bf16[1,2880]{1,0:T(2,128)(2,1)} %broadcast_in_dim.23.gain_ref, ...), custom_call_target="tpu_custom_call" | custom-call | tf_op jit(solution)/shard_map/norm_rows/pallas_call | solution.py:641
  18.9 4.0 %collective-permute-start.3 = (bf16[16,2944]{1,0:T(8,128)(2,1)}, bf16[16,2944]{1,0:T(8,128)(2,1)S(1)}, u32[]{:S(2)}, u32[]{:S(2)}) collective-permute-start(bf16[16,2944]{1,0:T(8,128)(2,1)} %get-tuple-element.29), channel_id=1, source_target_pairs={{0,24},{1,25},{2,26},{3,27},{4,28},{5,29},{6,30},{7,31},{8,16},{9,... | collective-permute-start | bytes 282632 | tf_op jit(solution)/shard_map/ppermute | solution.py:566
  23.5 0.9 constant_dynamic-update-slice_fusion.3
  24.4 3.7 %collective-permute-done.1 = bf16[16,2944]{1,0:T(8,128)(2,1)S(1)} collective-permute-done((bf16[16,2944]{1,0:T(8,128)(2,1)}, bf16[16,2944]{1,0:T(8,128)(2,1)S(1)}, u32[]{:S(2)}, u32[]{:S(2)}) %collective-permute-start.1) | collective-permute-done | bytes 94240 | tf_op jit(solution)/shard_map/ppermute | solution.py:566
  28.1 1.9 %collective-permute-done.2 = bf16[16,2944]{1,0:T(8,128)(2,1)S(1)} collective-permute-done((bf16[16,2944]{1,0:T(8,128)(2,1)}, bf16[16,2944]{1,0:T(8,128)(2,1)S(1)}, u32[]{:S(2)}, u32[]{:S(2)}) %collective-permute-start.2) | collective-permute-done | bytes 94240 | tf_op jit(solution)/shard_map/ppermute | solution.py:566
  30.1 1.6 %collective-permute-start.4 = (bf16[64,2944]{1,0:T(8,128)(2,1)S(1)}, bf16[64,2944]{1,0:T(8,128)(2,1)S(1)}, u32[]{:S(2)}, u32[]{:S(2)}) collective-permute-start(bf16[64,2944]{1,0:T(8,128)(2,1)S(1)} %constant_dynamic-update-slice_fusion.refs_0_), channel_id=1, source_target_pairs={{0,4},{1,5},{2,3},{3,2},{4,0},{5,1},{6,7},{7,6},{8,12},{9,13},{10,... | collective-permute-start | bytes 1130504 | tf_op jit(solution)/shard_map/ppermute | solution.py:577
  31.6 6.1 %load.2 = (bf16[1440,2880]{1,0:T(8,128)(2,1)S(1)}, bf16[1440,2880]{1,0:T(8,128)(2,1)S(1)}, bf16[16,128]{1,0:T(8,128)(2,1)S(1)}) custom-call(bf16[1440,2880]{1,0:T(8,128)(2,1)} %bitcast.17, bf16[1440,2880]{1,0:T(8,128)(2,1)} %bitcast.18), custom_call_target="tpu_custom_call" | custom-call | bytes 33177600 | tf_op jit(solution)/shard_map/load/pallas_call | solution.py:294
  37.8 1.6 %collective-permute-start.5 = (bf16[64,2944]{1,0:T(8,128)(2,1)S(1)}, bf16[64,2944]{1,0:T(8,128)(2,1)S(1)}, u32[]{:S(2)}, u32[]{:S(2)}) collective-permute-start(bf16[64,2944]{1,0:T(8,128)(2,1)S(1)} %constant_dynamic-update-slice_fusion.refs_0_), channel_id=1, source_target_pairs={{0,1},{1,0},{2,6},{3,7},{4,5},{5,4},{6,2},{7,3},{8,9},{9,8},{10,14... | collective-permute-start | bytes 1130504 | tf_op jit(solution)/shard_map/ppermute | solution.py:577
  39.9 1.5 %load.3 = (bf16[1440,2880]{1,0:T(8,128)(2,1)S(1)}, bf16[16,128]{1,0:T(8,128)(2,1)S(1)}) custom-call(bf16[1440,2880]{1,0:T(8,128)(2,1)S(1)} %bitcast.15), custom_call_target="tpu_custom_call" | custom-call | bytes 16588800 | tf_op jit(solution)/shard_map/load/pallas_call | solution.py:294
  42.0 3.4 %collective-permute-done.5.refs_2_ = bf16[64,2944]{1,0:T(8,128)(2,1)S(1)} collective-permute-done((bf16[64,2944]{1,0:T(8,128)(2,1)S(1)}, bf16[64,2944]{1,0:T(8,128)(2,1)S(1)}, u32[]{:S(2)}, u32[]{:S(2)}) %collective-permute-start.5) | collective-permute-done | bytes 376864 | tf_op jit(solution)/shard_map/ppermute | solution.py:577
  45.4 4.0 %collective-permute-done.6.refs_3_ = bf16[64,2944]{1,0:T(8,128)(2,1)S(1)} collective-permute-done((bf16[64,2944]{1,0:T(8,128)(2,1)S(1)}, bf16[64,2944]{1,0:T(8,128)(2,1)S(1)}, u32[]{:S(2)}, u32[]{:S(2)}) %collective-permute-start.6) | collective-permute-done | bytes 376864 | tf_op jit(solution)/shard_map/ppermute | solution.py:577
  49.5 1.7 %collective-permute-done.10.refs_7_ = bf16[64,2944]{1,0:T(8,128)(2,1)S(1)} collective-permute-done((bf16[64,2944]{1,0:T(8,128)(2,1)S(1)}, bf16[64,2944]{1,0:T(8,128)(2,1)S(1)}, u32[]{:S(2)}, u32[]{:S(2)}) %collective-permute-start.10) | collective-permute-done | bytes 376864 | tf_op jit(solution)/shard_map/ppermute | solution.py:566
  51.2 3.4 %copy-done.1 = bf16[1440,2880]{1,0:T(8,128)(2,1)S(1)} copy-done((bf16[1440,2880]{1,0:T(8,128)(2,1)S(1)}, bf16[1440,2880]{1,0:T(8,128)(2,1)}, u32[]{:S(2)}) %copy-start.1) | copy-done | bytes 8294424
  54.6 10.8 %expert.1 = (bf16[64,2880]{1,0:T(8,128)(2,1)S(1)}, bf16[64,2880]{1,0:T(8,128)(2,1)S(1)}, bf16[64,2880]{1,0:T(8,128)(2,1)S(1)}, bf16[64,2880]{1,0:T(8,128)(2,1)S(...) custom-call(s32[1]{0:T(128)} %get-tuple-element.28.expert_ref, ...), custom_call_target="tpu_custom_call" | custom-call | flops 6370099200 | bytes 24883200 | tf_op jit(solution)/shard_map/expert/pallas_call | solution.py:536
  66.5 0.7 collective-permute-done.15
  67.3 1.6 %collective-permute-start.16 = (bf16[64,2880]{1,0:T(8,128)(2,1)S(1)}, bf16[64,2880]{1,0:T(8,128)(2,1)S(1)}, u32[]{:S(2)}, u32[]{:S(2)}) collective-permute-start(bf16[64,2880]{1,0:T(8,128)(2,1)S(1)} %add_convert_fusion.2), channel_id=1, source_target_pairs={{0,1},{1,0},{2,6},{3,7},{4,5},{5,4},{6,2},{7,3},{8,9},{9,8},{10,14... | collective-permute-start | bytes 1105928 | tf_op jit(solution)/shard_map/ppermute | solution.py:577
  69.0 1.0 %collective-permute-start.13 = (bf16[64,2880]{1,0:T(8,128)(2,1)S(1)}, bf16[64,2880]{1,0:T(8,128)(2,1)S(1)}, u32[]{:S(2)}, u32[]{:S(2)}) collective-permute-start(bf16[64,2880]{1,0:T(8,128)(2,1)S(1)} %add_convert_fusion.5), channel_id=1, source_target_pairs={{0,1},{1,0},{2,6},{3,7},{4,5},{5,4},{6,2},{7,3},{8,9},{9,8},{10,14... | collective-permute-start | bytes 1105928 | tf_op jit(solution)/shard_map/ppermute | solution.py:577
  70.0 5.0 %collective-permute-done.16 = bf16[64,2880]{1,0:T(8,128)(2,1)S(1)} collective-permute-done((bf16[64,2880]{1,0:T(8,128)(2,1)S(1)}, bf16[64,2880]{1,0:T(8,128)(2,1)S(1)}, u32[]{:S(2)}, u32[]{:S(2)}) %collective-permute-start.16) | collective-permute-done | bytes 368672 | tf_op jit(solution)/shard_map/ppermute | solution.py:577
  75.1 0.8 collective-permute-start.17
  75.9 5.0 %collective-permute-done.13 = bf16[64,2880]{1,0:T(8,128)(2,1)S(1)} collective-permute-done((bf16[64,2880]{1,0:T(8,128)(2,1)S(1)}, bf16[64,2880]{1,0:T(8,128)(2,1)S(1)}, u32[]{:S(2)}, u32[]{:S(2)}) %collective-permute-start.13) | collective-permute-done | bytes 368672 | tf_op jit(solution)/shard_map/ppermute | solution.py:577
  80.9 1.9 %collective-permute-done.17 = bf16[64,2880]{1,0:T(8,128)(2,1)S(1)} collective-permute-done((bf16[64,2880]{1,0:T(8,128)(2,1)S(1)}, bf16[64,2880]{1,0:T(8,128)(2,1)S(1)}, u32[]{:S(2)}, u32[]{:S(2)}) %collective-permute-start.17) | collective-permute-done | bytes 368672 | tf_op jit(solution)/shard_map/ppermute | solution.py:577
  83.5 1.9 %collective-permute-start.20 = (bf16[16,2880]{1,0:T(8,128)(2,1)S(1)}, bf16[16,2880]{1,0:T(8,128)(2,1)S(1)}, u32[]{:S(2)}, u32[]{:S(2)}) collective-permute-start(bf16[16,2880]{1,0:T(8,128)(2,1)S(1)} %get-tuple-element.49), channel_id=1, source_target_pairs={{0,24},{1,25},{2,26},{3,27},{4,28},{5,29},{6,30},{7,31},{8,16},{9,... | collective-permute-start | bytes 276488 | tf_op jit(solution)/shard_map/ppermute | solution.py:566
  85.4 1.1 %collective-permute-start.19 = (bf16[16,2880]{1,0:T(8,128)(2,1)S(1)}, bf16[16,2880]{1,0:T(8,128)(2,1)S(1)}, u32[]{:S(2)}, u32[]{:S(2)}) collective-permute-start(bf16[16,2880]{1,0:T(8,128)(2,1)S(1)} %get-tuple-element.50), channel_id=1, source_target_pairs={{0,16},{1,17},{2,18},{3,19},{4,20},{5,21},{6,22},{7,23},{8,24},{9,... | collective-permute-start | bytes 276488 | tf_op jit(solution)/shard_map/ppermute | solution.py:566
  86.6 1.2 %collective-permute-done.18 = bf16[16,2880]{1,0:T(8,128)(2,1)S(1)} collective-permute-done((bf16[16,2880]{1,0:T(8,128)(2,1)S(1)}, bf16[16,2880]{1,0:T(8,128)(2,1)S(1)}, u32[]{:S(2)}, u32[]{:S(2)}) %collective-permute-start.18) | collective-permute-done | bytes 92192 | tf_op jit(solution)/shard_map/ppermute | solution.py:566
  87.8 3.3 %collective-permute-done.20 = bf16[16,2880]{1,0:T(8,128)(2,1)S(1)} collective-permute-done((bf16[16,2880]{1,0:T(8,128)(2,1)S(1)}, bf16[16,2880]{1,0:T(8,128)(2,1)S(1)}, u32[]{:S(2)}, u32[]{:S(2)}) %collective-permute-start.20) | collective-permute-done | bytes 92192 | tf_op jit(solution)/shard_map/ppermute | solution.py:566
  91.1 3.9 %collective-permute-done.19 = bf16[16,2880]{1,0:T(8,128)(2,1)S(1)} collective-permute-done((bf16[16,2880]{1,0:T(8,128)(2,1)S(1)}, bf16[16,2880]{1,0:T(8,128)(2,1)S(1)}, u32[]{:S(2)}, u32[]{:S(2)}) %collective-permute-start.19) | collective-permute-done | bytes 92192 | tf_op jit(solution)/shard_map/ppermute | solution.py:566
  95.0 0.7 add_convert_fusion.7
  (50 shorter events, 4.5 us)
Async XLA Ops:
  0.6 12.5 %copy-start.6 = (bf16[2880]{0:T(1024)(128)(2,1)S(1)}, bf16[2880]{0:T(1024)(128)(2,1)}, u32[]{:S(2)}) copy-start(bf16[2880]{0:T(1024)(128)(2,1)} %param.23) | copy-start | bytes 17284
  0.6 13.1 %copy-start.7 = (bf16[2880]{0:T(1024)(128)(2,1)S(1)}, bf16[2880]{0:T(1024)(128)(2,1)}, u32[]{:S(2)}) copy-start(bf16[2880]{0:T(1024)(128)(2,1)} %param.25) | copy-start | bytes 17284
  10.1 6.0 %collective-permute-start = (bf16[16,2880]{1,0:T(8,128)(2,1)}, bf16[16,2880]{1,0:T(8,128)(2,1)S(1)}, u32[]{:S(2)}, u32[]{:S(2)}) collective-permute-start(bf16[16,2880]{1,0:T(8,128)(2,1)} %get-tuple-element.26), channel_id=1, source_target_pairs={{0,1},{1,0},{2,3},{3,2},{4,5},{5,4},{6,7},{7,6},{8,9},{9,8},{10,11... | collective-permute-start | bytes 276488 | tf_op jit(solution)/shard_map/ppermute | solution.py:566
  16.0 0.6 copy-start.5
  18.9 11.1 %collective-permute-start.3 = (bf16[16,2944]{1,0:T(8,128)(2,1)}, bf16[16,2944]{1,0:T(8,128)(2,1)S(1)}, u32[]{:S(2)}, u32[]{:S(2)}) collective-permute-start(bf16[16,2944]{1,0:T(8,128)(2,1)} %get-tuple-element.29), channel_id=1, source_target_pairs={{0,24},{1,25},{2,26},{3,27},{4,28},{5,29},{6,30},{7,31},{8,16},{9,... | collective-permute-start | bytes 282632 | tf_op jit(solution)/shard_map/ppermute | solution.py:566
  22.9 7.1 %collective-permute-start.2 = (bf16[16,2944]{1,0:T(8,128)(2,1)}, bf16[16,2944]{1,0:T(8,128)(2,1)S(1)}, u32[]{:S(2)}, u32[]{:S(2)}) collective-permute-start(bf16[16,2944]{1,0:T(8,128)(2,1)} %get-tuple-element.29), channel_id=1, source_target_pairs={{0,16},{1,17},{2,18},{3,19},{4,20},{5,21},{6,22},{7,23},{8,24},{9,... | collective-permute-start | bytes 282632 | tf_op jit(solution)/shard_map/ppermute | solution.py:566
  22.9 5.2 %collective-permute-start.1 = (bf16[16,2944]{1,0:T(8,128)(2,1)}, bf16[16,2944]{1,0:T(8,128)(2,1)S(1)}, u32[]{:S(2)}, u32[]{:S(2)}) collective-permute-start(bf16[16,2944]{1,0:T(8,128)(2,1)} %get-tuple-element.29), channel_id=1, source_target_pairs={{0,8},{1,9},{2,10},{3,11},{4,12},{5,13},{6,14},{7,15},{8,0},{9,1},... | collective-permute-start | bytes 282632 | tf_op jit(solution)/shard_map/ppermute | solution.py:566
  30.0 9.8 %slice-start = ((s8[8478720]{0:T(1024)(128)(4,1)}), s8[4194304]{0:T(1024)(128)(4,1)S(1)}, s32[]{:S(2)}) async-start(s8[8478720]{0:T(1024)(128)(4,1)} %bitcast.13), calls=%async_computation | async-start | bytes 8388608
  30.1 9.3 %collective-permute-start.4 = (bf16[64,2944]{1,0:T(8,128)(2,1)S(1)}, bf16[64,2944]{1,0:T(8,128)(2,1)S(1)}, u32[]{:S(2)}, u32[]{:S(2)}) collective-permute-start(bf16[64,2944]{1,0:T(8,128)(2,1)S(1)} %constant_dynamic-update-slice_fusion.refs_0_), channel_id=1, source_target_pairs={{0,4},{1,5},{2,3},{3,2},{4,0},{5,1},{6,7},{7,6},{8,12},{9,13},{10,... | collective-permute-start | bytes 1130504 | tf_op jit(solution)/shard_map/ppermute | solution.py:577
  31.6 8.2 %slice-start.1 = ((s8[8478720]{0:T(1024)(128)(4,1)}), s8[4194304]{0:T(1024)(128)(4,1)S(1)}, s32[]{:S(2)}) async-start(s8[8478720]{0:T(1024)(128)(4,1)} %bitcast.13), calls=%async_computation.1 | async-start | bytes 8388608
  31.6 8.2 %slice-start.2 = ((s8[8478720]{0:T(1024)(128)(4,1)}), s8[90112]{0:T(1024)(128)(4,1)S(1)}, s32[]{:S(2)}) async-start(s8[8478720]{0:T(1024)(128)(4,1)} %bitcast.13), calls=%async_computation.2 | async-start | bytes 180224
  37.7 3.7 %copy-start = (bf16[1440,2880]{1,0:T(8,128)(2,1)}, bf16[1440,2880]{1,0:T(8,128)(2,1)S(1)}, u32[]{:S(2)}) copy-start(bf16[1440,2880]{1,0:T(8,128)(2,1)S(1)} %get-tuple-element.34.refs_8_) | copy-start | bytes 24883204
  37.7 13.4 %copy-start.2 = (bf16[1,1440]{1,0:T(2,128)(2,1)S(1)}, bf16[1,1440]{1,0:T(2,128)(2,1)}, u32[]{:S(2)}) copy-start(bf16[1,1440]{1,0:T(2,128)(2,1)} %refs_11_.1) | copy-start | bytes 8644
  37.8 13.4 %copy-start.3 = (bf16[1,1440]{1,0:T(2,128)(2,1)S(1)}, bf16[1,1440]{1,0:T(2,128)(2,1)}, u32[]{:S(2)}) copy-start(bf16[1,1440]{1,0:T(2,128)(2,1)} %refs_12_.1) | copy-start | bytes 8644
  37.8 7.7 %collective-permute-start.5 = (bf16[64,2944]{1,0:T(8,128)(2,1)S(1)}, bf16[64,2944]{1,0:T(8,128)(2,1)S(1)}, u32[]{:S(2)}, u32[]{:S(2)}) collective-permute-start(bf16[64,2944]{1,0:T(8,128)(2,1)S(1)} %constant_dynamic-update-slice_fusion.refs_0_), channel_id=1, source_target_pairs={{0,1},{1,0},{2,6},{3,7},{4,5},{5,4},{6,2},{7,3},{8,9},{9,8},{10,14... | collective-permute-start | bytes 1130504 | tf_op jit(solution)/shard_map/ppermute | solution.py:577
  39.4 10.1 %collective-permute-start.6 = (bf16[64,2944]{1,0:T(8,128)(2,1)S(1)}, bf16[64,2944]{1,0:T(8,128)(2,1)S(1)}, u32[]{:S(2)}, u32[]{:S(2)}) collective-permute-start(bf16[64,2944]{1,0:T(8,128)(2,1)S(1)} %collective-permute-done.4.refs_1_), channel_id=1, source_target_pairs={{0,1},{1,0},{2,6},{3,7},{4,5},{5,4},{6,2},{7,3},{8,9},{9,8},{10,14... | collective-permute-start | bytes 1130504 | tf_op jit(solution)/shard_map/ppermute | solution.py:577
  41.4 8.0 %collective-permute-start.7 = (bf16[64,2944]{1,0:T(8,128)(2,1)S(1)}, bf16[64,2944]{1,0:T(8,128)(2,1)S(1)}, u32[]{:S(2)}, u32[]{:S(2)}) collective-permute-start(bf16[64,2944]{1,0:T(8,128)(2,1)S(1)} %constant_dynamic-update-slice_fusion.refs_0_), channel_id=1, source_target_pairs={{0,2},{1,3},{2,0},{3,1},{4,6},{5,7},{6,4},{7,5},{8,10},{9,11},{10,... | collective-permute-start | bytes 1130504 | tf_op jit(solution)/shard_map/ppermute | solution.py:566
  41.5 8.0 %collective-permute-start.8 = (bf16[64,2944]{1,0:T(8,128)(2,1)S(1)}, bf16[64,2944]{1,0:T(8,128)(2,1)S(1)}, u32[]{:S(2)}, u32[]{:S(2)}) collective-permute-start(bf16[64,2944]{1,0:T(8,128)(2,1)S(1)} %collective-permute-done.4.refs_1_), channel_id=1, source_target_pairs={{0,2},{1,3},{2,0},{3,1},{4,6},{5,7},{6,4},{7,5},{8,10},{9,11},{10,... | collective-permute-start | bytes 1130504 | tf_op jit(solution)/shard_map/ppermute | solution.py:566
  45.4 4.0 %collective-permute-start.9 = (bf16[64,2944]{1,0:T(8,128)(2,1)S(1)}, bf16[64,2944]{1,0:T(8,128)(2,1)S(1)}, u32[]{:S(2)}, u32[]{:S(2)}) collective-permute-start(bf16[64,2944]{1,0:T(8,128)(2,1)S(1)} %collective-permute-done.5.refs_2_), channel_id=1, source_target_pairs={{0,2},{1,3},{2,0},{3,1},{4,6},{5,7},{6,4},{7,5},{8,10},{9,11},{10,... | collective-permute-start | bytes 1130504 | tf_op jit(solution)/shard_map/ppermute | solution.py:566
  49.5 1.7 %collective-permute-start.10 = (bf16[64,2944]{1,0:T(8,128)(2,1)S(1)}, bf16[64,2944]{1,0:T(8,128)(2,1)S(1)}, u32[]{:S(2)}, u32[]{:S(2)}) collective-permute-start(bf16[64,2944]{1,0:T(8,128)(2,1)S(1)} %collective-permute-done.6.refs_3_), channel_id=1, source_target_pairs={{0,2},{1,3},{2,0},{3,1},{4,6},{5,7},{6,4},{7,5},{8,10},{9,11},{10,... | collective-permute-start | bytes 1130504 | tf_op jit(solution)/shard_map/ppermute | solution.py:566
  51.2 3.4 %copy-start.1 = (bf16[1440,2880]{1,0:T(8,128)(2,1)S(1)}, bf16[1440,2880]{1,0:T(8,128)(2,1)}, u32[]{:S(2)}) copy-start(bf16[1440,2880]{1,0:T(8,128)(2,1)} %copy-done) | copy-start | bytes 24883204
  54.6 40.4 %copy-start.4 = (f32[16,2880]{1,0:T(8,128)S(1)}, f32[16,2880]{1,0:T(8,128)}, u32[]{:S(2)}) copy-start(f32[16,2880]{1,0:T(8,128)} %get-tuple-element.27) | copy-start | bytes 552964
  65.4 1.8 %collective-permute-start.15 = (bf16[64,2880]{1,0:T(8,128)(2,1)S(1)}, bf16[64,2880]{1,0:T(8,128)(2,1)S(1)}, u32[]{:S(2)}, u32[]{:S(2)}) collective-permute-start(bf16[64,2880]{1,0:T(8,128)(2,1)S(1)} %get-tuple-element.46), channel_id=1, source_target_pairs={{0,2},{1,3},{2,0},{3,1},{4,6},{5,7},{6,4},{7,5},{8,10},{9,11},{10,... | collective-permute-start | bytes 1105928 | tf_op jit(solution)/shard_map/ppermute | solution.py:566
  65.6 10.2 %collective-permute-start.11 = (bf16[64,2880]{1,0:T(8,128)(2,1)S(1)}, bf16[64,2880]{1,0:T(8,128)(2,1)S(1)}, u32[]{:S(2)}, u32[]{:S(2)}) collective-permute-start(bf16[64,2880]{1,0:T(8,128)(2,1)S(1)} %get-tuple-element.40), channel_id=1, source_target_pairs={{0,2},{1,3},{2,0},{3,1},{4,6},{5,7},{6,4},{7,5},{8,10},{9,11},{10,... | collective-permute-start | bytes 1105928 | tf_op jit(solution)/shard_map/ppermute | solution.py:566
  66.0 2.9 %collective-permute-start.12 = (bf16[64,2880]{1,0:T(8,128)(2,1)S(1)}, bf16[64,2880]{1,0:T(8,128)(2,1)S(1)}, u32[]{:S(2)}, u32[]{:S(2)}) collective-permute-start(bf16[64,2880]{1,0:T(8,128)(2,1)S(1)} %get-tuple-element.42), channel_id=1, source_target_pairs={{0,2},{1,3},{2,0},{3,1},{4,6},{5,7},{6,4},{7,5},{8,10},{9,11},{10,... | collective-permute-start | bytes 1105928 | tf_op jit(solution)/shard_map/ppermute | solution.py:566
  66.2 3.8 %collective-permute-start.14 = (bf16[64,2880]{1,0:T(8,128)(2,1)S(1)}, bf16[64,2880]{1,0:T(8,128)(2,1)S(1)}, u32[]{:S(2)}, u32[]{:S(2)}) collective-permute-start(bf16[64,2880]{1,0:T(8,128)(2,1)S(1)} %get-tuple-element.44), channel_id=1, source_target_pairs={{0,2},{1,3},{2,0},{3,1},{4,6},{5,7},{6,4},{7,5},{8,10},{9,11},{10,... | collective-permute-start | bytes 1105928 | tf_op jit(solution)/shard_map/ppermute | solution.py:566
  67.3 7.7 %collective-permute-start.16 = (bf16[64,2880]{1,0:T(8,128)(2,1)S(1)}, bf16[64,2880]{1,0:T(8,128)(2,1)S(1)}, u32[]{:S(2)}, u32[]{:S(2)}) collective-permute-start(bf16[64,2880]{1,0:T(8,128)(2,1)S(1)} %add_convert_fusion.2), channel_id=1, source_target_pairs={{0,1},{1,0},{2,6},{3,7},{4,5},{5,4},{6,2},{7,3},{8,9},{9,8},{10,14... | collective-permute-start | bytes 1105928 | tf_op jit(solution)/shard_map/ppermute | solution.py:577
  69.0 11.9 %collective-permute-start.13 = (bf16[64,2880]{1,0:T(8,128)(2,1)S(1)}, bf16[64,2880]{1,0:T(8,128)(2,1)S(1)}, u32[]{:S(2)}, u32[]{:S(2)}) collective-permute-start(bf16[64,2880]{1,0:T(8,128)(2,1)S(1)} %add_convert_fusion.5), channel_id=1, source_target_pairs={{0,1},{1,0},{2,6},{3,7},{4,5},{5,4},{6,2},{7,3},{8,9},{9,8},{10,14... | collective-permute-start | bytes 1105928 | tf_op jit(solution)/shard_map/ppermute | solution.py:577
  75.1 7.7 %collective-permute-start.17 = (bf16[64,2880]{1,0:T(8,128)(2,1)S(1)}, bf16[64,2880]{1,0:T(8,128)(2,1)S(1)}, u32[]{:S(2)}, u32[]{:S(2)}) collective-permute-start(bf16[64,2880]{1,0:T(8,128)(2,1)S(1)} %add_convert_fusion.1), channel_id=1, source_target_pairs={{0,4},{1,5},{2,3},{3,2},{4,0},{5,1},{6,7},{7,6},{8,12},{9,13},{10,... | collective-permute-start | bytes 1105928 | tf_op jit(solution)/shard_map/ppermute | solution.py:577
  83.0 4.8 %collective-permute-start.18 = (bf16[16,2880]{1,0:T(8,128)(2,1)S(1)}, bf16[16,2880]{1,0:T(8,128)(2,1)S(1)}, u32[]{:S(2)}, u32[]{:S(2)}) collective-permute-start(bf16[16,2880]{1,0:T(8,128)(2,1)S(1)} %get-tuple-element.48), channel_id=1, source_target_pairs={{0,8},{1,9},{2,10},{3,11},{4,12},{5,13},{6,14},{7,15},{8,0},{9,1},... | collective-permute-start | bytes 276488 | tf_op jit(solution)/shard_map/ppermute | solution.py:566
  83.5 7.5 %collective-permute-start.20 = (bf16[16,2880]{1,0:T(8,128)(2,1)S(1)}, bf16[16,2880]{1,0:T(8,128)(2,1)S(1)}, u32[]{:S(2)}, u32[]{:S(2)}) collective-permute-start(bf16[16,2880]{1,0:T(8,128)(2,1)S(1)} %get-tuple-element.49), channel_id=1, source_target_pairs={{0,24},{1,25},{2,26},{3,27},{4,28},{5,29},{6,30},{7,31},{8,16},{9,... | collective-permute-start | bytes 276488 | tf_op jit(solution)/shard_map/ppermute | solution.py:566
  85.4 9.6 %collective-permute-start.19 = (bf16[16,2880]{1,0:T(8,128)(2,1)S(1)}, bf16[16,2880]{1,0:T(8,128)(2,1)S(1)}, u32[]{:S(2)}, u32[]{:S(2)}) collective-permute-start(bf16[16,2880]{1,0:T(8,128)(2,1)S(1)} %get-tuple-element.50), channel_id=1, source_target_pairs={{0,16},{1,17},{2,18},{3,19},{4,20},{5,21},{6,22},{7,23},{8,24},{9,... | collective-permute-start | bytes 276488 | tf_op jit(solution)/shard_map/ppermute | solution.py:566

commit v4 on v3

--- a/solution.py
+++ b/solution.py
@@ -11,6 +11,7 @@
 HEAD = 64
 PAGE_LEN = 16
 LANES = 128
+DOWN_STEP = 512
 VMEM_LIMIT = 60 * 2**20
 LOAD_ROWS = 480
 
@@ -272,44 +273,40 @@
     )
 
 
-def load_kernel(parts, *refs):
-    sources, targets, sign, sems = refs[:parts], refs[parts : 2 * parts], refs[-2], refs[-1]
+def load_kernel(source, target, sign, sems):
     copies = []
-    for source, target in zip(sources, targets):
-        for start, size in tiles(source.shape[0], LOAD_ROWS):
-            here = pl.ds(start, size)
-            copies.append(
-                pltpu.make_async_copy(source.at[here], target.at[here], sems.at[len(copies)])
-            )
+    for i, (start, size) in enumerate(tiles(source.shape[0], LOAD_ROWS)):
+        here = pl.ds(start, size)
+        copies.append(pltpu.make_async_copy(source.at[here], target.at[here], sems.at[i]))
     for copy in copies:
         copy.start()
     for copy in copies:
         copy.wait()
-    sign[...] = targets[0][: sign.shape[0], : sign.shape[1]]
-
-
-def load(weights, reserve):
-    parts = len(weights)
-    copies = sum(len(tiles(weight.shape[0], LOAD_ROWS)) for weight in weights)
+    sign[...] = target[: sign.shape[0], : sign.shape[1]]
+
+
+def load(weight, reserve):
     return pl.pallas_call(
-        functools.partial(load_kernel, parts),
-        out_shape=[jax.ShapeDtypeStruct(weight.shape, weight.dtype) for weight in weights]
-        + [jax.ShapeDtypeStruct((16, LANES), weights[0].dtype)],
-        in_specs=[anywhere()] * parts,
-        out_specs=[vmem()] * (parts + 1),
-        scratch_shapes=[pltpu.SemaphoreType.DMA((copies,))],
+        load_kernel,
+        out_shape=[
+            jax.ShapeDtypeStruct(weight.shape, weight.dtype),
+            jax.ShapeDtypeStruct((16, LANES), weight.dtype),
+        ],
+        in_specs=[anywhere()],
+        out_specs=[vmem()] * 2,
+        scratch_shapes=[pltpu.SemaphoreType.DMA((len(tiles(weight.shape[0], LOAD_ROWS)),))],
         compiler_params=pltpu.CompilerParams(vmem_limit_bytes=reserve),
         cost_estimate=pl.CostEstimate(
-            flops=0, bytes_accessed=4 * sum(w.size for w in weights), transcendentals=0
+            flops=0, bytes_accessed=4 * weight.size, transcendentals=0
         ),
         name="load",
-    )(*weights)
+    )(weight)
 
 
 def expert_kernel(parts, block, limit, step, expert_ref, *refs):
     pieces, refs = refs[:parts], refs[parts:]
     gate_w, up_w, down_w, gate_bias_ref, up_bias_ref = refs[:5]
-    outs, (picked, active) = refs[7 : 7 + parts], refs[7 + parts :]
+    outs, (picked, active) = refs[8 : 8 + parts], refs[8 + parts :]
     piece, padded = pieces[0].shape
     total = parts * piece
     units, width = down_w.shape
@@ -356,17 +353,15 @@
             ).astype(jnp.bfloat16)
     slot_share = jnp.concatenate(shares, axis=0)
 
-    for start, size in tiles(units, step):
+    def activate(start, size, gate, up):
         here = slice(start, start + size)
-        gate = by_rows(gate_w[here], picked[...])
-        up = by_rows(up_w[here], picked[...])
         gate = jnp.minimum(gate + gate_bias[here, 0:1], swiglu_limit)
         up = jnp.clip(up + up_bias[here, 0:1], -swiglu_limit, swiglu_limit)
         value = gate * (1.0 / (1.0 + jnp.exp(-glu_alpha * gate))) * (up + 1.0)
         active[:, here] = value.T.astype(jnp.bfloat16)
-    for start, size in tiles(width, 2 * step):
+
+    def give(start, size, value):
         cols = slice(start, start + size)
-        value = jnp.dot(active[...], down_w[:, cols], preferred_element_type=jnp.float32)
         scaled = (value * slot_share).astype(jnp.bfloat16)
         for g, spread in enumerate(spreads):
             sums = jnp.dot(
@@ -376,6 +371,24 @@
             ).astype(jnp.bfloat16)
             outs[2 * g][:, cols] = sums[:piece]
             outs[2 * g + 1][:, cols] = sums[piece:]
+
+    last = None
+    for start, size in tiles(units, step):
+        here = slice(start, start + size)
+        gate = by_rows(gate_w[here], picked[...])
+        up = by_rows(up_w[here], picked[...])
+        if last is not None:
+            activate(*last)
+        last = (start, size, gate, up)
+    activate(*last)
+    last = None
+    for start, size in tiles(width, DOWN_STEP):
+        cols = slice(start, start + size)
+        value = jnp.dot(active[...], down_w[:, cols], preferred_element_type=jnp.float32)
+        if last is not None:
+            give(*last)
+        last = (start, size, value)
+    give(*last)
 
 
 def attention_kernel(
@@ -527,17 +540,17 @@
 
 
 def run_expert(
-    expert, pieces, gate_rows, gate_bias, up_rows, up_bias, down_weight, sign, late_sign, block, limit
+    expert, pieces, gate_rows, gate_bias, up_rows, up_bias, down_weight, signs, block, limit
 ):
     parts = len(pieces)
     piece, padded = pieces[0].shape
     hidden_units, width = down_weight.shape
     slots = parts * piece // block * limit
     return pl.pallas_call(
-        functools.partial(expert_kernel, parts, block, limit, 256),
+        functools.partial(expert_kernel, parts, block, limit, 512),
         out_shape=[jax.ShapeDtypeStruct((piece, width), jnp.bfloat16)] * parts,
         in_specs=[pl.BlockSpec(memory_space=pltpu.SMEM)] + [vmem()] * (parts + 5)
-        + [anywhere()] * 2,
+        + [anywhere()] * 3,
         out_specs=[vmem()] * parts,
         scratch_shapes=[
             pltpu.VMEM((slots, width), jnp.bfloat16),
@@ -550,7 +563,7 @@
             transcendentals=slots * hidden_units,
         ),
         name="expert",
-    )(expert, *pieces, gate_rows, up_rows, down_weight, gate_bias, up_bias, sign, late_sign)
+    )(expert, *pieces, gate_rows, up_rows, down_weight, gate_bias, up_bias, *signs)
 
 
 AXES = ("req", "tp")
@@ -577,17 +590,19 @@
     return lax.ppermute(array, AXES, pairs)
 
 
-def gather_rows(rows, n_req, sign, late_sign):
+def gather_rows(rows, n_req, signs):
+    signs = list(signs)
     outer = n_req // 4
-    line = jnp.concatenate([rows] + [moved(rows, n_req, (k, 0, 0, 0)) for k in range(1, outer)])
+    others = [moved(rows, n_req, (k, 0, 0, 0)) for k in range(1, outer)]
+    line = jnp.concatenate([rows] + others)
     first = crossed(line, n_req, 0)
     second = crossed(line, n_req, 1)
-    sent, sign = lax.optimization_barrier((first, sign))
+    sent, signs[0], signs[1] = lax.optimization_barrier((first, signs[0], signs[1]))
     both = crossed(sent, n_req, 1)
     own = [line, first, second, both]
-    sent, late_sign = lax.optimization_barrier((both, late_sign))
+    sent, signs[2] = lax.optimization_barrier((both, signs[2]))
     pieces = own + [moved(piece, n_req, (0, 0, 1, 0)) for piece in (line, first, second, sent)]
-    return pieces, sign, late_sign
+    return pieces, signs
 
 
 def add_rows(left, right):
@@ -646,6 +661,7 @@
         ],
         in_specs=[vmem()] * 8,
         out_specs=[vmem()] * 2,
+        compiler_params=pltpu.CompilerParams(vmem_limit_bytes=4 * 2**20),
         name="norm_rows",
     )(
         own,
@@ -657,9 +673,11 @@
         route_logits.T,
         down_bias,
     )
-    gate, up, sign = load([gate_weight[0].T, up_weight[0].T], 36 * 2**20)
-    down, late_sign = load([down_weight[0]], 2 * 2**20)
-    pieces, sign, late_sign = gather_rows(rows, n_req, sign, late_sign)
+    signs = [None] * 3
+    gate, signs[0] = load(gate_weight[0].T, 40 * 2**20)
+    up, signs[1] = load(up_weight[0].T, 2 * 2**20)
+    down, signs[2] = load(down_weight[0], 2 * 2**20)
+    pieces, signs = gather_rows(rows, n_req, signs)
     sums = run_expert(
         expert,
         pieces,
@@ -668,8 +686,7 @@
         up,
         up_bias,
         down,
-        sign,
-        late_sign,
+        signs,
         tok_count,
         slot_limit(tok_count, route_ids.shape[1], experts),
     )

time: 96 us -> 92.2 us (0.960)
  Pallas kernels: 30.2 us -> 26 us
  local copies, waits for them, and re-layouts: 6.3 us -> 7.85 us
  waiting for transfers between devices: 37.5 us -> 36.4 us
    ppermute x6, waiting for transfers between devices: 19.4 us -> 16.3 us  [crossed(): return lax.ppermute(array, AXES, pairs)]
    unnamed x25, local copies, waits for them, and re-layouts: 5.04 us -> 7.79 us
    pallas_call x3 -> x4, Pallas kernels: 18.5 us -> 16 us  [the longest x1 9.81 us: run_expert(): pl.pallas_call(functools.partial(expert_kernel, parts, block, limit, 512)...]
    ppermute x15, waiting for transfers between devices: 18.2 us -> 20 us  [moved(): return lax.ppermute(array, AXES, pairs)]
    pallas_call x1, Pallas kernels: 2.25 us -> 0.42 us  [gathered_body(): pl.pallas_call(mid_kernel, out_shape=[jax.ShapeDtypeStruct((tok_count, wi...]
  transfers between devices with their start and end apart: 21 -> 21, of which waited for: 13 -> 13; matrix products, arithmetic and copies ran while one was open for 3% -> 0% of each run, Pallas kernels for 8% -> 7%
where the time goes in v4:
time: 92.2 us; the launch traced here: 91.9 us
  waiting for transfers between devices  36.4 us (39%)
  Pallas kernels  26 us (28%)
  starting transfers between devices  19.7 us (21%)
  local copies, waits for them, and re-layouts  7.85 us (9%)
  other arithmetic  1.21 us (1%)
    ppermute x15, waiting for transfers between devices, moved(): return lax.ppermute(array, AXES, pairs)  20 us
    ppermute x6, waiting for transfers between devices, crossed(): return lax.ppermute(array, AXES, pairs)  16.3 us
    ppermute x15, starting transfers between devices, moved(): return lax.ppermute(array, AXES, pairs)  12.9 us
    pallas_call x1, Pallas kernels, run_expert(): pl.pallas_call(functools.partial(expert_kernel, parts, block, limit, 512)...  9.81 us
    pallas_call x1, Pallas kernels, run_attention(): pl.pallas_call(attention_kernel, out_shape=[jax.ShapeDtypeStruct((half, w...  9.51 us
    unnamed x25, local copies, waits for them, and re-layouts  7.79 us
    ppermute x6, starting transfers between devices, crossed(): return lax.ppermute(array, AXES, pairs)  6.81 us
    pallas_call x3, Pallas kernels, load(): pl.pallas_call(load_kernel, out_shape=[jax.ShapeDtypeStruct(weight.shape,...  6.22 us
  transfers between devices with their start and end apart: 21, of which 13 were waited for; matrix products, arithmetic and copies ran while one was open for 0% of the time, Pallas kernels for 7%

profile of v4, /device:TPU:0, one launch (start us, length us, event | category | flops | bytes accessed | tf_op | source)
XLA Modules:
  0.0 91.9 jit_solution(2602275740937024588)
XLA Ops:
  0.7 9.5 %attention.1 = (f32[16,2880]{1,0:T(8,128)}, bf16[16,2880]{1,0:T(8,128)(2,1)}, bf16[2,16,512]{2,1,0:T(8,128)(2,1)}, s32[1]{0:T(128)}) custom-call(s32[1]{0:T(128)} %bitcast.side_ref, s32[1]{0:T(128)} %bitcast.1.expert_in_ref, s32[1,2]{1,0:T(1,128)} %pages_ref.1, f32[32]{0:T(128)} %sink_ref.1, bf16[32,2048]{1,0:T(8,128)(2,1)} %queries_ref.1, ...), custom_call_target="tpu_custom_call" | custom-call | tf_op jit(solution)/shard_map/attention/pallas_call | solution.py:502
  10.2 3.0 %collective-permute-start = (bf16[16,2880]{1,0:T(8,128)(2,1)}, bf16[16,2880]{1,0:T(8,128)(2,1)S(1)}, u32[]{:S(2)}, u32[]{:S(2)}) collective-permute-start(bf16[16,2880]{1,0:T(8,128)(2,1)} %get-tuple-element.28), channel_id=1, source_target_pairs={{0,1},{1,0},{2,3},{3,2},{4,5},{5,4},{6,7},{7,6},{8,9},{9,8},{10,11... | collective-permute-start | bytes 276488 | tf_op jit(solution)/shard_map/ppermute | solution.py:579
  13.3 2.9 %collective-permute-done.got_ref = bf16[16,2880]{1,0:T(8,128)(2,1)S(1)} collective-permute-done((bf16[16,2880]{1,0:T(8,128)(2,1)}, bf16[16,2880]{1,0:T(8,128)(2,1)S(1)}, u32[]{:S(2)}, u32[]{:S(2)}) %collective-permute-start) | collective-permute-done | bytes 92192 | tf_op jit(solution)/shard_map/ppermute | solution.py:579
  16.2 0.9 copy-done.2
  17.5 4.0 %collective-permute-start.3 = (bf16[16,2944]{1,0:T(8,128)(2,1)S(1)}, bf16[16,2944]{1,0:T(8,128)(2,1)S(1)}, u32[]{:S(2)}, u32[]{:S(2)}) collective-permute-start(bf16[16,2944]{1,0:T(8,128)(2,1)S(1)} %get-tuple-element.31), channel_id=1, source_target_pairs={{0,24},{1,25},{2,26},{3,27},{4,28},{5,29},{6,30},{7,31},{8,16},{9,... | collective-permute-start | bytes 282632 | tf_op jit(solution)/shard_map/ppermute | solution.py:579
  21.6 0.6 collective-permute-start.1
  22.2 4.3 %collective-permute-done.1 = bf16[16,2944]{1,0:T(8,128)(2,1)S(1)} collective-permute-done((bf16[16,2944]{1,0:T(8,128)(2,1)S(1)}, bf16[16,2944]{1,0:T(8,128)(2,1)S(1)}, u32[]{:S(2)}, u32[]{:S(2)}) %collective-permute-start.1) | collective-permute-done | bytes 94240 | tf_op jit(solution)/shard_map/ppermute | solution.py:579
  26.5 2.0 %collective-permute-done.2 = bf16[16,2944]{1,0:T(8,128)(2,1)S(1)} collective-permute-done((bf16[16,2944]{1,0:T(8,128)(2,1)S(1)}, bf16[16,2944]{1,0:T(8,128)(2,1)S(1)}, u32[]{:S(2)}, u32[]{:S(2)}) %collective-permute-start.2) | collective-permute-done | bytes 94240 | tf_op jit(solution)/shard_map/ppermute | solution.py:579
  28.5 1.6 %collective-permute-start.4 = (bf16[64,2944]{1,0:T(8,128)(2,1)S(1)}, bf16[64,2944]{1,0:T(8,128)(2,1)S(1)}, u32[]{:S(2)}, u32[]{:S(2)}) collective-permute-start(bf16[64,2944]{1,0:T(8,128)(2,1)S(1)} %constant_dynamic-update-slice_fusion.refs_0_), channel_id=1, source_target_pairs={{0,4},{1,5},{2,3},{3,2},{4,0},{5,1},{6,7},{7,6},{8,12},{9,13},{10,... | collective-permute-start | bytes 1130504 | tf_op jit(solution)/shard_map/ppermute | solution.py:590
  30.1 3.5 %load.3 = (bf16[1440,2880]{1,0:T(8,128)(2,1)S(1)}, bf16[16,128]{1,0:T(8,128)(2,1)S(1)}) custom-call(bf16[1440,2880]{1,0:T(8,128)(2,1)} %bitcast.18), custom_call_target="tpu_custom_call" | custom-call | bytes 16588800 | tf_op jit(solution)/shard_map/load/pallas_call | solution.py:289
  33.6 3.4 %copy-done = bf16[1,2880,1440]{1,2,0:T(8,128)(2,1)S(1)} copy-done((bf16[1,2880,1440]{1,2,0:T(8,128)(2,1)S(1)}, bf16[1,2880,1440]{1,2,0:T(8,128)(2,1)}, u32[]{:S(2)}) %copy-start) | copy-done | bytes 8294424
  37.0 1.4 %load.4 = (bf16[1440,2880]{1,0:T(8,128)(2,1)S(1)}, bf16[16,128]{1,0:T(8,128)(2,1)S(1)}) custom-call(bf16[1440,2880]{1,0:T(8,128)(2,1)S(1)} %bitcast.13), custom_call_target="tpu_custom_call" | custom-call | bytes 16588800 | tf_op jit(solution)/shard_map/load/pallas_call | solution.py:289
  38.4 1.6 %collective-permute-start.5 = (bf16[64,2944]{1,0:T(8,128)(2,1)S(1)}, bf16[64,2944]{1,0:T(8,128)(2,1)S(1)}, u32[]{:S(2)}, u32[]{:S(2)}) collective-permute-start(bf16[64,2944]{1,0:T(8,128)(2,1)S(1)} %constant_dynamic-update-slice_fusion.refs_0_), channel_id=1, source_target_pairs={{0,1},{1,0},{2,6},{3,7},{4,5},{5,4},{6,2},{7,3},{8,9},{9,8},{10,14... | collective-permute-start | bytes 1130504 | tf_op jit(solution)/shard_map/ppermute | solution.py:590
  40.5 3.4 %copy-done.1 = bf16[1,1440,2880]{2,1,0:T(8,128)(2,1)S(1)} copy-done((bf16[1,1440,2880]{2,1,0:T(8,128)(2,1)S(1)}, bf16[1,1440,2880]{2,1,0:T(8,128)(2,1)}, u32[]{:S(2)}) %copy-start.1) | copy-done | bytes 8294424
  43.9 1.4 %load.5 = (bf16[1440,2880]{1,0:T(8,128)(2,1)S(1)}, bf16[16,128]{1,0:T(8,128)(2,1)S(1)}) custom-call(bf16[1440,2880]{1,0:T(8,128)(2,1)S(1)} %bitcast.14), custom_call_target="tpu_custom_call" | custom-call | bytes 16588800 | tf_op jit(solution)/shard_map/load/pallas_call | solution.py:289
  46.1 4.0 %collective-permute-done.6.refs_3_ = bf16[64,2944]{1,0:T(8,128)(2,1)S(1)} collective-permute-done((bf16[64,2944]{1,0:T(8,128)(2,1)S(1)}, bf16[64,2944]{1,0:T(8,128)(2,1)S(1)}, u32[]{:S(2)}, u32[]{:S(2)}) %collective-permute-start.6) | collective-permute-done | bytes 376864 | tf_op jit(solution)/shard_map/ppermute | solution.py:590
  50.1 1.7 %collective-permute-done.10.refs_7_ = bf16[64,2944]{1,0:T(8,128)(2,1)S(1)} collective-permute-done((bf16[64,2944]{1,0:T(8,128)(2,1)S(1)}, bf16[64,2944]{1,0:T(8,128)(2,1)S(1)}, u32[]{:S(2)}, u32[]{:S(2)}) %collective-permute-start.10) | collective-permute-done | bytes 376864 | tf_op jit(solution)/shard_map/ppermute | solution.py:579
  51.8 9.8 %expert.1 = (bf16[64,2880]{1,0:T(8,128)(2,1)S(1)}, bf16[64,2880]{1,0:T(8,128)(2,1)S(1)}, bf16[64,2880]{1,0:T(8,128)(2,1)S(1)}, bf16[64,2880]{1,0:T(8,128)(2,1)S(...) custom-call(s32[1]{0:T(128)} %get-tuple-element.30.expert_ref, ...), custom_call_target="tpu_custom_call" | custom-call | flops 6370099200 | bytes 24883200 | tf_op jit(solution)/shard_map/expert/pallas_call | solution.py:549
  62.7 0.7 collective-permute-done.15
  63.5 1.6 %collective-permute-start.16 = (bf16[64,2880]{1,0:T(8,128)(2,1)S(1)}, bf16[64,2880]{1,0:T(8,128)(2,1)S(1)}, u32[]{:S(2)}, u32[]{:S(2)}) collective-permute-start(bf16[64,2880]{1,0:T(8,128)(2,1)S(1)} %add_convert_fusion.2), channel_id=1, source_target_pairs={{0,1},{1,0},{2,6},{3,7},{4,5},{5,4},{6,2},{7,3},{8,9},{9,8},{10,14... | collective-permute-start | bytes 1105928 | tf_op jit(solution)/shard_map/ppermute | solution.py:590
  65.2 1.0 %collective-permute-start.13 = (bf16[64,2880]{1,0:T(8,128)(2,1)S(1)}, bf16[64,2880]{1,0:T(8,128)(2,1)S(1)}, u32[]{:S(2)}, u32[]{:S(2)}) collective-permute-start(bf16[64,2880]{1,0:T(8,128)(2,1)S(1)} %add_convert_fusion.5), channel_id=1, source_target_pairs={{0,1},{1,0},{2,6},{3,7},{4,5},{5,4},{6,2},{7,3},{8,9},{9,8},{10,14... | collective-permute-start | bytes 1105928 | tf_op jit(solution)/shard_map/ppermute | solution.py:590
  66.1 5.0 %collective-permute-done.16 = bf16[64,2880]{1,0:T(8,128)(2,1)S(1)} collective-permute-done((bf16[64,2880]{1,0:T(8,128)(2,1)S(1)}, bf16[64,2880]{1,0:T(8,128)(2,1)S(1)}, u32[]{:S(2)}, u32[]{:S(2)}) %collective-permute-start.16) | collective-permute-done | bytes 368672 | tf_op jit(solution)/shard_map/ppermute | solution.py:590
  71.3 0.6 collective-permute-start.17
  71.9 5.2 %collective-permute-done.13 = bf16[64,2880]{1,0:T(8,128)(2,1)S(1)} collective-permute-done((bf16[64,2880]{1,0:T(8,128)(2,1)S(1)}, bf16[64,2880]{1,0:T(8,128)(2,1)S(1)}, u32[]{:S(2)}, u32[]{:S(2)}) %collective-permute-start.13) | collective-permute-done | bytes 368672 | tf_op jit(solution)/shard_map/ppermute | solution.py:590
  77.1 1.9 %collective-permute-done.17 = bf16[64,2880]{1,0:T(8,128)(2,1)S(1)} collective-permute-done((bf16[64,2880]{1,0:T(8,128)(2,1)S(1)}, bf16[64,2880]{1,0:T(8,128)(2,1)S(1)}, u32[]{:S(2)}, u32[]{:S(2)}) %collective-permute-start.17) | collective-permute-done | bytes 368672 | tf_op jit(solution)/shard_map/ppermute | solution.py:590
  79.2 0.5 collective-permute-start.18
  79.7 2.0 %collective-permute-start.20 = (bf16[16,2880]{1,0:T(8,128)(2,1)S(1)}, bf16[16,2880]{1,0:T(8,128)(2,1)S(1)}, u32[]{:S(2)}, u32[]{:S(2)}) collective-permute-start(bf16[16,2880]{1,0:T(8,128)(2,1)S(1)} %get-tuple-element.53), channel_id=1, source_target_pairs={{0,24},{1,25},{2,26},{3,27},{4,28},{5,29},{6,30},{7,31},{8,16},{9,... | collective-permute-start | bytes 276488 | tf_op jit(solution)/shard_map/ppermute | solution.py:579
  81.7 1.0 %collective-permute-start.19 = (bf16[16,2880]{1,0:T(8,128)(2,1)S(1)}, bf16[16,2880]{1,0:T(8,128)(2,1)S(1)}, u32[]{:S(2)}, u32[]{:S(2)}) collective-permute-start(bf16[16,2880]{1,0:T(8,128)(2,1)S(1)} %get-tuple-element.54), channel_id=1, source_target_pairs={{0,16},{1,17},{2,18},{3,19},{4,20},{5,21},{6,22},{7,23},{8,24},{9,... | collective-permute-start | bytes 276488 | tf_op jit(solution)/shard_map/ppermute | solution.py:579
  82.7 1.2 %collective-permute-done.18 = bf16[16,2880]{1,0:T(8,128)(2,1)S(1)} collective-permute-done((bf16[16,2880]{1,0:T(8,128)(2,1)S(1)}, bf16[16,2880]{1,0:T(8,128)(2,1)S(1)}, u32[]{:S(2)}, u32[]{:S(2)}) %collective-permute-start.18) | collective-permute-done | bytes 92192 | tf_op jit(solution)/shard_map/ppermute | solution.py:579
  84.0 3.3 %collective-permute-done.20 = bf16[16,2880]{1,0:T(8,128)(2,1)S(1)} collective-permute-done((bf16[16,2880]{1,0:T(8,128)(2,1)S(1)}, bf16[16,2880]{1,0:T(8,128)(2,1)S(1)}, u32[]{:S(2)}, u32[]{:S(2)}) %collective-permute-start.20) | collective-permute-done | bytes 92192 | tf_op jit(solution)/shard_map/ppermute | solution.py:579
  87.2 4.0 %collective-permute-done.19 = bf16[16,2880]{1,0:T(8,128)(2,1)S(1)} collective-permute-done((bf16[16,2880]{1,0:T(8,128)(2,1)S(1)}, bf16[16,2880]{1,0:T(8,128)(2,1)S(1)}, u32[]{:S(2)}, u32[]{:S(2)}) %collective-permute-start.19) | collective-permute-done | bytes 92192 | tf_op jit(solution)/shard_map/ppermute | solution.py:579
  91.2 0.7 add_convert_fusion.7
  (50 shorter events, 3.5 us)
Async XLA Ops:
  0.6 12.6 %copy-start.9 = (bf16[2880]{0:T(1024)(128)(2,1)S(1)}, bf16[2880]{0:T(1024)(128)(2,1)}, u32[]{:S(2)}) copy-start(bf16[2880]{0:T(1024)(128)(2,1)} %param.23) | copy-start | bytes 17284
  0.6 12.6 %copy-start.10 = (bf16[2880]{0:T(1024)(128)(2,1)S(1)}, bf16[2880]{0:T(1024)(128)(2,1)}, u32[]{:S(2)}) copy-start(bf16[2880]{0:T(1024)(128)(2,1)} %param.25) | copy-start | bytes 17284
  0.7 15.5 %copy-start.4 = (bf16[16,2880]{1,0:T(8,128)(2,1)S(1)}, bf16[16,2880]{1,0:T(8,128)(2,1)}, u32[]{:S(2)}) copy-start(bf16[16,2880]{1,0:T(8,128)(2,1)} %down_bias_ref.1) | copy-start | bytes 276484
  0.7 15.5 %copy-start.8 = (f32[16,4]{0,1:T(4,128)S(1)}, f32[16,4]{0,1:T(4,128)}, u32[]{:S(2)}) copy-start(f32[16,4]{0,1:T(4,128)} %param.27) | copy-start | bytes 772
  0.7 15.5 %copy-start.7 = (s32[16,4]{0,1:T(4,128)S(1)}, s32[16,4]{0,1:T(4,128)}, u32[]{:S(2)}) copy-start(s32[16,4]{0,1:T(4,128)} %param.26) | copy-start | bytes 772
  0.7 15.5 %copy-start.3 = (bf16[16,2880]{1,0:T(8,128)(2,1)S(1)}, bf16[16,2880]{1,0:T(8,128)(2,1)}, u32[]{:S(2)}) copy-start(bf16[16,2880]{1,0:T(8,128)(2,1)} %residual_ref.1) | copy-start | bytes 276484
  10.2 5.9 %collective-permute-start = (bf16[16,2880]{1,0:T(8,128)(2,1)}, bf16[16,2880]{1,0:T(8,128)(2,1)S(1)}, u32[]{:S(2)}, u32[]{:S(2)}) collective-permute-start(bf16[16,2880]{1,0:T(8,128)(2,1)} %get-tuple-element.28), channel_id=1, source_target_pairs={{0,1},{1,0},{2,3},{3,2},{4,5},{5,4},{6,7},{7,6},{8,9},{9,8},{10,11... | collective-permute-start | bytes 276488 | tf_op jit(solution)/shard_map/ppermute | solution.py:579
  16.2 0.9 %copy-start.2 = (f32[16,2880]{1,0:T(8,128)S(1)}, f32[16,2880]{1,0:T(8,128)}, u32[]{:S(2)}) copy-start(f32[16,2880]{1,0:T(8,128)} %get-tuple-element.27.own_ref) | copy-start | bytes 552964
  17.5 11.0 %collective-permute-start.3 = (bf16[16,2944]{1,0:T(8,128)(2,1)S(1)}, bf16[16,2944]{1,0:T(8,128)(2,1)S(1)}, u32[]{:S(2)}, u32[]{:S(2)}) collective-permute-start(bf16[16,2944]{1,0:T(8,128)(2,1)S(1)} %get-tuple-element.31), channel_id=1, source_target_pairs={{0,24},{1,25},{2,26},{3,27},{4,28},{5,29},{6,30},{7,31},{8,16},{9,... | collective-permute-start | bytes 282632 | tf_op jit(solution)/shard_map/ppermute | solution.py:579
  21.5 6.9 %collective-permute-start.2 = (bf16[16,2944]{1,0:T(8,128)(2,1)S(1)}, bf16[16,2944]{1,0:T(8,128)(2,1)S(1)}, u32[]{:S(2)}, u32[]{:S(2)}) collective-permute-start(bf16[16,2944]{1,0:T(8,128)(2,1)S(1)} %get-tuple-element.31), channel_id=1, source_target_pairs={{0,16},{1,17},{2,18},{3,19},{4,20},{5,21},{6,22},{7,23},{8,24},{9,... | collective-permute-start | bytes 282632 | tf_op jit(solution)/shard_map/ppermute | solution.py:579
  21.6 4.9 %collective-permute-start.1 = (bf16[16,2944]{1,0:T(8,128)(2,1)S(1)}, bf16[16,2944]{1,0:T(8,128)(2,1)S(1)}, u32[]{:S(2)}, u32[]{:S(2)}) collective-permute-start(bf16[16,2944]{1,0:T(8,128)(2,1)S(1)} %get-tuple-element.31), channel_id=1, source_target_pairs={{0,8},{1,9},{2,10},{3,11},{4,12},{5,13},{6,14},{7,15},{8,0},{9,1},... | collective-permute-start | bytes 282632 | tf_op jit(solution)/shard_map/ppermute | solution.py:579
  28.5 11.4 %collective-permute-start.4 = (bf16[64,2944]{1,0:T(8,128)(2,1)S(1)}, bf16[64,2944]{1,0:T(8,128)(2,1)S(1)}, u32[]{:S(2)}, u32[]{:S(2)}) collective-permute-start(bf16[64,2944]{1,0:T(8,128)(2,1)S(1)} %constant_dynamic-update-slice_fusion.refs_0_), channel_id=1, source_target_pairs={{0,4},{1,5},{2,3},{3,2},{4,0},{5,1},{6,7},{7,6},{8,12},{9,13},{10,... | collective-permute-start | bytes 1130504 | tf_op jit(solution)/shard_map/ppermute | solution.py:590
  33.6 3.4 %copy-start = (bf16[1,2880,1440]{1,2,0:T(8,128)(2,1)S(1)}, bf16[1,2880,1440]{1,2,0:T(8,128)(2,1)}, u32[]{:S(2)}) copy-start(bf16[1,2880,1440]{1,2,0:T(8,128)(2,1)} %param.30) | copy-start | bytes 24883204
  37.0 14.8 %copy-start.5 = (bf16[1,1440]{1,0:T(2,128)(2,1)S(1)}, bf16[1,1440]{1,0:T(2,128)(2,1)}, u32[]{:S(2)}) copy-start(bf16[1,1440]{1,0:T(2,128)(2,1)} %refs_11_.1) | copy-start | bytes 8644
  37.0 14.8 %copy-start.6 = (bf16[1,1440]{1,0:T(2,128)(2,1)S(1)}, bf16[1,1440]{1,0:T(2,128)(2,1)}, u32[]{:S(2)}) copy-start(bf16[1,1440]{1,0:T(2,128)(2,1)} %refs_12_.1) | copy-start | bytes 8644
  38.4 7.7 %collective-permute-start.5 = (bf16[64,2944]{1,0:T(8,128)(2,1)S(1)}, bf16[64,2944]{1,0:T(8,128)(2,1)S(1)}, u32[]{:S(2)}, u32[]{:S(2)}) collective-permute-start(bf16[64,2944]{1,0:T(8,128)(2,1)S(1)} %constant_dynamic-update-slice_fusion.refs_0_), channel_id=1, source_target_pairs={{0,1},{1,0},{2,6},{3,7},{4,5},{5,4},{6,2},{7,3},{8,9},{9,8},{10,14... | collective-permute-start | bytes 1130504 | tf_op jit(solution)/shard_map/ppermute | solution.py:590
  40.0 10.1 %collective-permute-start.6 = (bf16[64,2944]{1,0:T(8,128)(2,1)S(1)}, bf16[64,2944]{1,0:T(8,128)(2,1)S(1)}, u32[]{:S(2)}, u32[]{:S(2)}) collective-permute-start(bf16[64,2944]{1,0:T(8,128)(2,1)S(1)} %collective-permute-done.4.refs_1_), channel_id=1, source_target_pairs={{0,1},{1,0},{2,6},{3,7},{4,5},{5,4},{6,2},{7,3},{8,9},{9,8},{10,14... | collective-permute-start | bytes 1130504 | tf_op jit(solution)/shard_map/ppermute | solution.py:590
  40.5 3.4 %copy-start.1 = (bf16[1,1440,2880]{2,1,0:T(8,128)(2,1)S(1)}, bf16[1,1440,2880]{2,1,0:T(8,128)(2,1)}, u32[]{:S(2)}) copy-start(bf16[1,1440,2880]{2,1,0:T(8,128)(2,1)} %param.32) | copy-start | bytes 24883204
  45.3 4.8 %collective-permute-start.7 = (bf16[64,2944]{1,0:T(8,128)(2,1)S(1)}, bf16[64,2944]{1,0:T(8,128)(2,1)S(1)}, u32[]{:S(2)}, u32[]{:S(2)}) collective-permute-start(bf16[64,2944]{1,0:T(8,128)(2,1)S(1)} %constant_dynamic-update-slice_fusion.refs_0_), channel_id=1, source_target_pairs={{0,2},{1,3},{2,0},{3,1},{4,6},{5,7},{6,4},{7,5},{8,10},{9,11},{10,... | collective-permute-start | bytes 1130504 | tf_op jit(solution)/shard_map/ppermute | solution.py:579
  45.3 4.8 %collective-permute-start.8 = (bf16[64,2944]{1,0:T(8,128)(2,1)S(1)}, bf16[64,2944]{1,0:T(8,128)(2,1)S(1)}, u32[]{:S(2)}, u32[]{:S(2)}) collective-permute-start(bf16[64,2944]{1,0:T(8,128)(2,1)S(1)} %collective-permute-done.4.refs_1_), channel_id=1, source_target_pairs={{0,2},{1,3},{2,0},{3,1},{4,6},{5,7},{6,4},{7,5},{8,10},{9,11},{10,... | collective-permute-start | bytes 1130504 | tf_op jit(solution)/shard_map/ppermute | solution.py:579
  46.1 4.0 %collective-permute-start.9 = (bf16[64,2944]{1,0:T(8,128)(2,1)S(1)}, bf16[64,2944]{1,0:T(8,128)(2,1)S(1)}, u32[]{:S(2)}, u32[]{:S(2)}) collective-permute-start(bf16[64,2944]{1,0:T(8,128)(2,1)S(1)} %collective-permute-done.5.refs_2_), channel_id=1, source_target_pairs={{0,2},{1,3},{2,0},{3,1},{4,6},{5,7},{6,4},{7,5},{8,10},{9,11},{10,... | collective-permute-start | bytes 1130504 | tf_op jit(solution)/shard_map/ppermute | solution.py:579
  50.1 1.7 %collective-permute-start.10 = (bf16[64,2944]{1,0:T(8,128)(2,1)S(1)}, bf16[64,2944]{1,0:T(8,128)(2,1)S(1)}, u32[]{:S(2)}, u32[]{:S(2)}) collective-permute-start(bf16[64,2944]{1,0:T(8,128)(2,1)S(1)} %collective-permute-done.6.refs_3_), channel_id=1, source_target_pairs={{0,2},{1,3},{2,0},{3,1},{4,6},{5,7},{6,4},{7,5},{8,10},{9,11},{10,... | collective-permute-start | bytes 1130504 | tf_op jit(solution)/shard_map/ppermute | solution.py:579
  61.6 1.8 %collective-permute-start.15 = (bf16[64,2880]{1,0:T(8,128)(2,1)S(1)}, bf16[64,2880]{1,0:T(8,128)(2,1)S(1)}, u32[]{:S(2)}, u32[]{:S(2)}) collective-permute-start(bf16[64,2880]{1,0:T(8,128)(2,1)S(1)} %get-tuple-element.50), channel_id=1, source_target_pairs={{0,2},{1,3},{2,0},{3,1},{4,6},{5,7},{6,4},{7,5},{8,10},{9,11},{10,... | collective-permute-start | bytes 1105928 | tf_op jit(solution)/shard_map/ppermute | solution.py:579
  61.8 10.1 %collective-permute-start.11 = (bf16[64,2880]{1,0:T(8,128)(2,1)S(1)}, bf16[64,2880]{1,0:T(8,128)(2,1)S(1)}, u32[]{:S(2)}, u32[]{:S(2)}) collective-permute-start(bf16[64,2880]{1,0:T(8,128)(2,1)S(1)} %get-tuple-element.44), channel_id=1, source_target_pairs={{0,2},{1,3},{2,0},{3,1},{4,6},{5,7},{6,4},{7,5},{8,10},{9,11},{10,... | collective-permute-start | bytes 1105928 | tf_op jit(solution)/shard_map/ppermute | solution.py:579
  62.2 2.9 %collective-permute-start.12 = (bf16[64,2880]{1,0:T(8,128)(2,1)S(1)}, bf16[64,2880]{1,0:T(8,128)(2,1)S(1)}, u32[]{:S(2)}, u32[]{:S(2)}) collective-permute-start(bf16[64,2880]{1,0:T(8,128)(2,1)S(1)} %get-tuple-element.46), channel_id=1, source_target_pairs={{0,2},{1,3},{2,0},{3,1},{4,6},{5,7},{6,4},{7,5},{8,10},{9,11},{10,... | collective-permute-start | bytes 1105928 | tf_op jit(solution)/shard_map/ppermute | solution.py:579
  62.3 3.8 %collective-permute-start.14 = (bf16[64,2880]{1,0:T(8,128)(2,1)S(1)}, bf16[64,2880]{1,0:T(8,128)(2,1)S(1)}, u32[]{:S(2)}, u32[]{:S(2)}) collective-permute-start(bf16[64,2880]{1,0:T(8,128)(2,1)S(1)} %get-tuple-element.48), channel_id=1, source_target_pairs={{0,2},{1,3},{2,0},{3,1},{4,6},{5,7},{6,4},{7,5},{8,10},{9,11},{10,... | collective-permute-start | bytes 1105928 | tf_op jit(solution)/shard_map/ppermute | solution.py:579
  63.5 7.7 %collective-permute-start.16 = (bf16[64,2880]{1,0:T(8,128)(2,1)S(1)}, bf16[64,2880]{1,0:T(8,128)(2,1)S(1)}, u32[]{:S(2)}, u32[]{:S(2)}) collective-permute-start(bf16[64,2880]{1,0:T(8,128)(2,1)S(1)} %add_convert_fusion.2), channel_id=1, source_target_pairs={{0,1},{1,0},{2,6},{3,7},{4,5},{5,4},{6,2},{7,3},{8,9},{9,8},{10,14... | collective-permute-start | bytes 1105928 | tf_op jit(solution)/shard_map/ppermute | solution.py:590
  65.2 11.9 %collective-permute-start.13 = (bf16[64,2880]{1,0:T(8,128)(2,1)S(1)}, bf16[64,2880]{1,0:T(8,128)(2,1)S(1)}, u32[]{:S(2)}, u32[]{:S(2)}) collective-permute-start(bf16[64,2880]{1,0:T(8,128)(2,1)S(1)} %add_convert_fusion.5), channel_id=1, source_target_pairs={{0,1},{1,0},{2,6},{3,7},{4,5},{5,4},{6,2},{7,3},{8,9},{9,8},{10,14... | collective-permute-start | bytes 1105928 | tf_op jit(solution)/shard_map/ppermute | solution.py:590
  71.3 7.7 %collective-permute-start.17 = (bf16[64,2880]{1,0:T(8,128)(2,1)S(1)}, bf16[64,2880]{1,0:T(8,128)(2,1)S(1)}, u32[]{:S(2)}, u32[]{:S(2)}) collective-permute-start(bf16[64,2880]{1,0:T(8,128)(2,1)S(1)} %add_convert_fusion.1), channel_id=1, source_target_pairs={{0,4},{1,5},{2,3},{3,2},{4,0},{5,1},{6,7},{7,6},{8,12},{9,13},{10,... | collective-permute-start | bytes 1105928 | tf_op jit(solution)/shard_map/ppermute | solution.py:590
  79.2 4.8 %collective-permute-start.18 = (bf16[16,2880]{1,0:T(8,128)(2,1)S(1)}, bf16[16,2880]{1,0:T(8,128)(2,1)S(1)}, u32[]{:S(2)}, u32[]{:S(2)}) collective-permute-start(bf16[16,2880]{1,0:T(8,128)(2,1)S(1)} %get-tuple-element.52), channel_id=1, source_target_pairs={{0,8},{1,9},{2,10},{3,11},{4,12},{5,13},{6,14},{7,15},{8,0},{9,1},... | collective-permute-start | bytes 276488 | tf_op jit(solution)/shard_map/ppermute | solution.py:579
  79.7 7.5 %collective-permute-start.20 = (bf16[16,2880]{1,0:T(8,128)(2,1)S(1)}, bf16[16,2880]{1,0:T(8,128)(2,1)S(1)}, u32[]{:S(2)}, u32[]{:S(2)}) collective-permute-start(bf16[16,2880]{1,0:T(8,128)(2,1)S(1)} %get-tuple-element.53), channel_id=1, source_target_pairs={{0,24},{1,25},{2,26},{3,27},{4,28},{5,29},{6,30},{7,31},{8,16},{9,... | collective-permute-start | bytes 276488 | tf_op jit(solution)/shard_map/ppermute | solution.py:579
  81.7 9.5 %collective-permute-start.19 = (bf16[16,2880]{1,0:T(8,128)(2,1)S(1)}, bf16[16,2880]{1,0:T(8,128)(2,1)S(1)}, u32[]{:S(2)}, u32[]{:S(2)}) collective-permute-start(bf16[16,2880]{1,0:T(8,128)(2,1)S(1)} %get-tuple-element.54), channel_id=1, source_target_pairs={{0,16},{1,17},{2,18},{3,19},{4,20},{5,21},{6,22},{7,23},{8,24},{9,... | collective-permute-start | bytes 276488 | tf_op jit(solution)/shard_map/ppermute | solution.py:579

commit v5 on v4

--- a/solution.py
+++ b/solution.py
@@ -273,7 +273,7 @@
     )
 
 
-def load_kernel(source, target, sign, sems):
+def load_kernel(after_ref, source, target, sign, sems):
     copies = []
     for i, (start, size) in enumerate(tiles(source.shape[0], LOAD_ROWS)):
         here = pl.ds(start, size)
@@ -285,14 +285,14 @@
     sign[...] = target[: sign.shape[0], : sign.shape[1]]
 
 
-def load(weight, reserve):
+def load(weight, after, reserve):
     return pl.pallas_call(
         load_kernel,
         out_shape=[
             jax.ShapeDtypeStruct(weight.shape, weight.dtype),
             jax.ShapeDtypeStruct((16, LANES), weight.dtype),
         ],
-        in_specs=[anywhere()],
+        in_specs=[anywhere()] * 2,
         out_specs=[vmem()] * 2,
         scratch_shapes=[pltpu.SemaphoreType.DMA((len(tiles(weight.shape[0], LOAD_ROWS)),))],
         compiler_params=pltpu.CompilerParams(vmem_limit_bytes=reserve),
@@ -300,7 +300,7 @@
             flops=0, bytes_accessed=4 * weight.size, transcendentals=0
         ),
         name="load",
-    )(weight)
+    )(after, weight)
 
 
 def expert_kernel(parts, block, limit, step, expert_ref, *refs):
@@ -421,7 +421,7 @@
         )
         for i, (start, size) in enumerate(chunks)
     ]
-    for copy in copies[:2]:
+    for copy in copies:
         copy.start()
     named = jnp.broadcast_to(segments_ref[...].astype(jnp.float32), (length, length))
     visible = (named == named.T) & (
@@ -443,7 +443,18 @@
         )
         return tile * cosine + swapped * sine
 
-    seen = jnp.concatenate([visible] * (2 * group_tiles), axis=0)
+    group_heads = 2 * group_tiles
+    token = lax.broadcasted_iota(jnp.int32, (length, group_heads * length), 1)
+    repeat = token % length == lax.broadcasted_iota(jnp.int32, token.shape, 0)
+    seen = (
+        jnp.dot(
+            jnp.where(visible, 1.0, 0.0).T.astype(jnp.bfloat16),
+            jnp.where(repeat, 1.0, 0.0).astype(jnp.bfloat16),
+            preferred_element_type=jnp.float32,
+        )
+        > 0.5
+    )
+    head_of = lax.broadcasted_iota(jnp.int32, (1, group_heads * length), 1) // length
     for k in range(kv_heads):
         raw = keys_values_ref[:, k * LANES : (k + 1) * LANES].astype(jnp.float32)
         pair = jnp.where(left, turned(raw), raw).astype(jnp.bfloat16)
@@ -452,25 +463,21 @@
                 b * PAGE_LEN : (b + 1) * PAGE_LEN
             ]
         heads = []
-        sinks = []
+        sink = jnp.zeros(head_of.shape, jnp.float32)
+        for h in range(group_heads):
+            sink = jnp.where(head_of == h, sink_ref[k * group_heads + h], sink)
         for t in range(k * group_tiles, (k + 1) * group_tiles):
             tile = turned(queries_ref[:, t * LANES : (t + 1) * LANES].astype(jnp.float32))
             heads.append(jnp.where(left, tile, 0.0))
             heads.append(jnp.where(left, pltpu.roll(tile, HEAD, 1), 0.0))
-            sinks.append(jnp.full((length, 1), sink_ref[2 * t], jnp.float32))
-            sinks.append(jnp.full((length, 1), sink_ref[2 * t + 1], jnp.float32))
-        sink = jnp.concatenate(sinks, axis=0)
-        scores = lax.dot_general(
-            jnp.concatenate(heads, axis=0).astype(jnp.bfloat16),
-            pair,
-            (((1,), (1,)), ((), ())),
-            preferred_element_type=jnp.float32,
+        scores = by_rows(
+            pair, jnp.concatenate(heads, axis=0).astype(jnp.bfloat16)
         ) * HEAD ** (-0.5)
         scores = jnp.where(seen, scores, -1e30)
-        highest = jnp.maximum(jnp.max(scores, axis=-1, keepdims=True), sink)
+        highest = jnp.maximum(jnp.max(scores, axis=0, keepdims=True), sink)
         expo = jnp.where(seen, jnp.exp(scores - highest), 0.0)
-        denominator = jnp.sum(expo, axis=-1, keepdims=True) + jnp.exp(sink - highest)
-        probabilities = (expo / denominator).astype(jnp.bfloat16)
+        denominator = jnp.sum(expo, axis=0, keepdims=True) + jnp.exp(sink - highest)
+        probabilities = (expo / denominator).T.astype(jnp.bfloat16)
         mixed = jnp.dot(probabilities, pair, preferred_element_type=jnp.float32)
         for t in range(group_tiles):
             even = mixed[2 * t * length : (2 * t + 1) * length]
@@ -483,8 +490,6 @@
     half = own_ref.shape[0]
     for i, (start, size) in enumerate(chunks):
         copies[i].wait()
-        if i + 2 < len(copies):
-            copies[i + 2].start()
         projected = by_rows(attended[...], weight[start : start + size])
         top, bottom = projected[:half], projected[half:]
         own_ref[:, start : start + size] = jnp.where(first_side, top, bottom)
@@ -590,19 +595,23 @@
     return lax.ppermute(array, AXES, pairs)
 
 
-def gather_rows(rows, n_req, signs):
-    signs = list(signs)
+def gather_rows(rows, n_req, weights, signs):
     outer = n_req // 4
     others = [moved(rows, n_req, (k, 0, 0, 0)) for k in range(1, outer)]
+    weights[0], signs[0] = load(weights[0], rows, 40 * 2**20)
+    others[0], signs[0] = lax.optimization_barrier((others[0], signs[0]))
     line = jnp.concatenate([rows] + others)
     first = crossed(line, n_req, 0)
-    second = crossed(line, n_req, 1)
-    sent, signs[0], signs[1] = lax.optimization_barrier((first, signs[0], signs[1]))
-    both = crossed(sent, n_req, 1)
+    weights[1], signs[1] = load(weights[1], line, 2 * 2**20)
+    late, signs[1] = lax.optimization_barrier((line, signs[1]))
+    second = crossed(late, n_req, 1)
+    both = crossed(first, n_req, 1)
     own = [line, first, second, both]
-    sent, signs[2] = lax.optimization_barrier((both, signs[2]))
+    sent = both
+    weights[2], signs[2] = load(weights[2], line, 2 * 2**20)
+    sent, signs[2] = lax.optimization_barrier((sent, signs[2]))
     pieces = own + [moved(piece, n_req, (0, 0, 1, 0)) for piece in (line, first, second, sent)]
-    return pieces, signs
+    return pieces
 
 
 def add_rows(left, right):
@@ -652,6 +661,8 @@
         side, expert, page_table, sink_logits, queries, keys_values, segments, out_weight
     )
     got = moved(other, n_req, (0, 0, 0, 1))
+    weights = [gate_weight[0].T, up_weight[0].T, down_weight[0]]
+    signs = [None] * len(weights)
     experts = down_bias.shape[0]
     base, rows = pl.pallas_call(
         mid_kernel,
@@ -673,19 +684,15 @@
         route_logits.T,
         down_bias,
     )
-    signs = [None] * 3
-    gate, signs[0] = load(gate_weight[0].T, 40 * 2**20)
-    up, signs[1] = load(up_weight[0].T, 2 * 2**20)
-    down, signs[2] = load(down_weight[0], 2 * 2**20)
-    pieces, signs = gather_rows(rows, n_req, signs)
+    pieces = gather_rows(rows, n_req, weights, signs)
     sums = run_expert(
         expert,
         pieces,
-        gate,
+        weights[0],
         gate_bias,
-        up,
+        weights[1],
         up_bias,
-        down,
+        weights[2],
         signs,
         tok_count,
         slot_limit(tok_count, route_ids.shape[1], experts),

time: 92.2 us -> 87.9 us (0.953)
  waiting for transfers between devices: 36.4 us -> 31.6 us
  starting transfers between devices: 19.7 us -> 21.3 us
  Pallas kernels: 26 us -> 24.8 us
    ppermute x15, waiting for transfers between devices: 20 us -> 16.8 us  [moved(): return lax.ppermute(array, AXES, pairs)]
    ppermute x6, waiting for transfers between devices: 16.3 us -> 14.8 us  [crossed(): return lax.ppermute(array, AXES, pairs)]
    ppermute x6, starting transfers between devices: 6.81 us -> 8.25 us  [crossed(): return lax.ppermute(array, AXES, pairs)]
    pallas_call x1, Pallas kernels: 9.51 us -> 8.32 us  [run_attention(): pl.pallas_call(attention_kernel, out_shape=[jax.ShapeDtypeStruct((half, w...]
  transfers between devices with their start and end apart: 21 -> 21, of which waited for: 13 -> 12; matrix products, arithmetic and copies ran while one was open for 0% -> 0% of each run, Pallas kernels for 7% -> 7%
where the time goes in v5:
time: 87.9 us; the launch traced here: 87.6 us
  waiting for transfers between devices  31.6 us (36%)
  Pallas kernels  24.8 us (28%)
  starting transfers between devices  21.3 us (24%)
  local copies, waits for them, and re-layouts  7.85 us (9%)
  other arithmetic  1.21 us (1%)
    ppermute x15, waiting for transfers between devices, moved(): return lax.ppermute(array, AXES, pairs)  16.8 us
    ppermute x6, waiting for transfers between devices, crossed(): return lax.ppermute(array, AXES, pairs)  14.8 us
    ppermute x15, starting transfers between devices, moved(): return lax.ppermute(array, AXES, pairs)  13.1 us
    pallas_call x1, Pallas kernels, run_expert(): pl.pallas_call(functools.partial(expert_kernel, parts, block, limit, 512)...  9.83 us
    pallas_call x1, Pallas kernels, run_attention(): pl.pallas_call(attention_kernel, out_shape=[jax.ShapeDtypeStruct((half, w...  8.32 us
    ppermute x6, starting transfers between devices, crossed(): return lax.ppermute(array, AXES, pairs)  8.25 us
    unnamed x25, local copies, waits for them, and re-layouts  7.8 us
    pallas_call x3, Pallas kernels, load(): pl.pallas_call(load_kernel, out_shape=[jax.ShapeDtypeStruct(weight.shape,...  6.22 us
  transfers between devices with their start and end apart: 21, of which 12 were waited for; matrix products, arithmetic and copies ran while one was open for 0% of the time, Pallas kernels for 7%

profile of v5, /device:TPU:0, one launch (start us, length us, event | category | flops | bytes accessed | tf_op | source)
XLA Modules:
  0.0 87.6 jit_solution(1070692380902167092)
XLA Ops:
  0.7 8.3 %attention.1 = (f32[16,2880]{1,0:T(8,128)}, bf16[16,2880]{1,0:T(8,128)(2,1)}, bf16[2,16,512]{2,1,0:T(8,128)(2,1)}, s32[1]{0:T(128)}) custom-call(s32[1]{0:T(128)} %bitcast.side_ref, s32[1]{0:T(128)} %bitcast.1.expert_in_ref, s32[1,2]{1,0:T(1,128)} %pages_ref.1, f32[32]{0:T(128)} %sink_ref.1, bf16[32,2048]{1,0:T(8,128)(2,1)} %queries_ref.1, ...), custom_call_target="tpu_custom_call" | custom-call | tf_op jit(solution)/shard_map/attention/pallas_call | solution.py:507
  9.0 3.0 %collective-permute-start = (bf16[16,2880]{1,0:T(8,128)(2,1)}, bf16[16,2880]{1,0:T(8,128)(2,1)S(1)}, u32[]{:S(2)}, u32[]{:S(2)}) collective-permute-start(bf16[16,2880]{1,0:T(8,128)(2,1)} %get-tuple-element.29), channel_id=1, source_target_pairs={{0,1},{1,0},{2,3},{3,2},{4,5},{5,4},{6,7},{7,6},{8,9},{9,8},{10,11... | collective-permute-start | bytes 276488 | tf_op jit(solution)/shard_map/ppermute | solution.py:584
  12.1 2.9 %collective-permute-done.got_ref = bf16[16,2880]{1,0:T(8,128)(2,1)S(1)} collective-permute-done((bf16[16,2880]{1,0:T(8,128)(2,1)}, bf16[16,2880]{1,0:T(8,128)(2,1)S(1)}, u32[]{:S(2)}, u32[]{:S(2)}) %collective-permute-start) | collective-permute-done | bytes 92192 | tf_op jit(solution)/shard_map/ppermute | solution.py:584
  15.0 0.9 %copy-done.2 = f32[16,2880]{1,0:T(8,128)S(1)} copy-done((f32[16,2880]{1,0:T(8,128)S(1)}, f32[16,2880]{1,0:T(8,128)}, u32[]{:S(2)}) %copy-start.2) | copy-done | bytes 184344
  16.4 4.0 %collective-permute-start.3 = (bf16[16,2944]{1,0:T(8,128)(2,1)S(1)}, bf16[16,2944]{1,0:T(8,128)(2,1)S(1)}, u32[]{:S(2)}, u32[]{:S(2)}) collective-permute-start(bf16[16,2944]{1,0:T(8,128)(2,1)S(1)} %get-tuple-element.32.after_ref), channel_id=1, source_target_pairs={{0,24},{1,25},{2,26},{3,27},{4,28},{5,29},{6,30},{7,31},{8,16},{9,... | collective-permute-start | bytes 282632 | tf_op jit(solution)/shard_map/ppermute | solution.py:584
  20.4 0.6 collective-permute-start.1
  21.0 3.5 %load.3 = (bf16[1440,2880]{1,0:T(8,128)(2,1)S(1)}, bf16[16,128]{1,0:T(8,128)(2,1)S(1)}) custom-call(bf16[16,2944]{1,0:T(8,128)(2,1)S(1)} %get-tuple-element.32.after_ref, bf16[1440,2880]{1,0:T(8,128)(2,1)} %bitcast.18), custom_call_target="tpu_custom_call" | custom-call | bytes 16588800 | tf_op jit(solution)/shard_map/load/pallas_call | solution.py:289
  24.5 0.7 collective-permute-done.1
  25.3 2.0 %collective-permute-done.2 = bf16[16,2944]{1,0:T(8,128)(2,1)S(1)} collective-permute-done((bf16[16,2944]{1,0:T(8,128)(2,1)S(1)}, bf16[16,2944]{1,0:T(8,128)(2,1)S(1)}, u32[]{:S(2)}, u32[]{:S(2)}) %collective-permute-start.2) | collective-permute-done | bytes 94240 | tf_op jit(solution)/shard_map/ppermute | solution.py:584
  27.3 1.6 %collective-permute-start.4 = (bf16[64,2944]{1,0:T(8,128)(2,1)S(1)}, bf16[64,2944]{1,0:T(8,128)(2,1)S(1)}, u32[]{:S(2)}, u32[]{:S(2)}) collective-permute-start(bf16[64,2944]{1,0:T(8,128)(2,1)S(1)} %constant_dynamic-update-slice_fusion.after_ref.refs_0_), channel_id=1, source_target_pairs={{0,4},{1,5},{2,3},{3,2},{4,0},{5,1},{6,7},{7,6},{8,12},{9,13},{10,... | collective-permute-start | bytes 1130504 | tf_op jit(solution)/shard_map/ppermute | solution.py:595
  28.9 3.4 %copy-done = bf16[1,2880,1440]{1,2,0:T(8,128)(2,1)S(1)} copy-done((bf16[1,2880,1440]{1,2,0:T(8,128)(2,1)S(1)}, bf16[1,2880,1440]{1,2,0:T(8,128)(2,1)}, u32[]{:S(2)}) %copy-start) | copy-done | bytes 8294424
  32.3 1.4 %load.4 = (bf16[1440,2880]{1,0:T(8,128)(2,1)S(1)}, bf16[16,128]{1,0:T(8,128)(2,1)S(1)}) custom-call(bf16[64,2944]{1,0:T(8,128)(2,1)S(1)} %constant_dynamic-update-slice_fusion.after_ref.refs_0_, bf16[1440,2880]{1,0:T(8,128)(2,1)S(1)} %bitcast.13), custom_call_target="tpu_custom_call" | custom-call | bytes 16588800 | tf_op jit(solution)/shard_map/load/pallas_call | solution.py:289
  33.7 1.6 %collective-permute-start.5 = (bf16[64,2944]{1,0:T(8,128)(2,1)S(1)}, bf16[64,2944]{1,0:T(8,128)(2,1)S(1)}, u32[]{:S(2)}, u32[]{:S(2)}) collective-permute-start(bf16[64,2944]{1,0:T(8,128)(2,1)S(1)} %constant_dynamic-update-slice_fusion.after_ref.refs_0_), channel_id=1, source_target_pairs={{0,1},{1,0},{2,6},{3,7},{4,5},{5,4},{6,2},{7,3},{8,9},{9,8},{10,14... | collective-permute-start | bytes 1130504 | tf_op jit(solution)/shard_map/ppermute | solution.py:595
  35.3 2.0 %collective-permute-start.6 = (bf16[64,2944]{1,0:T(8,128)(2,1)S(1)}, bf16[64,2944]{1,0:T(8,128)(2,1)S(1)}, u32[]{:S(2)}, u32[]{:S(2)}) collective-permute-start(bf16[64,2944]{1,0:T(8,128)(2,1)S(1)} %collective-permute-done.4.refs_1_), channel_id=1, source_target_pairs={{0,1},{1,0},{2,6},{3,7},{4,5},{5,4},{6,2},{7,3},{8,9},{9,8},{10,14... | collective-permute-start | bytes 1130504 | tf_op jit(solution)/shard_map/ppermute | solution.py:595
  37.2 3.4 %copy-done.1 = bf16[1,1440,2880]{2,1,0:T(8,128)(2,1)S(1)} copy-done((bf16[1,1440,2880]{2,1,0:T(8,128)(2,1)S(1)}, bf16[1,1440,2880]{2,1,0:T(8,128)(2,1)}, u32[]{:S(2)}) %copy-start.1) | copy-done | bytes 8294424
  40.6 1.4 %load.5 = (bf16[1440,2880]{1,0:T(8,128)(2,1)S(1)}, bf16[16,128]{1,0:T(8,128)(2,1)S(1)}) custom-call(bf16[64,2944]{1,0:T(8,128)(2,1)S(1)} %constant_dynamic-update-slice_fusion.after_ref.refs_0_, bf16[1440,2880]{1,0:T(8,128)(2,1)S(1)} %bitcast.14), custom_call_target="tpu_custom_call" | custom-call | bytes 16588800 | tf_op jit(solution)/shard_map/load/pallas_call | solution.py:289
  42.0 0.6 collective-permute-start.8
  42.7 2.7 %collective-permute-done.6.refs_3_ = bf16[64,2944]{1,0:T(8,128)(2,1)S(1)} collective-permute-done((bf16[64,2944]{1,0:T(8,128)(2,1)S(1)}, bf16[64,2944]{1,0:T(8,128)(2,1)S(1)}, u32[]{:S(2)}, u32[]{:S(2)}) %collective-permute-start.6) | collective-permute-done | bytes 376864 | tf_op jit(solution)/shard_map/ppermute | solution.py:595
  45.4 1.7 %collective-permute-done.10.refs_7_ = bf16[64,2944]{1,0:T(8,128)(2,1)S(1)} collective-permute-done((bf16[64,2944]{1,0:T(8,128)(2,1)S(1)}, bf16[64,2944]{1,0:T(8,128)(2,1)S(1)}, u32[]{:S(2)}, u32[]{:S(2)}) %collective-permute-start.10) | collective-permute-done | bytes 376864 | tf_op jit(solution)/shard_map/ppermute | solution.py:584
  47.1 9.8 %expert.1 = (bf16[64,2880]{1,0:T(8,128)(2,1)S(1)}, bf16[64,2880]{1,0:T(8,128)(2,1)S(1)}, bf16[64,2880]{1,0:T(8,128)(2,1)S(1)}, bf16[64,2880]{1,0:T(8,128)(2,1)S(...) custom-call(s32[1]{0:T(128)} %get-tuple-element.31.expert_ref, ...), custom_call_target="tpu_custom_call" | custom-call | flops 6370099200 | bytes 24883200 | tf_op jit(solution)/shard_map/expert/pallas_call | solution.py:554
  58.0 0.7 collective-permute-done.15
  58.8 1.6 %collective-permute-start.16 = (bf16[64,2880]{1,0:T(8,128)(2,1)S(1)}, bf16[64,2880]{1,0:T(8,128)(2,1)S(1)}, u32[]{:S(2)}, u32[]{:S(2)}) collective-permute-start(bf16[64,2880]{1,0:T(8,128)(2,1)S(1)} %add_convert_fusion.2), channel_id=1, source_target_pairs={{0,1},{1,0},{2,6},{3,7},{4,5},{5,4},{6,2},{7,3},{8,9},{9,8},{10,14... | collective-permute-start | bytes 1105928 | tf_op jit(solution)/shard_map/ppermute | solution.py:595
  60.5 1.0 %collective-permute-start.13 = (bf16[64,2880]{1,0:T(8,128)(2,1)S(1)}, bf16[64,2880]{1,0:T(8,128)(2,1)S(1)}, u32[]{:S(2)}, u32[]{:S(2)}) collective-permute-start(bf16[64,2880]{1,0:T(8,128)(2,1)S(1)} %add_convert_fusion.5), channel_id=1, source_target_pairs={{0,1},{1,0},{2,6},{3,7},{4,5},{5,4},{6,2},{7,3},{8,9},{9,8},{10,14... | collective-permute-start | bytes 1105928 | tf_op jit(solution)/shard_map/ppermute | solution.py:595
  61.4 5.0 %collective-permute-done.16 = bf16[64,2880]{1,0:T(8,128)(2,1)S(1)} collective-permute-done((bf16[64,2880]{1,0:T(8,128)(2,1)S(1)}, bf16[64,2880]{1,0:T(8,128)(2,1)S(1)}, u32[]{:S(2)}, u32[]{:S(2)}) %collective-permute-start.16) | collective-permute-done | bytes 368672 | tf_op jit(solution)/shard_map/ppermute | solution.py:595
  66.6 0.6 collective-permute-start.17
  67.2 5.2 %collective-permute-done.13 = bf16[64,2880]{1,0:T(8,128)(2,1)S(1)} collective-permute-done((bf16[64,2880]{1,0:T(8,128)(2,1)S(1)}, bf16[64,2880]{1,0:T(8,128)(2,1)S(1)}, u32[]{:S(2)}, u32[]{:S(2)}) %collective-permute-start.13) | collective-permute-done | bytes 368672 | tf_op jit(solution)/shard_map/ppermute | solution.py:595
  72.4 1.9 %collective-permute-done.17 = bf16[64,2880]{1,0:T(8,128)(2,1)S(1)} collective-permute-done((bf16[64,2880]{1,0:T(8,128)(2,1)S(1)}, bf16[64,2880]{1,0:T(8,128)(2,1)S(1)}, u32[]{:S(2)}, u32[]{:S(2)}) %collective-permute-start.17) | collective-permute-done | bytes 368672 | tf_op jit(solution)/shard_map/ppermute | solution.py:595
  75.0 2.6 %collective-permute-start.20 = (bf16[16,2880]{1,0:T(8,128)(2,1)S(1)}, bf16[16,2880]{1,0:T(8,128)(2,1)S(1)}, u32[]{:S(2)}, u32[]{:S(2)}) collective-permute-start(bf16[16,2880]{1,0:T(8,128)(2,1)S(1)} %get-tuple-element.55), channel_id=1, source_target_pairs={{0,24},{1,25},{2,26},{3,27},{4,28},{5,29},{6,30},{7,31},{8,16},{9,... | collective-permute-start | bytes 276488 | tf_op jit(solution)/shard_map/ppermute | solution.py:584
  78.1 1.1 %collective-permute-done.18 = bf16[16,2880]{1,0:T(8,128)(2,1)S(1)} collective-permute-done((bf16[16,2880]{1,0:T(8,128)(2,1)S(1)}, bf16[16,2880]{1,0:T(8,128)(2,1)S(1)}, u32[]{:S(2)}, u32[]{:S(2)}) %collective-permute-start.18) | collective-permute-done | bytes 92192 | tf_op jit(solution)/shard_map/ppermute | solution.py:584
  79.3 3.9 %collective-permute-done.20 = bf16[16,2880]{1,0:T(8,128)(2,1)S(1)} collective-permute-done((bf16[16,2880]{1,0:T(8,128)(2,1)S(1)}, bf16[16,2880]{1,0:T(8,128)(2,1)S(1)}, u32[]{:S(2)}, u32[]{:S(2)}) %collective-permute-start.20) | collective-permute-done | bytes 92192 | tf_op jit(solution)/shard_map/ppermute | solution.py:584
  83.2 3.7 %collective-permute-done.19 = bf16[16,2880]{1,0:T(8,128)(2,1)S(1)} collective-permute-done((bf16[16,2880]{1,0:T(8,128)(2,1)S(1)}, bf16[16,2880]{1,0:T(8,128)(2,1)S(1)}, u32[]{:S(2)}, u32[]{:S(2)}) %collective-permute-start.19) | collective-permute-done | bytes 92192 | tf_op jit(solution)/shard_map/ppermute | solution.py:584
  86.9 0.7 add_convert_fusion.7
  (50 shorter events, 3.3 us)
Async XLA Ops:
  0.6 11.4 %copy-start.9 = (bf16[2880]{0:T(1024)(128)(2,1)S(1)}, bf16[2880]{0:T(1024)(128)(2,1)}, u32[]{:S(2)}) copy-start(bf16[2880]{0:T(1024)(128)(2,1)} %param.23) | copy-start | bytes 17284
  0.6 11.4 %copy-start.10 = (bf16[2880]{0:T(1024)(128)(2,1)S(1)}, bf16[2880]{0:T(1024)(128)(2,1)}, u32[]{:S(2)}) copy-start(bf16[2880]{0:T(1024)(128)(2,1)} %param.25) | copy-start | bytes 17284
  0.7 14.3 %copy-start.4 = (bf16[16,2880]{1,0:T(8,128)(2,1)S(1)}, bf16[16,2880]{1,0:T(8,128)(2,1)}, u32[]{:S(2)}) copy-start(bf16[16,2880]{1,0:T(8,128)(2,1)} %down_bias_ref.1) | copy-start | bytes 276484
  0.7 14.3 %copy-start.8 = (f32[16,4]{0,1:T(4,128)S(1)}, f32[16,4]{0,1:T(4,128)}, u32[]{:S(2)}) copy-start(f32[16,4]{0,1:T(4,128)} %param.27) | copy-start | bytes 772
  0.7 14.3 %copy-start.7 = (s32[16,4]{0,1:T(4,128)S(1)}, s32[16,4]{0,1:T(4,128)}, u32[]{:S(2)}) copy-start(s32[16,4]{0,1:T(4,128)} %param.26) | copy-start | bytes 772
  0.7 14.3 %copy-start.3 = (bf16[16,2880]{1,0:T(8,128)(2,1)S(1)}, bf16[16,2880]{1,0:T(8,128)(2,1)}, u32[]{:S(2)}) copy-start(bf16[16,2880]{1,0:T(8,128)(2,1)} %residual_ref.1) | copy-start | bytes 276484
  9.0 6.0 %collective-permute-start = (bf16[16,2880]{1,0:T(8,128)(2,1)}, bf16[16,2880]{1,0:T(8,128)(2,1)S(1)}, u32[]{:S(2)}, u32[]{:S(2)}) collective-permute-start(bf16[16,2880]{1,0:T(8,128)(2,1)} %get-tuple-element.29), channel_id=1, source_target_pairs={{0,1},{1,0},{2,3},{3,2},{4,5},{5,4},{6,7},{7,6},{8,9},{9,8},{10,11... | collective-permute-start | bytes 276488 | tf_op jit(solution)/shard_map/ppermute | solution.py:584
  15.0 0.9 %copy-start.2 = (f32[16,2880]{1,0:T(8,128)S(1)}, f32[16,2880]{1,0:T(8,128)}, u32[]{:S(2)}) copy-start(f32[16,2880]{1,0:T(8,128)} %get-tuple-element.28.own_ref) | copy-start | bytes 552964
  16.4 11.0 %collective-permute-start.3 = (bf16[16,2944]{1,0:T(8,128)(2,1)S(1)}, bf16[16,2944]{1,0:T(8,128)(2,1)S(1)}, u32[]{:S(2)}, u32[]{:S(2)}) collective-permute-start(bf16[16,2944]{1,0:T(8,128)(2,1)S(1)} %get-tuple-element.32.after_ref), channel_id=1, source_target_pairs={{0,24},{1,25},{2,26},{3,27},{4,28},{5,29},{6,30},{7,31},{8,16},{9,... | collective-permute-start | bytes 282632 | tf_op jit(solution)/shard_map/ppermute | solution.py:584
  20.4 6.9 %collective-permute-start.2 = (bf16[16,2944]{1,0:T(8,128)(2,1)S(1)}, bf16[16,2944]{1,0:T(8,128)(2,1)S(1)}, u32[]{:S(2)}, u32[]{:S(2)}) collective-permute-start(bf16[16,2944]{1,0:T(8,128)(2,1)S(1)} %get-tuple-element.32.after_ref), channel_id=1, source_target_pairs={{0,16},{1,17},{2,18},{3,19},{4,20},{5,21},{6,22},{7,23},{8,24},{9,... | collective-permute-start | bytes 282632 | tf_op jit(solution)/shard_map/ppermute | solution.py:584
  20.4 4.9 %collective-permute-start.1 = (bf16[16,2944]{1,0:T(8,128)(2,1)S(1)}, bf16[16,2944]{1,0:T(8,128)(2,1)S(1)}, u32[]{:S(2)}, u32[]{:S(2)}) collective-permute-start(bf16[16,2944]{1,0:T(8,128)(2,1)S(1)} %get-tuple-element.32.after_ref), channel_id=1, source_target_pairs={{0,8},{1,9},{2,10},{3,11},{4,12},{5,13},{6,14},{7,15},{8,0},{9,1},... | collective-permute-start | bytes 282632 | tf_op jit(solution)/shard_map/ppermute | solution.py:584
  27.3 7.9 %collective-permute-start.4 = (bf16[64,2944]{1,0:T(8,128)(2,1)S(1)}, bf16[64,2944]{1,0:T(8,128)(2,1)S(1)}, u32[]{:S(2)}, u32[]{:S(2)}) collective-permute-start(bf16[64,2944]{1,0:T(8,128)(2,1)S(1)} %constant_dynamic-update-slice_fusion.after_ref.refs_0_), channel_id=1, source_target_pairs={{0,4},{1,5},{2,3},{3,2},{4,0},{5,1},{6,7},{7,6},{8,12},{9,13},{10,... | collective-permute-start | bytes 1130504 | tf_op jit(solution)/shard_map/ppermute | solution.py:595
  28.9 3.4 %copy-start = (bf16[1,2880,1440]{1,2,0:T(8,128)(2,1)S(1)}, bf16[1,2880,1440]{1,2,0:T(8,128)(2,1)}, u32[]{:S(2)}) copy-start(bf16[1,2880,1440]{1,2,0:T(8,128)(2,1)} %param.30) | copy-start | bytes 24883204
  32.3 14.8 %copy-start.5 = (bf16[1,1440]{1,0:T(2,128)(2,1)S(1)}, bf16[1,1440]{1,0:T(2,128)(2,1)}, u32[]{:S(2)}) copy-start(bf16[1,1440]{1,0:T(2,128)(2,1)} %refs_11_.1) | copy-start | bytes 8644
  32.3 14.8 %copy-start.6 = (bf16[1,1440]{1,0:T(2,128)(2,1)S(1)}, bf16[1,1440]{1,0:T(2,128)(2,1)}, u32[]{:S(2)}) copy-start(bf16[1,1440]{1,0:T(2,128)(2,1)} %refs_12_.1) | copy-start | bytes 8644
  33.7 8.9 %collective-permute-start.5 = (bf16[64,2944]{1,0:T(8,128)(2,1)S(1)}, bf16[64,2944]{1,0:T(8,128)(2,1)S(1)}, u32[]{:S(2)}, u32[]{:S(2)}) collective-permute-start(bf16[64,2944]{1,0:T(8,128)(2,1)S(1)} %constant_dynamic-update-slice_fusion.after_ref.refs_0_), channel_id=1, source_target_pairs={{0,1},{1,0},{2,6},{3,7},{4,5},{5,4},{6,2},{7,3},{8,9},{9,8},{10,14... | collective-permute-start | bytes 1130504 | tf_op jit(solution)/shard_map/ppermute | solution.py:595
  35.3 10.1 %collective-permute-start.6 = (bf16[64,2944]{1,0:T(8,128)(2,1)S(1)}, bf16[64,2944]{1,0:T(8,128)(2,1)S(1)}, u32[]{:S(2)}, u32[]{:S(2)}) collective-permute-start(bf16[64,2944]{1,0:T(8,128)(2,1)S(1)} %collective-permute-done.4.refs_1_), channel_id=1, source_target_pairs={{0,1},{1,0},{2,6},{3,7},{4,5},{5,4},{6,2},{7,3},{8,9},{9,8},{10,14... | collective-permute-start | bytes 1130504 | tf_op jit(solution)/shard_map/ppermute | solution.py:595
  37.2 8.2 %collective-permute-start.7 = (bf16[64,2944]{1,0:T(8,128)(2,1)S(1)}, bf16[64,2944]{1,0:T(8,128)(2,1)S(1)}, u32[]{:S(2)}, u32[]{:S(2)}) collective-permute-start(bf16[64,2944]{1,0:T(8,128)(2,1)S(1)} %constant_dynamic-update-slice_fusion.after_ref.refs_0_), channel_id=1, source_target_pairs={{0,2},{1,3},{2,0},{3,1},{4,6},{5,7},{6,4},{7,5},{8,10},{9,11},{10,... | collective-permute-start | bytes 1130504 | tf_op jit(solution)/shard_map/ppermute | solution.py:584
  37.2 3.4 %copy-start.1 = (bf16[1,1440,2880]{2,1,0:T(8,128)(2,1)S(1)}, bf16[1,1440,2880]{2,1,0:T(8,128)(2,1)}, u32[]{:S(2)}) copy-start(bf16[1,1440,2880]{2,1,0:T(8,128)(2,1)} %param.32) | copy-start | bytes 24883204
  42.0 3.4 %collective-permute-start.8 = (bf16[64,2944]{1,0:T(8,128)(2,1)S(1)}, bf16[64,2944]{1,0:T(8,128)(2,1)S(1)}, u32[]{:S(2)}, u32[]{:S(2)}) collective-permute-start(bf16[64,2944]{1,0:T(8,128)(2,1)S(1)} %collective-permute-done.4.refs_1_), channel_id=1, source_target_pairs={{0,2},{1,3},{2,0},{3,1},{4,6},{5,7},{6,4},{7,5},{8,10},{9,11},{10,... | collective-permute-start | bytes 1130504 | tf_op jit(solution)/shard_map/ppermute | solution.py:584
  42.6 2.8 %collective-permute-start.9 = (bf16[64,2944]{1,0:T(8,128)(2,1)S(1)}, bf16[64,2944]{1,0:T(8,128)(2,1)S(1)}, u32[]{:S(2)}, u32[]{:S(2)}) collective-permute-start(bf16[64,2944]{1,0:T(8,128)(2,1)S(1)} %collective-permute-done.5.refs_2_), channel_id=1, source_target_pairs={{0,2},{1,3},{2,0},{3,1},{4,6},{5,7},{6,4},{7,5},{8,10},{9,11},{10,... | collective-permute-start | bytes 1130504 | tf_op jit(solution)/shard_map/ppermute | solution.py:584
  45.4 1.7 %collective-permute-start.10 = (bf16[64,2944]{1,0:T(8,128)(2,1)S(1)}, bf16[64,2944]{1,0:T(8,128)(2,1)S(1)}, u32[]{:S(2)}, u32[]{:S(2)}) collective-permute-start(bf16[64,2944]{1,0:T(8,128)(2,1)S(1)} %collective-permute-done.6.refs_3_), channel_id=1, source_target_pairs={{0,2},{1,3},{2,0},{3,1},{4,6},{5,7},{6,4},{7,5},{8,10},{9,11},{10,... | collective-permute-start | bytes 1130504 | tf_op jit(solution)/shard_map/ppermute | solution.py:584
  56.9 1.8 %collective-permute-start.15 = (bf16[64,2880]{1,0:T(8,128)(2,1)S(1)}, bf16[64,2880]{1,0:T(8,128)(2,1)S(1)}, u32[]{:S(2)}, u32[]{:S(2)}) collective-permute-start(bf16[64,2880]{1,0:T(8,128)(2,1)S(1)} %get-tuple-element.52), channel_id=1, source_target_pairs={{0,2},{1,3},{2,0},{3,1},{4,6},{5,7},{6,4},{7,5},{8,10},{9,11},{10,... | collective-permute-start | bytes 1105928 | tf_op jit(solution)/shard_map/ppermute | solution.py:584
  57.1 10.1 %collective-permute-start.11 = (bf16[64,2880]{1,0:T(8,128)(2,1)S(1)}, bf16[64,2880]{1,0:T(8,128)(2,1)S(1)}, u32[]{:S(2)}, u32[]{:S(2)}) collective-permute-start(bf16[64,2880]{1,0:T(8,128)(2,1)S(1)} %get-tuple-element.46), channel_id=1, source_target_pairs={{0,2},{1,3},{2,0},{3,1},{4,6},{5,7},{6,4},{7,5},{8,10},{9,11},{10,... | collective-permute-start | bytes 1105928 | tf_op jit(solution)/shard_map/ppermute | solution.py:584
  57.5 2.9 %collective-permute-start.12 = (bf16[64,2880]{1,0:T(8,128)(2,1)S(1)}, bf16[64,2880]{1,0:T(8,128)(2,1)S(1)}, u32[]{:S(2)}, u32[]{:S(2)}) collective-permute-start(bf16[64,2880]{1,0:T(8,128)(2,1)S(1)} %get-tuple-element.48), channel_id=1, source_target_pairs={{0,2},{1,3},{2,0},{3,1},{4,6},{5,7},{6,4},{7,5},{8,10},{9,11},{10,... | collective-permute-start | bytes 1105928 | tf_op jit(solution)/shard_map/ppermute | solution.py:584
  57.6 3.8 %collective-permute-start.14 = (bf16[64,2880]{1,0:T(8,128)(2,1)S(1)}, bf16[64,2880]{1,0:T(8,128)(2,1)S(1)}, u32[]{:S(2)}, u32[]{:S(2)}) collective-permute-start(bf16[64,2880]{1,0:T(8,128)(2,1)S(1)} %get-tuple-element.50), channel_id=1, source_target_pairs={{0,2},{1,3},{2,0},{3,1},{4,6},{5,7},{6,4},{7,5},{8,10},{9,11},{10,... | collective-permute-start | bytes 1105928 | tf_op jit(solution)/shard_map/ppermute | solution.py:584
  58.8 7.7 %collective-permute-start.16 = (bf16[64,2880]{1,0:T(8,128)(2,1)S(1)}, bf16[64,2880]{1,0:T(8,128)(2,1)S(1)}, u32[]{:S(2)}, u32[]{:S(2)}) collective-permute-start(bf16[64,2880]{1,0:T(8,128)(2,1)S(1)} %add_convert_fusion.2), channel_id=1, source_target_pairs={{0,1},{1,0},{2,6},{3,7},{4,5},{5,4},{6,2},{7,3},{8,9},{9,8},{10,14... | collective-permute-start | bytes 1105928 | tf_op jit(solution)/shard_map/ppermute | solution.py:595
  60.5 11.9 %collective-permute-start.13 = (bf16[64,2880]{1,0:T(8,128)(2,1)S(1)}, bf16[64,2880]{1,0:T(8,128)(2,1)S(1)}, u32[]{:S(2)}, u32[]{:S(2)}) collective-permute-start(bf16[64,2880]{1,0:T(8,128)(2,1)S(1)} %add_convert_fusion.5), channel_id=1, source_target_pairs={{0,1},{1,0},{2,6},{3,7},{4,5},{5,4},{6,2},{7,3},{8,9},{9,8},{10,14... | collective-permute-start | bytes 1105928 | tf_op jit(solution)/shard_map/ppermute | solution.py:595
  66.6 7.7 %collective-permute-start.17 = (bf16[64,2880]{1,0:T(8,128)(2,1)S(1)}, bf16[64,2880]{1,0:T(8,128)(2,1)S(1)}, u32[]{:S(2)}, u32[]{:S(2)}) collective-permute-start(bf16[64,2880]{1,0:T(8,128)(2,1)S(1)} %add_convert_fusion.1), channel_id=1, source_target_pairs={{0,4},{1,5},{2,3},{3,2},{4,0},{5,1},{6,7},{7,6},{8,12},{9,13},{10,... | collective-permute-start | bytes 1105928 | tf_op jit(solution)/shard_map/ppermute | solution.py:595
  74.5 4.8 %collective-permute-start.18 = (bf16[16,2880]{1,0:T(8,128)(2,1)S(1)}, bf16[16,2880]{1,0:T(8,128)(2,1)S(1)}, u32[]{:S(2)}, u32[]{:S(2)}) collective-permute-start(bf16[16,2880]{1,0:T(8,128)(2,1)S(1)} %get-tuple-element.54), channel_id=1, source_target_pairs={{0,8},{1,9},{2,10},{3,11},{4,12},{5,13},{6,14},{7,15},{8,0},{9,1},... | collective-permute-start | bytes 276488 | tf_op jit(solution)/shard_map/ppermute | solution.py:584
  75.0 8.2 %collective-permute-start.20 = (bf16[16,2880]{1,0:T(8,128)(2,1)S(1)}, bf16[16,2880]{1,0:T(8,128)(2,1)S(1)}, u32[]{:S(2)}, u32[]{:S(2)}) collective-permute-start(bf16[16,2880]{1,0:T(8,128)(2,1)S(1)} %get-tuple-element.55), channel_id=1, source_target_pairs={{0,24},{1,25},{2,26},{3,27},{4,28},{5,29},{6,30},{7,31},{8,16},{9,... | collective-permute-start | bytes 276488 | tf_op jit(solution)/shard_map/ppermute | solution.py:584
  77.7 9.2 %collective-permute-start.19 = (bf16[16,2880]{1,0:T(8,128)(2,1)S(1)}, bf16[16,2880]{1,0:T(8,128)(2,1)S(1)}, u32[]{:S(2)}, u32[]{:S(2)}) collective-permute-start(bf16[16,2880]{1,0:T(8,128)(2,1)S(1)} %get-tuple-element.56), channel_id=1, source_target_pairs={{0,16},{1,17},{2,18},{3,19},{4,20},{5,21},{6,22},{7,23},{8,24},{9,... | collective-permute-start | bytes 276488 | tf_op jit(solution)/shard_map/ppermute | solution.py:584

commit v6 on v5

--- a/solution.py
+++ b/solution.py
@@ -311,6 +311,7 @@
     total = parts * piece
     units, width = down_w.shape
     group = 2 * piece
+    half = piece // 2
     group_slots = group // block * limit
     up_bias = jnp.broadcast_to(up_bias_ref[...].astype(jnp.float32), (8, units)).T
     gate_bias = jnp.broadcast_to(gate_bias_ref[...].astype(jnp.float32), (8, units)).T
@@ -369,8 +370,11 @@
                 scaled[g * group_slots : (g + 1) * group_slots],
                 preferred_element_type=jnp.float32,
             ).astype(jnp.bfloat16)
-            outs[2 * g][:, cols] = sums[:piece]
-            outs[2 * g + 1][:, cols] = sums[piece:]
+            near, far = outs[g // 2 * 4 + g % 2], outs[g // 2 * 4 + g % 2 + 2]
+            near[:half, cols] = sums[:half]
+            far[:half, cols] = sums[half:piece]
+            near[half:, cols] = sums[piece : piece + half]
+            far[half:, cols] = sums[piece + half :]
 
     last = None
     for start, size in tiles(units, step):
@@ -620,18 +624,23 @@
 
 def scatter_rows(sums, n_req):
     own, other = sums[:4], sums[4:]
-    line, first, second, both = [
-        add_rows(mine, moved(theirs, n_req, (0, 0, 1, 0))) for mine, theirs in zip(own, other)
-    ]
-    first = add_rows(first, crossed(both, n_req, 1))
-    line = add_rows(line, crossed(second, n_req, 1))
-    line = add_rows(line, crossed(first, n_req, 0))
     outer = n_req // 4
-    count = line.shape[0] // outer
-    blocks = [line[k * count : (k + 1) * count] for k in range(outer)]
-    return [blocks[0]] + [
-        moved(block, n_req, (k, 0, 0, 0)) for k, block in enumerate(blocks) if k > 0
-    ]
+    half = outer // 2
+    parts = []
+    for side in (1, 0):
+        here, beyond = [
+            add_rows(own[i], moved(other[i], n_req, (0, 0, 1, 0)))
+            for i in (2 * side, 2 * side + 1)
+        ]
+        here = add_rows(here, crossed(beyond, n_req, 1))
+        middle = here.shape[0] // 2
+        line = add_rows(here[:middle], crossed(here[middle:], n_req, 0))
+        count = middle // half
+        for i in range(half):
+            block = line[i * count : (i + 1) * count]
+            step = half * side + i
+            parts.append(moved(block, n_req, (step, 0, 0, 0)) if step > 0 else block)
+    return parts
 
 
 def gathered_body(

time: 87.9 us -> 84.1 us (0.957)
  waiting for transfers between devices: 31.6 us -> 25.8 us
  starting transfers between devices: 21.3 us -> 23.3 us
    ppermute x15, waiting for transfers between devices: 16.8 us -> 12.5 us  [moved(): return lax.ppermute(array, AXES, pairs)]
    ppermute x6 -> x7, waiting for transfers between devices: 14.8 us -> 13.3 us  [crossed(): return lax.ppermute(array, AXES, pairs)]
    ppermute x6 -> x7, starting transfers between devices: 8.25 us -> 9.41 us  [crossed(): return lax.ppermute(array, AXES, pairs)]
  transfers between devices with their start and end apart: 21 -> 22, of which waited for: 12 -> 11; matrix products, arithmetic and copies ran while one was open for 0% -> 1% of each run, Pallas kernels for 7% -> 7%
where the time goes in v6:
time: 84.1 us; the launch traced here: 83.9 us
  waiting for transfers between devices  25.8 us (31%)
  Pallas kernels  24.7 us (29%)
  starting transfers between devices  23.3 us (28%)
  local copies, waits for them, and re-layouts  7.88 us (9%)
  other arithmetic  1.25 us (1%)
  between operations  0.88 us (1%)
    ppermute x15, starting transfers between devices, moved(): return lax.ppermute(array, AXES, pairs)  13.9 us
    ppermute x7, waiting for transfers between devices, crossed(): return lax.ppermute(array, AXES, pairs)  13.3 us
    ppermute x15, waiting for transfers between devices, moved(): return lax.ppermute(array, AXES, pairs)  12.5 us
    pallas_call x1, Pallas kernels, run_expert(): pl.pallas_call(functools.partial(expert_kernel, parts, block, limit, 512)...  9.76 us
    ppermute x7, starting transfers between devices, crossed(): return lax.ppermute(array, AXES, pairs)  9.41 us
    pallas_call x1, Pallas kernels, run_attention(): pl.pallas_call(attention_kernel, out_shape=[jax.ShapeDtypeStruct((half, w...  8.32 us
    unnamed x25, local copies, waits for them, and re-layouts  7.8 us
    pallas_call x3, Pallas kernels, load(): pl.pallas_call(load_kernel, out_shape=[jax.ShapeDtypeStruct(weight.shape,...  6.22 us
  transfers between devices with their start and end apart: 22, of which 11 were waited for; matrix products, arithmetic and copies ran while one was open for 1% of the time, Pallas kernels for 7%

profile of v6, /device:TPU:0, one launch (start us, length us, event | category | flops | bytes accessed | tf_op | source)
XLA Modules:
  0.0 83.9 jit_solution(17647845397662420900)
XLA Ops:
  0.7 8.3 %attention.1 = (f32[16,2880]{1,0:T(8,128)}, bf16[16,2880]{1,0:T(8,128)(2,1)}, bf16[2,16,512]{2,1,0:T(8,128)(2,1)}, s32[1]{0:T(128)}) custom-call(s32[1]{0:T(128)} %bitcast.side_ref, s32[1]{0:T(128)} %bitcast.1.expert_in_ref, s32[1,2]{1,0:T(1,128)} %pages_ref.1, f32[32]{0:T(128)} %sink_ref.1, bf16[32,2048]{1,0:T(8,128)(2,1)} %queries_ref.1, ...), custom_call_target="tpu_custom_call" | custom-call | tf_op jit(solution)/shard_map/attention/pallas_call | solution.py:511
  9.0 3.0 %collective-permute-start = (bf16[16,2880]{1,0:T(8,128)(2,1)}, bf16[16,2880]{1,0:T(8,128)(2,1)S(1)}, u32[]{:S(2)}, u32[]{:S(2)}) collective-permute-start(bf16[16,2880]{1,0:T(8,128)(2,1)} %get-tuple-element.29), channel_id=1, source_target_pairs={{0,1},{1,0},{2,3},{3,2},{4,5},{5,4},{6,7},{7,6},{8,9},{9,8},{10,11... | collective-permute-start | bytes 276488 | tf_op jit(solution)/shard_map/ppermute | solution.py:588
  12.1 2.9 %collective-permute-done.got_ref = bf16[16,2880]{1,0:T(8,128)(2,1)S(1)} collective-permute-done((bf16[16,2880]{1,0:T(8,128)(2,1)}, bf16[16,2880]{1,0:T(8,128)(2,1)S(1)}, u32[]{:S(2)}, u32[]{:S(2)}) %collective-permute-start) | collective-permute-done | bytes 92192 | tf_op jit(solution)/shard_map/ppermute | solution.py:588
  15.0 0.9 %copy-done.2 = f32[16,2880]{1,0:T(8,128)S(1)} copy-done((f32[16,2880]{1,0:T(8,128)S(1)}, f32[16,2880]{1,0:T(8,128)}, u32[]{:S(2)}) %copy-start.2) | copy-done | bytes 184344
  16.4 4.0 %collective-permute-start.3 = (bf16[16,2944]{1,0:T(8,128)(2,1)S(1)}, bf16[16,2944]{1,0:T(8,128)(2,1)S(1)}, u32[]{:S(2)}, u32[]{:S(2)}) collective-permute-start(bf16[16,2944]{1,0:T(8,128)(2,1)S(1)} %get-tuple-element.32.after_ref), channel_id=1, source_target_pairs={{0,24},{1,25},{2,26},{3,27},{4,28},{5,29},{6,30},{7,31},{8,16},{9,... | collective-permute-start | bytes 282632 | tf_op jit(solution)/shard_map/ppermute | solution.py:588
  20.4 0.6 collective-permute-start.1
  21.0 3.5 %load.3 = (bf16[1440,2880]{1,0:T(8,128)(2,1)S(1)}, bf16[16,128]{1,0:T(8,128)(2,1)S(1)}) custom-call(bf16[16,2944]{1,0:T(8,128)(2,1)S(1)} %get-tuple-element.32.after_ref, bf16[1440,2880]{1,0:T(8,128)(2,1)} %bitcast.18), custom_call_target="tpu_custom_call" | custom-call | bytes 16588800 | tf_op jit(solution)/shard_map/load/pallas_call | solution.py:289
  24.5 0.7 collective-permute-done.1
  25.3 2.0 %collective-permute-done.2 = bf16[16,2944]{1,0:T(8,128)(2,1)S(1)} collective-permute-done((bf16[16,2944]{1,0:T(8,128)(2,1)S(1)}, bf16[16,2944]{1,0:T(8,128)(2,1)S(1)}, u32[]{:S(2)}, u32[]{:S(2)}) %collective-permute-start.2) | collective-permute-done | bytes 94240 | tf_op jit(solution)/shard_map/ppermute | solution.py:588
  27.3 1.6 %collective-permute-start.4 = (bf16[64,2944]{1,0:T(8,128)(2,1)S(1)}, bf16[64,2944]{1,0:T(8,128)(2,1)S(1)}, u32[]{:S(2)}, u32[]{:S(2)}) collective-permute-start(bf16[64,2944]{1,0:T(8,128)(2,1)S(1)} %constant_dynamic-update-slice_fusion.after_ref.refs_0_), channel_id=1, source_target_pairs={{0,4},{1,5},{2,3},{3,2},{4,0},{5,1},{6,7},{7,6},{8,12},{9,13},{10,... | collective-permute-start | bytes 1130504 | tf_op jit(solution)/shard_map/ppermute | solution.py:599
  28.9 3.4 %copy-done = bf16[1,2880,1440]{1,2,0:T(8,128)(2,1)S(1)} copy-done((bf16[1,2880,1440]{1,2,0:T(8,128)(2,1)S(1)}, bf16[1,2880,1440]{1,2,0:T(8,128)(2,1)}, u32[]{:S(2)}) %copy-start) | copy-done | bytes 8294424
  32.3 1.4 %load.4 = (bf16[1440,2880]{1,0:T(8,128)(2,1)S(1)}, bf16[16,128]{1,0:T(8,128)(2,1)S(1)}) custom-call(bf16[64,2944]{1,0:T(8,128)(2,1)S(1)} %constant_dynamic-update-slice_fusion.after_ref.refs_0_, bf16[1440,2880]{1,0:T(8,128)(2,1)S(1)} %bitcast.13), custom_call_target="tpu_custom_call" | custom-call | bytes 16588800 | tf_op jit(solution)/shard_map/load/pallas_call | solution.py:289
  33.7 1.6 %collective-permute-start.5 = (bf16[64,2944]{1,0:T(8,128)(2,1)S(1)}, bf16[64,2944]{1,0:T(8,128)(2,1)S(1)}, u32[]{:S(2)}, u32[]{:S(2)}) collective-permute-start(bf16[64,2944]{1,0:T(8,128)(2,1)S(1)} %constant_dynamic-update-slice_fusion.after_ref.refs_0_), channel_id=1, source_target_pairs={{0,1},{1,0},{2,6},{3,7},{4,5},{5,4},{6,2},{7,3},{8,9},{9,8},{10,14... | collective-permute-start | bytes 1130504 | tf_op jit(solution)/shard_map/ppermute | solution.py:599
  35.3 2.0 %collective-permute-start.6 = (bf16[64,2944]{1,0:T(8,128)(2,1)S(1)}, bf16[64,2944]{1,0:T(8,128)(2,1)S(1)}, u32[]{:S(2)}, u32[]{:S(2)}) collective-permute-start(bf16[64,2944]{1,0:T(8,128)(2,1)S(1)} %collective-permute-done.4.refs_1_), channel_id=1, source_target_pairs={{0,1},{1,0},{2,6},{3,7},{4,5},{5,4},{6,2},{7,3},{8,9},{9,8},{10,14... | collective-permute-start | bytes 1130504 | tf_op jit(solution)/shard_map/ppermute | solution.py:599
  37.2 3.4 %copy-done.1 = bf16[1,1440,2880]{2,1,0:T(8,128)(2,1)S(1)} copy-done((bf16[1,1440,2880]{2,1,0:T(8,128)(2,1)S(1)}, bf16[1,1440,2880]{2,1,0:T(8,128)(2,1)}, u32[]{:S(2)}) %copy-start.1) | copy-done | bytes 8294424
  40.6 1.4 %load.5 = (bf16[1440,2880]{1,0:T(8,128)(2,1)S(1)}, bf16[16,128]{1,0:T(8,128)(2,1)S(1)}) custom-call(bf16[64,2944]{1,0:T(8,128)(2,1)S(1)} %constant_dynamic-update-slice_fusion.after_ref.refs_0_, bf16[1440,2880]{1,0:T(8,128)(2,1)S(1)} %bitcast.14), custom_call_target="tpu_custom_call" | custom-call | bytes 16588800 | tf_op jit(solution)/shard_map/load/pallas_call | solution.py:289
  42.0 0.6 collective-permute-start.8
  42.7 2.7 %collective-permute-done.6.refs_3_ = bf16[64,2944]{1,0:T(8,128)(2,1)S(1)} collective-permute-done((bf16[64,2944]{1,0:T(8,128)(2,1)S(1)}, bf16[64,2944]{1,0:T(8,128)(2,1)S(1)}, u32[]{:S(2)}, u32[]{:S(2)}) %collective-permute-start.6) | collective-permute-done | bytes 376864 | tf_op jit(solution)/shard_map/ppermute | solution.py:599
  45.4 1.7 %collective-permute-done.10.refs_7_ = bf16[64,2944]{1,0:T(8,128)(2,1)S(1)} collective-permute-done((bf16[64,2944]{1,0:T(8,128)(2,1)S(1)}, bf16[64,2944]{1,0:T(8,128)(2,1)S(1)}, u32[]{:S(2)}, u32[]{:S(2)}) %collective-permute-start.10) | collective-permute-done | bytes 376864 | tf_op jit(solution)/shard_map/ppermute | solution.py:588
  47.1 9.8 %expert.1 = (bf16[64,2880]{1,0:T(8,128)(2,1)S(1)}, bf16[64,2880]{1,0:T(8,128)(2,1)S(1)}, bf16[64,2880]{1,0:T(8,128)(2,1)S(1)}, bf16[64,2880]{1,0:T(8,128)(2,1)S(...) custom-call(s32[1]{0:T(128)} %get-tuple-element.31.expert_ref, ...), custom_call_target="tpu_custom_call" | custom-call | flops 6370099200 | bytes 24883200 | tf_op jit(solution)/shard_map/expert/pallas_call | solution.py:558
  57.9 0.7 collective-permute-done.12
  58.7 1.6 %collective-permute-start.13 = (bf16[64,2880]{1,0:T(8,128)(2,1)S(1)}, bf16[64,2880]{1,0:T(8,128)(2,1)S(1)}, u32[]{:S(2)}, u32[]{:S(2)}) collective-permute-start(bf16[64,2880]{1,0:T(8,128)(2,1)S(1)} %add_convert_fusion.4), channel_id=1, source_target_pairs={{0,1},{1,0},{2,6},{3,7},{4,5},{5,4},{6,2},{7,3},{8,9},{9,8},{10,14... | collective-permute-start | bytes 1105928 | tf_op jit(solution)/shard_map/ppermute | solution.py:599
  60.4 1.5 %collective-permute-start.19 = (bf16[64,2880]{1,0:T(8,128)(2,1)S(1)}, bf16[64,2880]{1,0:T(8,128)(2,1)S(1)}, u32[]{:S(2)}, u32[]{:S(2)}) collective-permute-start(bf16[64,2880]{1,0:T(8,128)(2,1)S(1)} %add_convert_fusion.1), channel_id=1, source_target_pairs={{0,1},{1,0},{2,6},{3,7},{4,5},{5,4},{6,2},{7,3},{8,9},{9,8},{10,14... | collective-permute-start | bytes 1105928 | tf_op jit(solution)/shard_map/ppermute | solution.py:599
  61.9 4.5 %collective-permute-done.13 = bf16[64,2880]{1,0:T(8,128)(2,1)S(1)} collective-permute-done((bf16[64,2880]{1,0:T(8,128)(2,1)S(1)}, bf16[64,2880]{1,0:T(8,128)(2,1)S(1)}, u32[]{:S(2)}, u32[]{:S(2)}) %collective-permute-start.13) | collective-permute-done | bytes 368672 | tf_op jit(solution)/shard_map/ppermute | solution.py:599
  66.5 0.6 collective-permute-start.14
  67.1 5.1 %collective-permute-done.19 = bf16[64,2880]{1,0:T(8,128)(2,1)S(1)} collective-permute-done((bf16[64,2880]{1,0:T(8,128)(2,1)S(1)}, bf16[64,2880]{1,0:T(8,128)(2,1)S(1)}, u32[]{:S(2)}, u32[]{:S(2)}) %collective-permute-start.19) | collective-permute-done | bytes 368672 | tf_op jit(solution)/shard_map/ppermute | solution.py:599
  72.4 0.6 collective-permute-start.20
  73.6 3.5 %collective-permute-start.16 = (bf16[16,2880]{1,0:T(8,128)(2,1)S(1)}, bf16[16,2880]{1,0:T(8,128)(2,1)S(1)}, u32[]{:S(2)}, u32[]{:S(2)}) collective-permute-start(bf16[16,2880]{1,0:T(8,128)(2,1)S(1)} %get-tuple-element.55), channel_id=1, source_target_pairs={{0,24},{1,25},{2,26},{3,27},{4,28},{5,29},{6,30},{7,31},{8,16},{9,... | collective-permute-start | bytes 276488 | tf_op jit(solution)/shard_map/ppermute | solution.py:588
  77.1 1.0 %collective-permute-done.20 = bf16[32,2880]{1,0:T(8,128)(2,1)S(1)} collective-permute-done((bf16[32,2880]{1,0:T(8,128)(2,1)S(1)}, bf16[32,2880]{1,0:T(8,128)(2,1)S(1)}, u32[]{:S(2)}, u32[]{:S(2)}) %collective-permute-start.20) | collective-permute-done | bytes 184352 | tf_op jit(solution)/shard_map/ppermute | solution.py:599
  78.7 3.9 %collective-permute-done.15 = bf16[16,2880]{1,0:T(8,128)(2,1)S(1)} collective-permute-done((bf16[16,2880]{1,0:T(8,128)(2,1)S(1)}, bf16[16,2880]{1,0:T(8,128)(2,1)S(1)}, u32[]{:S(2)}, u32[]{:S(2)}) %collective-permute-start.15) | collective-permute-done | bytes 92192 | tf_op jit(solution)/shard_map/ppermute | solution.py:588
  82.6 0.6 collective-permute-done.21
  83.2 0.7 add_convert_fusion.8
  (57 shorter events, 3.4 us)
Async XLA Ops:
  0.6 11.4 %copy-start.9 = (bf16[2880]{0:T(1024)(128)(2,1)S(1)}, bf16[2880]{0:T(1024)(128)(2,1)}, u32[]{:S(2)}) copy-start(bf16[2880]{0:T(1024)(128)(2,1)} %param.23) | copy-start | bytes 17284
  0.6 11.4 %copy-start.10 = (bf16[2880]{0:T(1024)(128)(2,1)S(1)}, bf16[2880]{0:T(1024)(128)(2,1)}, u32[]{:S(2)}) copy-start(bf16[2880]{0:T(1024)(128)(2,1)} %param.25) | copy-start | bytes 17284
  0.7 14.3 %copy-start.4 = (bf16[16,2880]{1,0:T(8,128)(2,1)S(1)}, bf16[16,2880]{1,0:T(8,128)(2,1)}, u32[]{:S(2)}) copy-start(bf16[16,2880]{1,0:T(8,128)(2,1)} %down_bias_ref.1) | copy-start | bytes 276484
  0.7 14.3 %copy-start.8 = (f32[16,4]{0,1:T(4,128)S(1)}, f32[16,4]{0,1:T(4,128)}, u32[]{:S(2)}) copy-start(f32[16,4]{0,1:T(4,128)} %param.27) | copy-start | bytes 772
  0.7 14.3 %copy-start.7 = (s32[16,4]{0,1:T(4,128)S(1)}, s32[16,4]{0,1:T(4,128)}, u32[]{:S(2)}) copy-start(s32[16,4]{0,1:T(4,128)} %param.26) | copy-start | bytes 772
  0.7 14.3 %copy-start.3 = (bf16[16,2880]{1,0:T(8,128)(2,1)S(1)}, bf16[16,2880]{1,0:T(8,128)(2,1)}, u32[]{:S(2)}) copy-start(bf16[16,2880]{1,0:T(8,128)(2,1)} %residual_ref.1) | copy-start | bytes 276484
  9.0 6.0 %collective-permute-start = (bf16[16,2880]{1,0:T(8,128)(2,1)}, bf16[16,2880]{1,0:T(8,128)(2,1)S(1)}, u32[]{:S(2)}, u32[]{:S(2)}) collective-permute-start(bf16[16,2880]{1,0:T(8,128)(2,1)} %get-tuple-element.29), channel_id=1, source_target_pairs={{0,1},{1,0},{2,3},{3,2},{4,5},{5,4},{6,7},{7,6},{8,9},{9,8},{10,11... | collective-permute-start | bytes 276488 | tf_op jit(solution)/shard_map/ppermute | solution.py:588
  16.4 11.0 %collective-permute-start.3 = (bf16[16,2944]{1,0:T(8,128)(2,1)S(1)}, bf16[16,2944]{1,0:T(8,128)(2,1)S(1)}, u32[]{:S(2)}, u32[]{:S(2)}) collective-permute-start(bf16[16,2944]{1,0:T(8,128)(2,1)S(1)} %get-tuple-element.32.after_ref), channel_id=1, source_target_pairs={{0,24},{1,25},{2,26},{3,27},{4,28},{5,29},{6,30},{7,31},{8,16},{9,... | collective-permute-start | bytes 282632 | tf_op jit(solution)/shard_map/ppermute | solution.py:588
  20.4 6.9 %collective-permute-start.2 = (bf16[16,2944]{1,0:T(8,128)(2,1)S(1)}, bf16[16,2944]{1,0:T(8,128)(2,1)S(1)}, u32[]{:S(2)}, u32[]{:S(2)}) collective-permute-start(bf16[16,2944]{1,0:T(8,128)(2,1)S(1)} %get-tuple-element.32.after_ref), channel_id=1, source_target_pairs={{0,16},{1,17},{2,18},{3,19},{4,20},{5,21},{6,22},{7,23},{8,24},{9,... | collective-permute-start | bytes 282632 | tf_op jit(solution)/shard_map/ppermute | solution.py:588
  20.4 4.9 %collective-permute-start.1 = (bf16[16,2944]{1,0:T(8,128)(2,1)S(1)}, bf16[16,2944]{1,0:T(8,128)(2,1)S(1)}, u32[]{:S(2)}, u32[]{:S(2)}) collective-permute-start(bf16[16,2944]{1,0:T(8,128)(2,1)S(1)} %get-tuple-element.32.after_ref), channel_id=1, source_target_pairs={{0,8},{1,9},{2,10},{3,11},{4,12},{5,13},{6,14},{7,15},{8,0},{9,1},... | collective-permute-start | bytes 282632 | tf_op jit(solution)/shard_map/ppermute | solution.py:588
  27.3 7.9 %collective-permute-start.4 = (bf16[64,2944]{1,0:T(8,128)(2,1)S(1)}, bf16[64,2944]{1,0:T(8,128)(2,1)S(1)}, u32[]{:S(2)}, u32[]{:S(2)}) collective-permute-start(bf16[64,2944]{1,0:T(8,128)(2,1)S(1)} %constant_dynamic-update-slice_fusion.after_ref.refs_0_), channel_id=1, source_target_pairs={{0,4},{1,5},{2,3},{3,2},{4,0},{5,1},{6,7},{7,6},{8,12},{9,13},{10,... | collective-permute-start | bytes 1130504 | tf_op jit(solution)/shard_map/ppermute | solution.py:599
  28.9 3.4 %copy-start = (bf16[1,2880,1440]{1,2,0:T(8,128)(2,1)S(1)}, bf16[1,2880,1440]{1,2,0:T(8,128)(2,1)}, u32[]{:S(2)}) copy-start(bf16[1,2880,1440]{1,2,0:T(8,128)(2,1)} %param.30) | copy-start | bytes 24883204
  32.3 14.8 %copy-start.5 = (bf16[1,1440]{1,0:T(2,128)(2,1)S(1)}, bf16[1,1440]{1,0:T(2,128)(2,1)}, u32[]{:S(2)}) copy-start(bf16[1,1440]{1,0:T(2,128)(2,1)} %refs_11_.1) | copy-start | bytes 8644
  32.3 14.8 %copy-start.6 = (bf16[1,1440]{1,0:T(2,128)(2,1)S(1)}, bf16[1,1440]{1,0:T(2,128)(2,1)}, u32[]{:S(2)}) copy-start(bf16[1,1440]{1,0:T(2,128)(2,1)} %refs_12_.1) | copy-start | bytes 8644
  33.7 8.9 %collective-permute-start.5 = (bf16[64,2944]{1,0:T(8,128)(2,1)S(1)}, bf16[64,2944]{1,0:T(8,128)(2,1)S(1)}, u32[]{:S(2)}, u32[]{:S(2)}) collective-permute-start(bf16[64,2944]{1,0:T(8,128)(2,1)S(1)} %constant_dynamic-update-slice_fusion.after_ref.refs_0_), channel_id=1, source_target_pairs={{0,1},{1,0},{2,6},{3,7},{4,5},{5,4},{6,2},{7,3},{8,9},{9,8},{10,14... | collective-permute-start | bytes 1130504 | tf_op jit(solution)/shard_map/ppermute | solution.py:599
  35.3 10.1 %collective-permute-start.6 = (bf16[64,2944]{1,0:T(8,128)(2,1)S(1)}, bf16[64,2944]{1,0:T(8,128)(2,1)S(1)}, u32[]{:S(2)}, u32[]{:S(2)}) collective-permute-start(bf16[64,2944]{1,0:T(8,128)(2,1)S(1)} %collective-permute-done.4.refs_1_), channel_id=1, source_target_pairs={{0,1},{1,0},{2,6},{3,7},{4,5},{5,4},{6,2},{7,3},{8,9},{9,8},{10,14... | collective-permute-start | bytes 1130504 | tf_op jit(solution)/shard_map/ppermute | solution.py:599
  37.2 8.2 %collective-permute-start.7 = (bf16[64,2944]{1,0:T(8,128)(2,1)S(1)}, bf16[64,2944]{1,0:T(8,128)(2,1)S(1)}, u32[]{:S(2)}, u32[]{:S(2)}) collective-permute-start(bf16[64,2944]{1,0:T(8,128)(2,1)S(1)} %constant_dynamic-update-slice_fusion.after_ref.refs_0_), channel_id=1, source_target_pairs={{0,2},{1,3},{2,0},{3,1},{4,6},{5,7},{6,4},{7,5},{8,10},{9,11},{10,... | collective-permute-start | bytes 1130504 | tf_op jit(solution)/shard_map/ppermute | solution.py:588
  37.2 3.4 %copy-start.1 = (bf16[1,1440,2880]{2,1,0:T(8,128)(2,1)S(1)}, bf16[1,1440,2880]{2,1,0:T(8,128)(2,1)}, u32[]{:S(2)}) copy-start(bf16[1,1440,2880]{2,1,0:T(8,128)(2,1)} %param.32) | copy-start | bytes 24883204
  42.0 3.4 %collective-permute-start.8 = (bf16[64,2944]{1,0:T(8,128)(2,1)S(1)}, bf16[64,2944]{1,0:T(8,128)(2,1)S(1)}, u32[]{:S(2)}, u32[]{:S(2)}) collective-permute-start(bf16[64,2944]{1,0:T(8,128)(2,1)S(1)} %collective-permute-done.4.refs_1_), channel_id=1, source_target_pairs={{0,2},{1,3},{2,0},{3,1},{4,6},{5,7},{6,4},{7,5},{8,10},{9,11},{10,... | collective-permute-start | bytes 1130504 | tf_op jit(solution)/shard_map/ppermute | solution.py:588
  42.6 2.8 %collective-permute-start.9 = (bf16[64,2944]{1,0:T(8,128)(2,1)S(1)}, bf16[64,2944]{1,0:T(8,128)(2,1)S(1)}, u32[]{:S(2)}, u32[]{:S(2)}) collective-permute-start(bf16[64,2944]{1,0:T(8,128)(2,1)S(1)} %collective-permute-done.5.refs_2_), channel_id=1, source_target_pairs={{0,2},{1,3},{2,0},{3,1},{4,6},{5,7},{6,4},{7,5},{8,10},{9,11},{10,... | collective-permute-start | bytes 1130504 | tf_op jit(solution)/shard_map/ppermute | solution.py:588
  45.4 1.7 %collective-permute-start.10 = (bf16[64,2944]{1,0:T(8,128)(2,1)S(1)}, bf16[64,2944]{1,0:T(8,128)(2,1)S(1)}, u32[]{:S(2)}, u32[]{:S(2)}) collective-permute-start(bf16[64,2944]{1,0:T(8,128)(2,1)S(1)} %collective-permute-done.6.refs_3_), channel_id=1, source_target_pairs={{0,2},{1,3},{2,0},{3,1},{4,6},{5,7},{6,4},{7,5},{8,10},{9,11},{10,... | collective-permute-start | bytes 1130504 | tf_op jit(solution)/shard_map/ppermute | solution.py:588
  56.9 1.8 %collective-permute-start.12 = (bf16[64,2880]{1,0:T(8,128)(2,1)S(1)}, bf16[64,2880]{1,0:T(8,128)(2,1)S(1)}, u32[]{:S(2)}, u32[]{:S(2)}) collective-permute-start(bf16[64,2880]{1,0:T(8,128)(2,1)S(1)} %get-tuple-element.48), channel_id=1, source_target_pairs={{0,2},{1,3},{2,0},{3,1},{4,6},{5,7},{6,4},{7,5},{8,10},{9,11},{10,... | collective-permute-start | bytes 1105928 | tf_op jit(solution)/shard_map/ppermute | solution.py:588
  57.1 4.9 %collective-permute-start.11 = (bf16[64,2880]{1,0:T(8,128)(2,1)S(1)}, bf16[64,2880]{1,0:T(8,128)(2,1)S(1)}, u32[]{:S(2)}, u32[]{:S(2)}) collective-permute-start(bf16[64,2880]{1,0:T(8,128)(2,1)S(1)} %get-tuple-element.46), channel_id=1, source_target_pairs={{0,2},{1,3},{2,0},{3,1},{4,6},{5,7},{6,4},{7,5},{8,10},{9,11},{10,... | collective-permute-start | bytes 1105928 | tf_op jit(solution)/shard_map/ppermute | solution.py:588
  57.4 9.7 %collective-permute-start.17 = (bf16[64,2880]{1,0:T(8,128)(2,1)S(1)}, bf16[64,2880]{1,0:T(8,128)(2,1)S(1)}, u32[]{:S(2)}, u32[]{:S(2)}) collective-permute-start(bf16[64,2880]{1,0:T(8,128)(2,1)S(1)} %get-tuple-element.50), channel_id=1, source_target_pairs={{0,2},{1,3},{2,0},{3,1},{4,6},{5,7},{6,4},{7,5},{8,10},{9,11},{10,... | collective-permute-start | bytes 1105928 | tf_op jit(solution)/shard_map/ppermute | solution.py:588
  57.6 2.7 %collective-permute-start.18 = (bf16[64,2880]{1,0:T(8,128)(2,1)S(1)}, bf16[64,2880]{1,0:T(8,128)(2,1)S(1)}, u32[]{:S(2)}, u32[]{:S(2)}) collective-permute-start(bf16[64,2880]{1,0:T(8,128)(2,1)S(1)} %get-tuple-element.52), channel_id=1, source_target_pairs={{0,2},{1,3},{2,0},{3,1},{4,6},{5,7},{6,4},{7,5},{8,10},{9,11},{10,... | collective-permute-start | bytes 1105928 | tf_op jit(solution)/shard_map/ppermute | solution.py:588
  58.7 7.7 %collective-permute-start.13 = (bf16[64,2880]{1,0:T(8,128)(2,1)S(1)}, bf16[64,2880]{1,0:T(8,128)(2,1)S(1)}, u32[]{:S(2)}, u32[]{:S(2)}) collective-permute-start(bf16[64,2880]{1,0:T(8,128)(2,1)S(1)} %add_convert_fusion.4), channel_id=1, source_target_pairs={{0,1},{1,0},{2,6},{3,7},{4,5},{5,4},{6,2},{7,3},{8,9},{9,8},{10,14... | collective-permute-start | bytes 1105928 | tf_op jit(solution)/shard_map/ppermute | solution.py:599
  60.4 11.9 %collective-permute-start.19 = (bf16[64,2880]{1,0:T(8,128)(2,1)S(1)}, bf16[64,2880]{1,0:T(8,128)(2,1)S(1)}, u32[]{:S(2)}, u32[]{:S(2)}) collective-permute-start(bf16[64,2880]{1,0:T(8,128)(2,1)S(1)} %add_convert_fusion.1), channel_id=1, source_target_pairs={{0,1},{1,0},{2,6},{3,7},{4,5},{5,4},{6,2},{7,3},{8,9},{9,8},{10,14... | collective-permute-start | bytes 1105928 | tf_op jit(solution)/shard_map/ppermute | solution.py:599
  66.5 6.5 %collective-permute-start.14 = (bf16[32,2880]{1,0:T(8,128)(2,1)S(1)}, bf16[32,2880]{1,0:T(8,128)(2,1)S(1)}, u32[]{:S(2)}, u32[]{:S(2)}) collective-permute-start(bf16[32,2880]{1,0:T(8,128)(2,1)S(1)} %slice.33), channel_id=1, source_target_pairs={{0,4},{1,5},{2,3},{3,2},{4,0},{5,1},{6,7},{7,6},{8,12},{9,13},{10,... | collective-permute-start | bytes 552968 | tf_op jit(solution)/shard_map/ppermute | solution.py:599
  72.4 5.6 %collective-permute-start.20 = (bf16[32,2880]{1,0:T(8,128)(2,1)S(1)}, bf16[32,2880]{1,0:T(8,128)(2,1)S(1)}, u32[]{:S(2)}, u32[]{:S(2)}) collective-permute-start(bf16[32,2880]{1,0:T(8,128)(2,1)S(1)} %slice.37), channel_id=1, source_target_pairs={{0,4},{1,5},{2,3},{3,2},{4,0},{5,1},{6,7},{7,6},{8,12},{9,13},{10,... | collective-permute-start | bytes 552968 | tf_op jit(solution)/shard_map/ppermute | solution.py:599
  73.1 9.4 %collective-permute-start.15 = (bf16[16,2880]{1,0:T(8,128)(2,1)S(1)}, bf16[16,2880]{1,0:T(8,128)(2,1)S(1)}, u32[]{:S(2)}, u32[]{:S(2)}) collective-permute-start(bf16[16,2880]{1,0:T(8,128)(2,1)S(1)} %get-tuple-element.54), channel_id=1, source_target_pairs={{0,16},{1,17},{2,18},{3,19},{4,20},{5,21},{6,22},{7,23},{8,24},{9,... | collective-permute-start | bytes 276488 | tf_op jit(solution)/shard_map/ppermute | solution.py:588
  73.6 8.9 %collective-permute-start.16 = (bf16[16,2880]{1,0:T(8,128)(2,1)S(1)}, bf16[16,2880]{1,0:T(8,128)(2,1)S(1)}, u32[]{:S(2)}, u32[]{:S(2)}) collective-permute-start(bf16[16,2880]{1,0:T(8,128)(2,1)S(1)} %get-tuple-element.55), channel_id=1, source_target_pairs={{0,24},{1,25},{2,26},{3,27},{4,28},{5,29},{6,30},{7,31},{8,16},{9,... | collective-permute-start | bytes 276488 | tf_op jit(solution)/shard_map/ppermute | solution.py:588
  78.2 5.0 %collective-permute-start.21 = (bf16[16,2880]{1,0:T(8,128)(2,1)S(1)}, bf16[16,2880]{1,0:T(8,128)(2,1)S(1)}, u32[]{:S(2)}, u32[]{:S(2)}) collective-permute-start(bf16[16,2880]{1,0:T(8,128)(2,1)S(1)} %slice.39), channel_id=1, source_target_pairs={{0,8},{1,9},{2,10},{3,11},{4,12},{5,13},{6,14},{7,15},{8,0},{9,1},... | collective-permute-start | bytes 276488 | tf_op jit(solution)/shard_map/ppermute | solution.py:588
  (1 other events, 0.9 us)

commit v7 on v6

--- a/solution.py
+++ b/solution.py
@@ -212,8 +212,6 @@
 def mid_kernel(
     own_ref,
     got_ref,
-    residual_ref,
-    out_bias_ref,
     gain_ref,
     ids_ref,
     logits_ref,
@@ -221,14 +219,9 @@
     base_ref,
     rows_ref,
 ):
-    width = residual_ref.shape[1]
+    width = own_ref.shape[1]
     experts = down_bias_ref.shape[0]
-    hidden = (
-        residual_ref[...].astype(jnp.float32)
-        + own_ref[...].astype(jnp.float32)
-        + got_ref[...].astype(jnp.float32)
-        + out_bias_ref[...].astype(jnp.float32)
-    ).astype(jnp.bfloat16)
+    hidden = (own_ref[...] + got_ref[...].astype(jnp.float32)).astype(jnp.bfloat16)
     stream = hidden.astype(jnp.float32)
     normed = (
         stream
@@ -679,15 +672,13 @@
             jax.ShapeDtypeStruct((tok_count, width), jnp.float32),
             jax.ShapeDtypeStruct((tok_count, width + 4 * experts), jnp.bfloat16),
         ],
-        in_specs=[vmem()] * 8,
+        in_specs=[vmem()] * 6,
         out_specs=[vmem()] * 2,
         compiler_params=pltpu.CompilerParams(vmem_limit_bytes=4 * 2**20),
         name="norm_rows",
     )(
-        own,
+        own + residual.astype(jnp.float32) + out_bias.astype(jnp.float32),
         got,
-        residual,
-        out_bias[None],
         norm_gain[None],
         route_ids.T,
         route_logits.T,

time: 84.1 us -> 83.3 us (level)
  other arithmetic: 1.25 us -> 2.2 us
  local copies, waits for them, and re-layouts: 7.88 us -> 6.96 us
  waiting for transfers between devices: 25.8 us -> 24.9 us
    ppermute x15, waiting for transfers between devices: 12.5 us -> 11.5 us  [moved(): return lax.ppermute(array, AXES, pairs)]
    add x0 -> x1, other arithmetic: none -> 0.95 us  [gathered_body(): own + residual.astype(jnp.float32) + out_bias.astype(jnp.float32)]
    unnamed x25 -> x23, local copies, waits for them, and re-layouts: 7.8 us -> 6.88 us
  transfers between devices with their start and end apart: 22 -> 22, of which waited for: 11 -> 11; matrix products, arithmetic and copies ran while one was open for 1% -> 2% of each run, Pallas kernels for 7% -> 7%
where the time goes in v7:
time: 83.3 us; the launch traced here: 83 us
  waiting for transfers between devices  24.9 us (30%)
  Pallas kernels  24.8 us (30%)
  starting transfers between devices  23.3 us (28%)
  local copies, waits for them, and re-layouts  6.96 us (8%)
  other arithmetic  2.2 us (3%)
  between operations  0.86 us (1%)
    ppermute x15, starting transfers between devices, moved(): return lax.ppermute(array, AXES, pairs)  13.9 us
    ppermute x7, waiting for transfers between devices, crossed(): return lax.ppermute(array, AXES, pairs)  13.3 us
    ppermute x15, waiting for transfers between devices, moved(): return lax.ppermute(array, AXES, pairs)  11.5 us
    pallas_call x1, Pallas kernels, run_expert(): pl.pallas_call(functools.partial(expert_kernel, parts, block, limit, 512)...  9.82 us
    ppermute x7, starting transfers between devices, crossed(): return lax.ppermute(array, AXES, pairs)  9.39 us
    pallas_call x1, Pallas kernels, run_attention(): pl.pallas_call(attention_kernel, out_shape=[jax.ShapeDtypeStruct((half, w...  8.32 us
    unnamed x23, local copies, waits for them, and re-layouts  6.88 us
    pallas_call x3, Pallas kernels, load(): pl.pallas_call(load_kernel, out_shape=[jax.ShapeDtypeStruct(weight.shape,...  6.22 us
  transfers between devices with their start and end apart: 22, of which 11 were waited for; matrix products, arithmetic and copies ran while one was open for 2% of the time, Pallas kernels for 7%

profile of v7, /device:TPU:0, one launch (start us, length us, event | category | flops | bytes accessed | tf_op | source)
XLA Modules:
  0.0 83.0 jit_solution(10396738684467992357)
XLA Ops:
  0.7 8.3 %attention.1 = (f32[16,2880]{1,0:T(8,128)}, bf16[16,2880]{1,0:T(8,128)(2,1)}, bf16[2,16,512]{2,1,0:T(8,128)(2,1)}, s32[1]{0:T(128)}) custom-call(s32[1]{0:T(128)} %bitcast.side_ref, s32[1]{0:T(128)} %bitcast.1.expert_in_ref, s32[1,2]{1,0:T(1,128)} %pages_ref.1, f32[32]{0:T(128)} %sink_ref.1, bf16[32,2048]{1,0:T(8,128)(2,1)} %queries_ref.1, ...), custom_call_target="tpu_custom_call" | custom-call | tf_op jit(solution)/shard_map/attention/pallas_call | solution.py:504
  9.0 3.0 %collective-permute-start = (bf16[16,2880]{1,0:T(8,128)(2,1)}, bf16[16,2880]{1,0:T(8,128)(2,1)S(1)}, u32[]{:S(2)}, u32[]{:S(2)}) collective-permute-start(bf16[16,2880]{1,0:T(8,128)(2,1)} %get-tuple-element.29), channel_id=1, source_target_pairs={{0,1},{1,0},{2,3},{3,2},{4,5},{5,4},{6,7},{7,6},{8,9},{9,8},{10,11... | collective-permute-start | bytes 276488 | tf_op jit(solution)/shard_map/ppermute | solution.py:581
  12.1 1.0 %add_add_fusion.own_ref = f32[16,2880]{1,0:T(8,128)S(1)} fusion(f32[16,2880]{1,0:T(8,128)} %get-tuple-element.28, bf16[16,2880]{1,0:T(8,128)(2,1)S(1)} %copy-done.7, f32[2880]{0:T(1024)S(1)} %convert_element_type.94), kind=kLoop, calls=%fused_computation.9 | loop fusion | flops 138240 | bytes 472320 | tf_op jit(solution)/shard_map/add | solution.py:680
  13.1 1.9 %collective-permute-done.got_ref = bf16[16,2880]{1,0:T(8,128)(2,1)S(1)} collective-permute-done((bf16[16,2880]{1,0:T(8,128)(2,1)}, bf16[16,2880]{1,0:T(8,128)(2,1)S(1)}, u32[]{:S(2)}, u32[]{:S(2)}) %collective-permute-start) | collective-permute-done | bytes 92192 | tf_op jit(solution)/shard_map/ppermute | solution.py:581
  15.4 4.0 %collective-permute-start.3 = (bf16[16,2944]{1,0:T(8,128)(2,1)S(1)}, bf16[16,2944]{1,0:T(8,128)(2,1)S(1)}, u32[]{:S(2)}, u32[]{:S(2)}) collective-permute-start(bf16[16,2944]{1,0:T(8,128)(2,1)S(1)} %get-tuple-element.32.after_ref), channel_id=1, source_target_pairs={{0,24},{1,25},{2,26},{3,27},{4,28},{5,29},{6,30},{7,31},{8,16},{9,... | collective-permute-start | bytes 282632 | tf_op jit(solution)/shard_map/ppermute | solution.py:581
  19.4 0.6 collective-permute-start.1
  20.1 3.5 %load.3 = (bf16[1440,2880]{1,0:T(8,128)(2,1)S(1)}, bf16[16,128]{1,0:T(8,128)(2,1)S(1)}) custom-call(bf16[16,2944]{1,0:T(8,128)(2,1)S(1)} %get-tuple-element.32.after_ref, bf16[1440,2880]{1,0:T(8,128)(2,1)} %bitcast.18), custom_call_target="tpu_custom_call" | custom-call | bytes 16588800 | tf_op jit(solution)/shard_map/load/pallas_call | solution.py:282
  23.6 0.7 collective-permute-done.1
  24.3 2.0 %collective-permute-done.2 = bf16[16,2944]{1,0:T(8,128)(2,1)S(1)} collective-permute-done((bf16[16,2944]{1,0:T(8,128)(2,1)S(1)}, bf16[16,2944]{1,0:T(8,128)(2,1)S(1)}, u32[]{:S(2)}, u32[]{:S(2)}) %collective-permute-start.2) | collective-permute-done | bytes 94240 | tf_op jit(solution)/shard_map/ppermute | solution.py:581
  26.4 1.6 %collective-permute-start.4 = (bf16[64,2944]{1,0:T(8,128)(2,1)S(1)}, bf16[64,2944]{1,0:T(8,128)(2,1)S(1)}, u32[]{:S(2)}, u32[]{:S(2)}) collective-permute-start(bf16[64,2944]{1,0:T(8,128)(2,1)S(1)} %constant_dynamic-update-slice_fusion.after_ref.refs_0_), channel_id=1, source_target_pairs={{0,4},{1,5},{2,3},{3,2},{4,0},{5,1},{6,7},{7,6},{8,12},{9,13},{10,... | collective-permute-start | bytes 1130504 | tf_op jit(solution)/shard_map/ppermute | solution.py:592
  28.0 3.4 %copy-done = bf16[1,2880,1440]{1,2,0:T(8,128)(2,1)S(1)} copy-done((bf16[1,2880,1440]{1,2,0:T(8,128)(2,1)S(1)}, bf16[1,2880,1440]{1,2,0:T(8,128)(2,1)}, u32[]{:S(2)}) %copy-start) | copy-done | bytes 8294424
  31.4 1.4 %load.4 = (bf16[1440,2880]{1,0:T(8,128)(2,1)S(1)}, bf16[16,128]{1,0:T(8,128)(2,1)S(1)}) custom-call(bf16[64,2944]{1,0:T(8,128)(2,1)S(1)} %constant_dynamic-update-slice_fusion.after_ref.refs_0_, bf16[1440,2880]{1,0:T(8,128)(2,1)S(1)} %bitcast.13), custom_call_target="tpu_custom_call" | custom-call | bytes 16588800 | tf_op jit(solution)/shard_map/load/pallas_call | solution.py:282
  32.7 1.6 %collective-permute-start.5 = (bf16[64,2944]{1,0:T(8,128)(2,1)S(1)}, bf16[64,2944]{1,0:T(8,128)(2,1)S(1)}, u32[]{:S(2)}, u32[]{:S(2)}) collective-permute-start(bf16[64,2944]{1,0:T(8,128)(2,1)S(1)} %constant_dynamic-update-slice_fusion.after_ref.refs_0_), channel_id=1, source_target_pairs={{0,1},{1,0},{2,6},{3,7},{4,5},{5,4},{6,2},{7,3},{8,9},{9,8},{10,14... | collective-permute-start | bytes 1130504 | tf_op jit(solution)/shard_map/ppermute | solution.py:592
  34.3 1.9 %collective-permute-start.6 = (bf16[64,2944]{1,0:T(8,128)(2,1)S(1)}, bf16[64,2944]{1,0:T(8,128)(2,1)S(1)}, u32[]{:S(2)}, u32[]{:S(2)}) collective-permute-start(bf16[64,2944]{1,0:T(8,128)(2,1)S(1)} %collective-permute-done.4.refs_1_), channel_id=1, source_target_pairs={{0,1},{1,0},{2,6},{3,7},{4,5},{5,4},{6,2},{7,3},{8,9},{9,8},{10,14... | collective-permute-start | bytes 1130504 | tf_op jit(solution)/shard_map/ppermute | solution.py:592
  36.3 3.4 %copy-done.1 = bf16[1,1440,2880]{2,1,0:T(8,128)(2,1)S(1)} copy-done((bf16[1,1440,2880]{2,1,0:T(8,128)(2,1)S(1)}, bf16[1,1440,2880]{2,1,0:T(8,128)(2,1)}, u32[]{:S(2)}) %copy-start.1) | copy-done | bytes 8294424
  39.7 1.4 %load.5 = (bf16[1440,2880]{1,0:T(8,128)(2,1)S(1)}, bf16[16,128]{1,0:T(8,128)(2,1)S(1)}) custom-call(bf16[64,2944]{1,0:T(8,128)(2,1)S(1)} %constant_dynamic-update-slice_fusion.after_ref.refs_0_, bf16[1440,2880]{1,0:T(8,128)(2,1)S(1)} %bitcast.14), custom_call_target="tpu_custom_call" | custom-call | bytes 16588800 | tf_op jit(solution)/shard_map/load/pallas_call | solution.py:282
  41.0 0.6 collective-permute-start.8
  41.7 2.7 %collective-permute-done.6.refs_3_ = bf16[64,2944]{1,0:T(8,128)(2,1)S(1)} collective-permute-done((bf16[64,2944]{1,0:T(8,128)(2,1)S(1)}, bf16[64,2944]{1,0:T(8,128)(2,1)S(1)}, u32[]{:S(2)}, u32[]{:S(2)}) %collective-permute-start.6) | collective-permute-done | bytes 376864 | tf_op jit(solution)/shard_map/ppermute | solution.py:592
  44.5 1.7 %collective-permute-done.10.refs_7_ = bf16[64,2944]{1,0:T(8,128)(2,1)S(1)} collective-permute-done((bf16[64,2944]{1,0:T(8,128)(2,1)S(1)}, bf16[64,2944]{1,0:T(8,128)(2,1)S(1)}, u32[]{:S(2)}, u32[]{:S(2)}) %collective-permute-start.10) | collective-permute-done | bytes 376864 | tf_op jit(solution)/shard_map/ppermute | solution.py:581
  46.2 9.8 %expert.1 = (bf16[64,2880]{1,0:T(8,128)(2,1)S(1)}, bf16[64,2880]{1,0:T(8,128)(2,1)S(1)}, bf16[64,2880]{1,0:T(8,128)(2,1)S(1)}, bf16[64,2880]{1,0:T(8,128)(2,1)S(...) custom-call(s32[1]{0:T(128)} %get-tuple-element.31.expert_ref, ...), custom_call_target="tpu_custom_call" | custom-call | flops 6370099200 | bytes 24883200 | tf_op jit(solution)/shard_map/expert/pallas_call | solution.py:551
  57.1 0.7 collective-permute-done.12
  57.8 1.6 %collective-permute-start.13 = (bf16[64,2880]{1,0:T(8,128)(2,1)S(1)}, bf16[64,2880]{1,0:T(8,128)(2,1)S(1)}, u32[]{:S(2)}, u32[]{:S(2)}) collective-permute-start(bf16[64,2880]{1,0:T(8,128)(2,1)S(1)} %add_convert_fusion.4), channel_id=1, source_target_pairs={{0,1},{1,0},{2,6},{3,7},{4,5},{5,4},{6,2},{7,3},{8,9},{9,8},{10,14... | collective-permute-start | bytes 1105928 | tf_op jit(solution)/shard_map/ppermute | solution.py:592
  59.5 1.5 %collective-permute-start.19 = (bf16[64,2880]{1,0:T(8,128)(2,1)S(1)}, bf16[64,2880]{1,0:T(8,128)(2,1)S(1)}, u32[]{:S(2)}, u32[]{:S(2)}) collective-permute-start(bf16[64,2880]{1,0:T(8,128)(2,1)S(1)} %add_convert_fusion.1), channel_id=1, source_target_pairs={{0,1},{1,0},{2,6},{3,7},{4,5},{5,4},{6,2},{7,3},{8,9},{9,8},{10,14... | collective-permute-start | bytes 1105928 | tf_op jit(solution)/shard_map/ppermute | solution.py:592
  61.0 4.5 %collective-permute-done.13 = bf16[64,2880]{1,0:T(8,128)(2,1)S(1)} collective-permute-done((bf16[64,2880]{1,0:T(8,128)(2,1)S(1)}, bf16[64,2880]{1,0:T(8,128)(2,1)S(1)}, u32[]{:S(2)}, u32[]{:S(2)}) %collective-permute-start.13) | collective-permute-done | bytes 368672 | tf_op jit(solution)/shard_map/ppermute | solution.py:592
  65.7 0.6 collective-permute-start.14
  66.3 5.1 %collective-permute-done.19 = bf16[64,2880]{1,0:T(8,128)(2,1)S(1)} collective-permute-done((bf16[64,2880]{1,0:T(8,128)(2,1)S(1)}, bf16[64,2880]{1,0:T(8,128)(2,1)S(1)}, u32[]{:S(2)}, u32[]{:S(2)}) %collective-permute-start.19) | collective-permute-done | bytes 368672 | tf_op jit(solution)/shard_map/ppermute | solution.py:592
  71.6 0.6 collective-permute-start.20
  72.8 3.5 %collective-permute-start.16 = (bf16[16,2880]{1,0:T(8,128)(2,1)S(1)}, bf16[16,2880]{1,0:T(8,128)(2,1)S(1)}, u32[]{:S(2)}, u32[]{:S(2)}) collective-permute-start(bf16[16,2880]{1,0:T(8,128)(2,1)S(1)} %get-tuple-element.55), channel_id=1, source_target_pairs={{0,24},{1,25},{2,26},{3,27},{4,28},{5,29},{6,30},{7,31},{8,16},{9,... | collective-permute-start | bytes 276488 | tf_op jit(solution)/shard_map/ppermute | solution.py:581
  76.2 1.0 %collective-permute-done.20 = bf16[32,2880]{1,0:T(8,128)(2,1)S(1)} collective-permute-done((bf16[32,2880]{1,0:T(8,128)(2,1)S(1)}, bf16[32,2880]{1,0:T(8,128)(2,1)S(1)}, u32[]{:S(2)}, u32[]{:S(2)}) %collective-permute-start.20) | collective-permute-done | bytes 184352 | tf_op jit(solution)/shard_map/ppermute | solution.py:592
  77.8 3.9 %collective-permute-done.15 = bf16[16,2880]{1,0:T(8,128)(2,1)S(1)} collective-permute-done((bf16[16,2880]{1,0:T(8,128)(2,1)S(1)}, bf16[16,2880]{1,0:T(8,128)(2,1)S(1)}, u32[]{:S(2)}, u32[]{:S(2)}) %collective-permute-start.15) | collective-permute-done | bytes 92192 | tf_op jit(solution)/shard_map/ppermute | solution.py:581
  81.7 0.6 collective-permute-done.21
  82.3 0.7 add_convert_fusion.8
  (56 shorter events, 3.4 us)
Async XLA Ops:
  0.6 11.4 %copy-start.9 = (bf16[2880]{0:T(1024)(128)(2,1)S(1)}, bf16[2880]{0:T(1024)(128)(2,1)}, u32[]{:S(2)}) copy-start(bf16[2880]{0:T(1024)(128)(2,1)} %param.23) | copy-start | bytes 17284
  0.6 11.4 %copy-start.7 = (bf16[16,2880]{1,0:T(8,128)(2,1)S(1)}, bf16[16,2880]{1,0:T(8,128)(2,1)}, u32[]{:S(2)}) copy-start(bf16[16,2880]{1,0:T(8,128)(2,1)} %param.24) | copy-start | bytes 276484
  0.7 12.4 %copy-start.8 = (bf16[2880]{0:T(1024)(128)(2,1)S(1)}, bf16[2880]{0:T(1024)(128)(2,1)}, u32[]{:S(2)}) copy-start(bf16[2880]{0:T(1024)(128)(2,1)} %param.25) | copy-start | bytes 17284
  0.7 14.3 %copy-start.2 = (bf16[16,2880]{1,0:T(8,128)(2,1)S(1)}, bf16[16,2880]{1,0:T(8,128)(2,1)}, u32[]{:S(2)}) copy-start(bf16[16,2880]{1,0:T(8,128)(2,1)} %down_bias_ref.1) | copy-start | bytes 276484
  0.7 14.3 %copy-start.6 = (f32[16,4]{0,1:T(4,128)S(1)}, f32[16,4]{0,1:T(4,128)}, u32[]{:S(2)}) copy-start(f32[16,4]{0,1:T(4,128)} %param.27) | copy-start | bytes 772
  0.7 14.3 %copy-start.5 = (s32[16,4]{0,1:T(4,128)S(1)}, s32[16,4]{0,1:T(4,128)}, u32[]{:S(2)}) copy-start(s32[16,4]{0,1:T(4,128)} %param.26) | copy-start | bytes 772
  9.0 6.0 %collective-permute-start = (bf16[16,2880]{1,0:T(8,128)(2,1)}, bf16[16,2880]{1,0:T(8,128)(2,1)S(1)}, u32[]{:S(2)}, u32[]{:S(2)}) collective-permute-start(bf16[16,2880]{1,0:T(8,128)(2,1)} %get-tuple-element.29), channel_id=1, source_target_pairs={{0,1},{1,0},{2,3},{3,2},{4,5},{5,4},{6,7},{7,6},{8,9},{9,8},{10,11... | collective-permute-start | bytes 276488 | tf_op jit(solution)/shard_map/ppermute | solution.py:581
  15.4 11.0 %collective-permute-start.3 = (bf16[16,2944]{1,0:T(8,128)(2,1)S(1)}, bf16[16,2944]{1,0:T(8,128)(2,1)S(1)}, u32[]{:S(2)}, u32[]{:S(2)}) collective-permute-start(bf16[16,2944]{1,0:T(8,128)(2,1)S(1)} %get-tuple-element.32.after_ref), channel_id=1, source_target_pairs={{0,24},{1,25},{2,26},{3,27},{4,28},{5,29},{6,30},{7,31},{8,16},{9,... | collective-permute-start | bytes 282632 | tf_op jit(solution)/shard_map/ppermute | solution.py:581
  19.4 6.9 %collective-permute-start.2 = (bf16[16,2944]{1,0:T(8,128)(2,1)S(1)}, bf16[16,2944]{1,0:T(8,128)(2,1)S(1)}, u32[]{:S(2)}, u32[]{:S(2)}) collective-permute-start(bf16[16,2944]{1,0:T(8,128)(2,1)S(1)} %get-tuple-element.32.after_ref), channel_id=1, source_target_pairs={{0,16},{1,17},{2,18},{3,19},{4,20},{5,21},{6,22},{7,23},{8,24},{9,... | collective-permute-start | bytes 282632 | tf_op jit(solution)/shard_map/ppermute | solution.py:581
  19.4 4.9 %collective-permute-start.1 = (bf16[16,2944]{1,0:T(8,128)(2,1)S(1)}, bf16[16,2944]{1,0:T(8,128)(2,1)S(1)}, u32[]{:S(2)}, u32[]{:S(2)}) collective-permute-start(bf16[16,2944]{1,0:T(8,128)(2,1)S(1)} %get-tuple-element.32.after_ref), channel_id=1, source_target_pairs={{0,8},{1,9},{2,10},{3,11},{4,12},{5,13},{6,14},{7,15},{8,0},{9,1},... | collective-permute-start | bytes 282632 | tf_op jit(solution)/shard_map/ppermute | solution.py:581
  26.4 7.9 %collective-permute-start.4 = (bf16[64,2944]{1,0:T(8,128)(2,1)S(1)}, bf16[64,2944]{1,0:T(8,128)(2,1)S(1)}, u32[]{:S(2)}, u32[]{:S(2)}) collective-permute-start(bf16[64,2944]{1,0:T(8,128)(2,1)S(1)} %constant_dynamic-update-slice_fusion.after_ref.refs_0_), channel_id=1, source_target_pairs={{0,4},{1,5},{2,3},{3,2},{4,0},{5,1},{6,7},{7,6},{8,12},{9,13},{10,... | collective-permute-start | bytes 1130504 | tf_op jit(solution)/shard_map/ppermute | solution.py:592
  28.0 3.4 %copy-start = (bf16[1,2880,1440]{1,2,0:T(8,128)(2,1)S(1)}, bf16[1,2880,1440]{1,2,0:T(8,128)(2,1)}, u32[]{:S(2)}) copy-start(bf16[1,2880,1440]{1,2,0:T(8,128)(2,1)} %param.30) | copy-start | bytes 24883204
  31.4 14.8 %copy-start.3 = (bf16[1,1440]{1,0:T(2,128)(2,1)S(1)}, bf16[1,1440]{1,0:T(2,128)(2,1)}, u32[]{:S(2)}) copy-start(bf16[1,1440]{1,0:T(2,128)(2,1)} %refs_11_.1) | copy-start | bytes 8644
  31.4 14.8 %copy-start.4 = (bf16[1,1440]{1,0:T(2,128)(2,1)S(1)}, bf16[1,1440]{1,0:T(2,128)(2,1)}, u32[]{:S(2)}) copy-start(bf16[1,1440]{1,0:T(2,128)(2,1)} %refs_12_.1) | copy-start | bytes 8644
  32.7 8.9 %collective-permute-start.5 = (bf16[64,2944]{1,0:T(8,128)(2,1)S(1)}, bf16[64,2944]{1,0:T(8,128)(2,1)S(1)}, u32[]{:S(2)}, u32[]{:S(2)}) collective-permute-start(bf16[64,2944]{1,0:T(8,128)(2,1)S(1)} %constant_dynamic-update-slice_fusion.after_ref.refs_0_), channel_id=1, source_target_pairs={{0,1},{1,0},{2,6},{3,7},{4,5},{5,4},{6,2},{7,3},{8,9},{9,8},{10,14... | collective-permute-start | bytes 1130504 | tf_op jit(solution)/shard_map/ppermute | solution.py:592
  34.3 10.1 %collective-permute-start.6 = (bf16[64,2944]{1,0:T(8,128)(2,1)S(1)}, bf16[64,2944]{1,0:T(8,128)(2,1)S(1)}, u32[]{:S(2)}, u32[]{:S(2)}) collective-permute-start(bf16[64,2944]{1,0:T(8,128)(2,1)S(1)} %collective-permute-done.4.refs_1_), channel_id=1, source_target_pairs={{0,1},{1,0},{2,6},{3,7},{4,5},{5,4},{6,2},{7,3},{8,9},{9,8},{10,14... | collective-permute-start | bytes 1130504 | tf_op jit(solution)/shard_map/ppermute | solution.py:592
  36.3 8.2 %collective-permute-start.7 = (bf16[64,2944]{1,0:T(8,128)(2,1)S(1)}, bf16[64,2944]{1,0:T(8,128)(2,1)S(1)}, u32[]{:S(2)}, u32[]{:S(2)}) collective-permute-start(bf16[64,2944]{1,0:T(8,128)(2,1)S(1)} %constant_dynamic-update-slice_fusion.after_ref.refs_0_), channel_id=1, source_target_pairs={{0,2},{1,3},{2,0},{3,1},{4,6},{5,7},{6,4},{7,5},{8,10},{9,11},{10,... | collective-permute-start | bytes 1130504 | tf_op jit(solution)/shard_map/ppermute | solution.py:581
  36.3 3.4 %copy-start.1 = (bf16[1,1440,2880]{2,1,0:T(8,128)(2,1)S(1)}, bf16[1,1440,2880]{2,1,0:T(8,128)(2,1)}, u32[]{:S(2)}) copy-start(bf16[1,1440,2880]{2,1,0:T(8,128)(2,1)} %param.32) | copy-start | bytes 24883204
  41.0 3.4 %collective-permute-start.8 = (bf16[64,2944]{1,0:T(8,128)(2,1)S(1)}, bf16[64,2944]{1,0:T(8,128)(2,1)S(1)}, u32[]{:S(2)}, u32[]{:S(2)}) collective-permute-start(bf16[64,2944]{1,0:T(8,128)(2,1)S(1)} %collective-permute-done.4.refs_1_), channel_id=1, source_target_pairs={{0,2},{1,3},{2,0},{3,1},{4,6},{5,7},{6,4},{7,5},{8,10},{9,11},{10,... | collective-permute-start | bytes 1130504 | tf_op jit(solution)/shard_map/ppermute | solution.py:581
  41.6 2.8 %collective-permute-start.9 = (bf16[64,2944]{1,0:T(8,128)(2,1)S(1)}, bf16[64,2944]{1,0:T(8,128)(2,1)S(1)}, u32[]{:S(2)}, u32[]{:S(2)}) collective-permute-start(bf16[64,2944]{1,0:T(8,128)(2,1)S(1)} %collective-permute-done.5.refs_2_), channel_id=1, source_target_pairs={{0,2},{1,3},{2,0},{3,1},{4,6},{5,7},{6,4},{7,5},{8,10},{9,11},{10,... | collective-permute-start | bytes 1130504 | tf_op jit(solution)/shard_map/ppermute | solution.py:581
  44.5 1.7 %collective-permute-start.10 = (bf16[64,2944]{1,0:T(8,128)(2,1)S(1)}, bf16[64,2944]{1,0:T(8,128)(2,1)S(1)}, u32[]{:S(2)}, u32[]{:S(2)}) collective-permute-start(bf16[64,2944]{1,0:T(8,128)(2,1)S(1)} %collective-permute-done.6.refs_3_), channel_id=1, source_target_pairs={{0,2},{1,3},{2,0},{3,1},{4,6},{5,7},{6,4},{7,5},{8,10},{9,11},{10,... | collective-permute-start | bytes 1130504 | tf_op jit(solution)/shard_map/ppermute | solution.py:581
  56.0 1.8 %collective-permute-start.12 = (bf16[64,2880]{1,0:T(8,128)(2,1)S(1)}, bf16[64,2880]{1,0:T(8,128)(2,1)S(1)}, u32[]{:S(2)}, u32[]{:S(2)}) collective-permute-start(bf16[64,2880]{1,0:T(8,128)(2,1)S(1)} %get-tuple-element.48), channel_id=1, source_target_pairs={{0,2},{1,3},{2,0},{3,1},{4,6},{5,7},{6,4},{7,5},{8,10},{9,11},{10,... | collective-permute-start | bytes 1105928 | tf_op jit(solution)/shard_map/ppermute | solution.py:581
  56.2 4.9 %collective-permute-start.11 = (bf16[64,2880]{1,0:T(8,128)(2,1)S(1)}, bf16[64,2880]{1,0:T(8,128)(2,1)S(1)}, u32[]{:S(2)}, u32[]{:S(2)}) collective-permute-start(bf16[64,2880]{1,0:T(8,128)(2,1)S(1)} %get-tuple-element.46), channel_id=1, source_target_pairs={{0,2},{1,3},{2,0},{3,1},{4,6},{5,7},{6,4},{7,5},{8,10},{9,11},{10,... | collective-permute-start | bytes 1105928 | tf_op jit(solution)/shard_map/ppermute | solution.py:581
  56.6 9.7 %collective-permute-start.17 = (bf16[64,2880]{1,0:T(8,128)(2,1)S(1)}, bf16[64,2880]{1,0:T(8,128)(2,1)S(1)}, u32[]{:S(2)}, u32[]{:S(2)}) collective-permute-start(bf16[64,2880]{1,0:T(8,128)(2,1)S(1)} %get-tuple-element.50), channel_id=1, source_target_pairs={{0,2},{1,3},{2,0},{3,1},{4,6},{5,7},{6,4},{7,5},{8,10},{9,11},{10,... | collective-permute-start | bytes 1105928 | tf_op jit(solution)/shard_map/ppermute | solution.py:581
  56.7 2.7 %collective-permute-start.18 = (bf16[64,2880]{1,0:T(8,128)(2,1)S(1)}, bf16[64,2880]{1,0:T(8,128)(2,1)S(1)}, u32[]{:S(2)}, u32[]{:S(2)}) collective-permute-start(bf16[64,2880]{1,0:T(8,128)(2,1)S(1)} %get-tuple-element.52), channel_id=1, source_target_pairs={{0,2},{1,3},{2,0},{3,1},{4,6},{5,7},{6,4},{7,5},{8,10},{9,11},{10,... | collective-permute-start | bytes 1105928 | tf_op jit(solution)/shard_map/ppermute | solution.py:581
  57.8 7.7 %collective-permute-start.13 = (bf16[64,2880]{1,0:T(8,128)(2,1)S(1)}, bf16[64,2880]{1,0:T(8,128)(2,1)S(1)}, u32[]{:S(2)}, u32[]{:S(2)}) collective-permute-start(bf16[64,2880]{1,0:T(8,128)(2,1)S(1)} %add_convert_fusion.4), channel_id=1, source_target_pairs={{0,1},{1,0},{2,6},{3,7},{4,5},{5,4},{6,2},{7,3},{8,9},{9,8},{10,14... | collective-permute-start | bytes 1105928 | tf_op jit(solution)/shard_map/ppermute | solution.py:592
  59.5 11.9 %collective-permute-start.19 = (bf16[64,2880]{1,0:T(8,128)(2,1)S(1)}, bf16[64,2880]{1,0:T(8,128)(2,1)S(1)}, u32[]{:S(2)}, u32[]{:S(2)}) collective-permute-start(bf16[64,2880]{1,0:T(8,128)(2,1)S(1)} %add_convert_fusion.1), channel_id=1, source_target_pairs={{0,1},{1,0},{2,6},{3,7},{4,5},{5,4},{6,2},{7,3},{8,9},{9,8},{10,14... | collective-permute-start | bytes 1105928 | tf_op jit(solution)/shard_map/ppermute | solution.py:592
  65.7 6.5 %collective-permute-start.14 = (bf16[32,2880]{1,0:T(8,128)(2,1)S(1)}, bf16[32,2880]{1,0:T(8,128)(2,1)S(1)}, u32[]{:S(2)}, u32[]{:S(2)}) collective-permute-start(bf16[32,2880]{1,0:T(8,128)(2,1)S(1)} %slice.33), channel_id=1, source_target_pairs={{0,4},{1,5},{2,3},{3,2},{4,0},{5,1},{6,7},{7,6},{8,12},{9,13},{10,... | collective-permute-start | bytes 552968 | tf_op jit(solution)/shard_map/ppermute | solution.py:592
  71.6 5.6 %collective-permute-start.20 = (bf16[32,2880]{1,0:T(8,128)(2,1)S(1)}, bf16[32,2880]{1,0:T(8,128)(2,1)S(1)}, u32[]{:S(2)}, u32[]{:S(2)}) collective-permute-start(bf16[32,2880]{1,0:T(8,128)(2,1)S(1)} %slice.37), channel_id=1, source_target_pairs={{0,4},{1,5},{2,3},{3,2},{4,0},{5,1},{6,7},{7,6},{8,12},{9,13},{10,... | collective-permute-start | bytes 552968 | tf_op jit(solution)/shard_map/ppermute | solution.py:592
  72.3 9.4 %collective-permute-start.15 = (bf16[16,2880]{1,0:T(8,128)(2,1)S(1)}, bf16[16,2880]{1,0:T(8,128)(2,1)S(1)}, u32[]{:S(2)}, u32[]{:S(2)}) collective-permute-start(bf16[16,2880]{1,0:T(8,128)(2,1)S(1)} %get-tuple-element.54), channel_id=1, source_target_pairs={{0,16},{1,17},{2,18},{3,19},{4,20},{5,21},{6,22},{7,23},{8,24},{9,... | collective-permute-start | bytes 276488 | tf_op jit(solution)/shard_map/ppermute | solution.py:581
  72.8 8.9 %collective-permute-start.16 = (bf16[16,2880]{1,0:T(8,128)(2,1)S(1)}, bf16[16,2880]{1,0:T(8,128)(2,1)S(1)}, u32[]{:S(2)}, u32[]{:S(2)}) collective-permute-start(bf16[16,2880]{1,0:T(8,128)(2,1)S(1)} %get-tuple-element.55), channel_id=1, source_target_pairs={{0,24},{1,25},{2,26},{3,27},{4,28},{5,29},{6,30},{7,31},{8,16},{9,... | collective-permute-start | bytes 276488 | tf_op jit(solution)/shard_map/ppermute | solution.py:581
  77.3 5.0 %collective-permute-start.21 = (bf16[16,2880]{1,0:T(8,128)(2,1)S(1)}, bf16[16,2880]{1,0:T(8,128)(2,1)S(1)}, u32[]{:S(2)}, u32[]{:S(2)}) collective-permute-start(bf16[16,2880]{1,0:T(8,128)(2,1)S(1)} %slice.39), channel_id=1, source_target_pairs={{0,8},{1,9},{2,10},{3,11},{4,12},{5,13},{6,14},{7,15},{8,0},{9,1},... | collective-permute-start | bytes 276488 | tf_op jit(solution)/shard_map/ppermute | solution.py:581

commit v8 on v7

--- a/solution.py
+++ b/solution.py
@@ -11,7 +11,7 @@
 HEAD = 64
 PAGE_LEN = 16
 LANES = 128
-DOWN_STEP = 512
+DOWN_STEP = 768
 VMEM_LIMIT = 60 * 2**20
 LOAD_ROWS = 480
 

time: 83.3 us -> 83.3 us (level)
  no operation moved by 1% of the time
where the time goes in v8:
time: 83.3 us; the launch traced here: 83 us
  waiting for transfers between devices  24.9 us (30%)
  Pallas kernels  24.8 us (30%)
  starting transfers between devices  23.3 us (28%)
  local copies, waits for them, and re-layouts  6.96 us (8%)
  other arithmetic  2.2 us (3%)
  between operations  0.86 us (1%)
    ppermute x15, starting transfers between devices, moved(): return lax.ppermute(array, AXES, pairs)  13.9 us
    ppermute x7, waiting for transfers between devices, crossed(): return lax.ppermute(array, AXES, pairs)  13.3 us
    ppermute x15, waiting for transfers between devices, moved(): return lax.ppermute(array, AXES, pairs)  11.6 us
    pallas_call x1, Pallas kernels, run_expert(): pl.pallas_call(functools.partial(expert_kernel, parts, block, limit, 512)...  9.84 us
    ppermute x7, starting transfers between devices, crossed(): return lax.ppermute(array, AXES, pairs)  9.37 us
    pallas_call x1, Pallas kernels, run_attention(): pl.pallas_call(attention_kernel, out_shape=[jax.ShapeDtypeStruct((half, w...  8.32 us
    unnamed x23, local copies, waits for them, and re-layouts  6.88 us
    pallas_call x3, Pallas kernels, load(): pl.pallas_call(load_kernel, out_shape=[jax.ShapeDtypeStruct(weight.shape,...  6.22 us
  transfers between devices with their start and end apart: 22, of which 11 were waited for; matrix products, arithmetic and copies ran while one was open for 2% of the time, Pallas kernels for 7%

profile of v8, /device:TPU:0, one launch (start us, length us, event | category | flops | bytes accessed | tf_op | source)
XLA Modules:
  0.0 83.0 jit_solution(4147522545812711266)
XLA Ops:
  0.7 8.3 %attention.1 = (f32[16,2880]{1,0:T(8,128)}, bf16[16,2880]{1,0:T(8,128)(2,1)}, bf16[2,16,512]{2,1,0:T(8,128)(2,1)}, s32[1]{0:T(128)}) custom-call(s32[1]{0:T(128)} %bitcast.side_ref, s32[1]{0:T(128)} %bitcast.1.expert_in_ref, s32[1,2]{1,0:T(1,128)} %pages_ref.1, f32[32]{0:T(128)} %sink_ref.1, bf16[32,2048]{1,0:T(8,128)(2,1)} %queries_ref.1, ...), custom_call_target="tpu_custom_call" | custom-call | tf_op jit(solution)/shard_map/attention/pallas_call | solution.py:504
  9.0 3.0 %collective-permute-start = (bf16[16,2880]{1,0:T(8,128)(2,1)}, bf16[16,2880]{1,0:T(8,128)(2,1)S(1)}, u32[]{:S(2)}, u32[]{:S(2)}) collective-permute-start(bf16[16,2880]{1,0:T(8,128)(2,1)} %get-tuple-element.29), channel_id=1, source_target_pairs={{0,1},{1,0},{2,3},{3,2},{4,5},{5,4},{6,7},{7,6},{8,9},{9,8},{10,11... | collective-permute-start | bytes 276488 | tf_op jit(solution)/shard_map/ppermute | solution.py:581
  12.1 1.0 %add_add_fusion.own_ref = f32[16,2880]{1,0:T(8,128)S(1)} fusion(f32[16,2880]{1,0:T(8,128)} %get-tuple-element.28, bf16[16,2880]{1,0:T(8,128)(2,1)S(1)} %copy-done.7, f32[2880]{0:T(1024)S(1)} %convert_element_type.94), kind=kLoop, calls=%fused_computation.9 | loop fusion | flops 138240 | bytes 472320 | tf_op jit(solution)/shard_map/add | solution.py:680
  13.1 1.9 %collective-permute-done.got_ref = bf16[16,2880]{1,0:T(8,128)(2,1)S(1)} collective-permute-done((bf16[16,2880]{1,0:T(8,128)(2,1)}, bf16[16,2880]{1,0:T(8,128)(2,1)S(1)}, u32[]{:S(2)}, u32[]{:S(2)}) %collective-permute-start) | collective-permute-done | bytes 92192 | tf_op jit(solution)/shard_map/ppermute | solution.py:581
  15.4 4.0 %collective-permute-start.3 = (bf16[16,2944]{1,0:T(8,128)(2,1)S(1)}, bf16[16,2944]{1,0:T(8,128)(2,1)S(1)}, u32[]{:S(2)}, u32[]{:S(2)}) collective-permute-start(bf16[16,2944]{1,0:T(8,128)(2,1)S(1)} %get-tuple-element.32.after_ref), channel_id=1, source_target_pairs={{0,24},{1,25},{2,26},{3,27},{4,28},{5,29},{6,30},{7,31},{8,16},{9,... | collective-permute-start | bytes 282632 | tf_op jit(solution)/shard_map/ppermute | solution.py:581
  19.4 0.6 collective-permute-start.1
  20.1 3.5 %load.3 = (bf16[1440,2880]{1,0:T(8,128)(2,1)S(1)}, bf16[16,128]{1,0:T(8,128)(2,1)S(1)}) custom-call(bf16[16,2944]{1,0:T(8,128)(2,1)S(1)} %get-tuple-element.32.after_ref, bf16[1440,2880]{1,0:T(8,128)(2,1)} %bitcast.18), custom_call_target="tpu_custom_call" | custom-call | bytes 16588800 | tf_op jit(solution)/shard_map/load/pallas_call | solution.py:282
  23.6 0.7 collective-permute-done.1
  24.3 2.0 %collective-permute-done.2 = bf16[16,2944]{1,0:T(8,128)(2,1)S(1)} collective-permute-done((bf16[16,2944]{1,0:T(8,128)(2,1)S(1)}, bf16[16,2944]{1,0:T(8,128)(2,1)S(1)}, u32[]{:S(2)}, u32[]{:S(2)}) %collective-permute-start.2) | collective-permute-done | bytes 94240 | tf_op jit(solution)/shard_map/ppermute | solution.py:581
  26.4 1.6 %collective-permute-start.4 = (bf16[64,2944]{1,0:T(8,128)(2,1)S(1)}, bf16[64,2944]{1,0:T(8,128)(2,1)S(1)}, u32[]{:S(2)}, u32[]{:S(2)}) collective-permute-start(bf16[64,2944]{1,0:T(8,128)(2,1)S(1)} %constant_dynamic-update-slice_fusion.after_ref.refs_0_), channel_id=1, source_target_pairs={{0,4},{1,5},{2,3},{3,2},{4,0},{5,1},{6,7},{7,6},{8,12},{9,13},{10,... | collective-permute-start | bytes 1130504 | tf_op jit(solution)/shard_map/ppermute | solution.py:592
  28.0 3.4 %copy-done = bf16[1,2880,1440]{1,2,0:T(8,128)(2,1)S(1)} copy-done((bf16[1,2880,1440]{1,2,0:T(8,128)(2,1)S(1)}, bf16[1,2880,1440]{1,2,0:T(8,128)(2,1)}, u32[]{:S(2)}) %copy-start) | copy-done | bytes 8294424
  31.4 1.4 %load.4 = (bf16[1440,2880]{1,0:T(8,128)(2,1)S(1)}, bf16[16,128]{1,0:T(8,128)(2,1)S(1)}) custom-call(bf16[64,2944]{1,0:T(8,128)(2,1)S(1)} %constant_dynamic-update-slice_fusion.after_ref.refs_0_, bf16[1440,2880]{1,0:T(8,128)(2,1)S(1)} %bitcast.13), custom_call_target="tpu_custom_call" | custom-call | bytes 16588800 | tf_op jit(solution)/shard_map/load/pallas_call | solution.py:282
  32.7 1.6 %collective-permute-start.5 = (bf16[64,2944]{1,0:T(8,128)(2,1)S(1)}, bf16[64,2944]{1,0:T(8,128)(2,1)S(1)}, u32[]{:S(2)}, u32[]{:S(2)}) collective-permute-start(bf16[64,2944]{1,0:T(8,128)(2,1)S(1)} %constant_dynamic-update-slice_fusion.after_ref.refs_0_), channel_id=1, source_target_pairs={{0,1},{1,0},{2,6},{3,7},{4,5},{5,4},{6,2},{7,3},{8,9},{9,8},{10,14... | collective-permute-start | bytes 1130504 | tf_op jit(solution)/shard_map/ppermute | solution.py:592
  34.3 1.9 %collective-permute-start.6 = (bf16[64,2944]{1,0:T(8,128)(2,1)S(1)}, bf16[64,2944]{1,0:T(8,128)(2,1)S(1)}, u32[]{:S(2)}, u32[]{:S(2)}) collective-permute-start(bf16[64,2944]{1,0:T(8,128)(2,1)S(1)} %collective-permute-done.4.refs_1_), channel_id=1, source_target_pairs={{0,1},{1,0},{2,6},{3,7},{4,5},{5,4},{6,2},{7,3},{8,9},{9,8},{10,14... | collective-permute-start | bytes 1130504 | tf_op jit(solution)/shard_map/ppermute | solution.py:592
  36.3 3.4 %copy-done.1 = bf16[1,1440,2880]{2,1,0:T(8,128)(2,1)S(1)} copy-done((bf16[1,1440,2880]{2,1,0:T(8,128)(2,1)S(1)}, bf16[1,1440,2880]{2,1,0:T(8,128)(2,1)}, u32[]{:S(2)}) %copy-start.1) | copy-done | bytes 8294424
  39.7 1.4 %load.5 = (bf16[1440,2880]{1,0:T(8,128)(2,1)S(1)}, bf16[16,128]{1,0:T(8,128)(2,1)S(1)}) custom-call(bf16[64,2944]{1,0:T(8,128)(2,1)S(1)} %constant_dynamic-update-slice_fusion.after_ref.refs_0_, bf16[1440,2880]{1,0:T(8,128)(2,1)S(1)} %bitcast.14), custom_call_target="tpu_custom_call" | custom-call | bytes 16588800 | tf_op jit(solution)/shard_map/load/pallas_call | solution.py:282
  41.0 0.6 collective-permute-start.8
  41.7 2.7 %collective-permute-done.6.refs_3_ = bf16[64,2944]{1,0:T(8,128)(2,1)S(1)} collective-permute-done((bf16[64,2944]{1,0:T(8,128)(2,1)S(1)}, bf16[64,2944]{1,0:T(8,128)(2,1)S(1)}, u32[]{:S(2)}, u32[]{:S(2)}) %collective-permute-start.6) | collective-permute-done | bytes 376864 | tf_op jit(solution)/shard_map/ppermute | solution.py:592
  44.5 1.7 %collective-permute-done.10.refs_7_ = bf16[64,2944]{1,0:T(8,128)(2,1)S(1)} collective-permute-done((bf16[64,2944]{1,0:T(8,128)(2,1)S(1)}, bf16[64,2944]{1,0:T(8,128)(2,1)S(1)}, u32[]{:S(2)}, u32[]{:S(2)}) %collective-permute-start.10) | collective-permute-done | bytes 376864 | tf_op jit(solution)/shard_map/ppermute | solution.py:581
  46.2 9.8 %expert.1 = (bf16[64,2880]{1,0:T(8,128)(2,1)S(1)}, bf16[64,2880]{1,0:T(8,128)(2,1)S(1)}, bf16[64,2880]{1,0:T(8,128)(2,1)S(1)}, bf16[64,2880]{1,0:T(8,128)(2,1)S(...) custom-call(s32[1]{0:T(128)} %get-tuple-element.31.expert_ref, ...), custom_call_target="tpu_custom_call" | custom-call | flops 6370099200 | bytes 24883200 | tf_op jit(solution)/shard_map/expert/pallas_call | solution.py:551
  57.1 0.7 collective-permute-done.12
  57.9 1.6 %collective-permute-start.13 = (bf16[64,2880]{1,0:T(8,128)(2,1)S(1)}, bf16[64,2880]{1,0:T(8,128)(2,1)S(1)}, u32[]{:S(2)}, u32[]{:S(2)}) collective-permute-start(bf16[64,2880]{1,0:T(8,128)(2,1)S(1)} %add_convert_fusion.4), channel_id=1, source_target_pairs={{0,1},{1,0},{2,6},{3,7},{4,5},{5,4},{6,2},{7,3},{8,9},{9,8},{10,14... | collective-permute-start | bytes 1105928 | tf_op jit(solution)/shard_map/ppermute | solution.py:592
  59.5 1.5 %collective-permute-start.19 = (bf16[64,2880]{1,0:T(8,128)(2,1)S(1)}, bf16[64,2880]{1,0:T(8,128)(2,1)S(1)}, u32[]{:S(2)}, u32[]{:S(2)}) collective-permute-start(bf16[64,2880]{1,0:T(8,128)(2,1)S(1)} %add_convert_fusion.1), channel_id=1, source_target_pairs={{0,1},{1,0},{2,6},{3,7},{4,5},{5,4},{6,2},{7,3},{8,9},{9,8},{10,14... | collective-permute-start | bytes 1105928 | tf_op jit(solution)/shard_map/ppermute | solution.py:592
  61.1 4.5 %collective-permute-done.13 = bf16[64,2880]{1,0:T(8,128)(2,1)S(1)} collective-permute-done((bf16[64,2880]{1,0:T(8,128)(2,1)S(1)}, bf16[64,2880]{1,0:T(8,128)(2,1)S(1)}, u32[]{:S(2)}, u32[]{:S(2)}) %collective-permute-start.13) | collective-permute-done | bytes 368672 | tf_op jit(solution)/shard_map/ppermute | solution.py:592
  65.7 0.6 collective-permute-start.14
  66.3 5.1 %collective-permute-done.19 = bf16[64,2880]{1,0:T(8,128)(2,1)S(1)} collective-permute-done((bf16[64,2880]{1,0:T(8,128)(2,1)S(1)}, bf16[64,2880]{1,0:T(8,128)(2,1)S(1)}, u32[]{:S(2)}, u32[]{:S(2)}) %collective-permute-start.19) | collective-permute-done | bytes 368672 | tf_op jit(solution)/shard_map/ppermute | solution.py:592
  71.6 0.6 collective-permute-start.20
  72.8 3.5 %collective-permute-start.16 = (bf16[16,2880]{1,0:T(8,128)(2,1)S(1)}, bf16[16,2880]{1,0:T(8,128)(2,1)S(1)}, u32[]{:S(2)}, u32[]{:S(2)}) collective-permute-start(bf16[16,2880]{1,0:T(8,128)(2,1)S(1)} %get-tuple-element.55), channel_id=1, source_target_pairs={{0,24},{1,25},{2,26},{3,27},{4,28},{5,29},{6,30},{7,31},{8,16},{9,... | collective-permute-start | bytes 276488 | tf_op jit(solution)/shard_map/ppermute | solution.py:581
  76.2 1.0 %collective-permute-done.20 = bf16[32,2880]{1,0:T(8,128)(2,1)S(1)} collective-permute-done((bf16[32,2880]{1,0:T(8,128)(2,1)S(1)}, bf16[32,2880]{1,0:T(8,128)(2,1)S(1)}, u32[]{:S(2)}, u32[]{:S(2)}) %collective-permute-start.20) | collective-permute-done | bytes 184352 | tf_op jit(solution)/shard_map/ppermute | solution.py:592
  77.8 3.9 %collective-permute-done.15 = bf16[16,2880]{1,0:T(8,128)(2,1)S(1)} collective-permute-done((bf16[16,2880]{1,0:T(8,128)(2,1)S(1)}, bf16[16,2880]{1,0:T(8,128)(2,1)S(1)}, u32[]{:S(2)}, u32[]{:S(2)}) %collective-permute-start.15) | collective-permute-done | bytes 92192 | tf_op jit(solution)/shard_map/ppermute | solution.py:581
  81.7 0.6 collective-permute-done.21
  82.3 0.7 add_convert_fusion.8
  (56 shorter events, 3.4 us)
Async XLA Ops:
  0.6 11.4 %copy-start.9 = (bf16[2880]{0:T(1024)(128)(2,1)S(1)}, bf16[2880]{0:T(1024)(128)(2,1)}, u32[]{:S(2)}) copy-start(bf16[2880]{0:T(1024)(128)(2,1)} %param.23) | copy-start | bytes 17284
  0.6 11.4 %copy-start.7 = (bf16[16,2880]{1,0:T(8,128)(2,1)S(1)}, bf16[16,2880]{1,0:T(8,128)(2,1)}, u32[]{:S(2)}) copy-start(bf16[16,2880]{1,0:T(8,128)(2,1)} %param.24) | copy-start | bytes 276484
  0.7 12.4 %copy-start.8 = (bf16[2880]{0:T(1024)(128)(2,1)S(1)}, bf16[2880]{0:T(1024)(128)(2,1)}, u32[]{:S(2)}) copy-start(bf16[2880]{0:T(1024)(128)(2,1)} %param.25) | copy-start | bytes 17284
  0.7 14.3 %copy-start.2 = (bf16[16,2880]{1,0:T(8,128)(2,1)S(1)}, bf16[16,2880]{1,0:T(8,128)(2,1)}, u32[]{:S(2)}) copy-start(bf16[16,2880]{1,0:T(8,128)(2,1)} %down_bias_ref.1) | copy-start | bytes 276484
  0.7 14.3 %copy-start.6 = (f32[16,4]{0,1:T(4,128)S(1)}, f32[16,4]{0,1:T(4,128)}, u32[]{:S(2)}) copy-start(f32[16,4]{0,1:T(4,128)} %param.27) | copy-start | bytes 772
  0.7 14.3 %copy-start.5 = (s32[16,4]{0,1:T(4,128)S(1)}, s32[16,4]{0,1:T(4,128)}, u32[]{:S(2)}) copy-start(s32[16,4]{0,1:T(4,128)} %param.26) | copy-start | bytes 772
  9.0 6.0 %collective-permute-start = (bf16[16,2880]{1,0:T(8,128)(2,1)}, bf16[16,2880]{1,0:T(8,128)(2,1)S(1)}, u32[]{:S(2)}, u32[]{:S(2)}) collective-permute-start(bf16[16,2880]{1,0:T(8,128)(2,1)} %get-tuple-element.29), channel_id=1, source_target_pairs={{0,1},{1,0},{2,3},{3,2},{4,5},{5,4},{6,7},{7,6},{8,9},{9,8},{10,11... | collective-permute-start | bytes 276488 | tf_op jit(solution)/shard_map/ppermute | solution.py:581
  15.4 11.0 %collective-permute-start.3 = (bf16[16,2944]{1,0:T(8,128)(2,1)S(1)}, bf16[16,2944]{1,0:T(8,128)(2,1)S(1)}, u32[]{:S(2)}, u32[]{:S(2)}) collective-permute-start(bf16[16,2944]{1,0:T(8,128)(2,1)S(1)} %get-tuple-element.32.after_ref), channel_id=1, source_target_pairs={{0,24},{1,25},{2,26},{3,27},{4,28},{5,29},{6,30},{7,31},{8,16},{9,... | collective-permute-start | bytes 282632 | tf_op jit(solution)/shard_map/ppermute | solution.py:581
  19.4 6.9 %collective-permute-start.2 = (bf16[16,2944]{1,0:T(8,128)(2,1)S(1)}, bf16[16,2944]{1,0:T(8,128)(2,1)S(1)}, u32[]{:S(2)}, u32[]{:S(2)}) collective-permute-start(bf16[16,2944]{1,0:T(8,128)(2,1)S(1)} %get-tuple-element.32.after_ref), channel_id=1, source_target_pairs={{0,16},{1,17},{2,18},{3,19},{4,20},{5,21},{6,22},{7,23},{8,24},{9,... | collective-permute-start | bytes 282632 | tf_op jit(solution)/shard_map/ppermute | solution.py:581
  19.4 4.9 %collective-permute-start.1 = (bf16[16,2944]{1,0:T(8,128)(2,1)S(1)}, bf16[16,2944]{1,0:T(8,128)(2,1)S(1)}, u32[]{:S(2)}, u32[]{:S(2)}) collective-permute-start(bf16[16,2944]{1,0:T(8,128)(2,1)S(1)} %get-tuple-element.32.after_ref), channel_id=1, source_target_pairs={{0,8},{1,9},{2,10},{3,11},{4,12},{5,13},{6,14},{7,15},{8,0},{9,1},... | collective-permute-start | bytes 282632 | tf_op jit(solution)/shard_map/ppermute | solution.py:581
  26.4 7.9 %collective-permute-start.4 = (bf16[64,2944]{1,0:T(8,128)(2,1)S(1)}, bf16[64,2944]{1,0:T(8,128)(2,1)S(1)}, u32[]{:S(2)}, u32[]{:S(2)}) collective-permute-start(bf16[64,2944]{1,0:T(8,128)(2,1)S(1)} %constant_dynamic-update-slice_fusion.after_ref.refs_0_), channel_id=1, source_target_pairs={{0,4},{1,5},{2,3},{3,2},{4,0},{5,1},{6,7},{7,6},{8,12},{9,13},{10,... | collective-permute-start | bytes 1130504 | tf_op jit(solution)/shard_map/ppermute | solution.py:592
  28.0 3.4 %copy-start = (bf16[1,2880,1440]{1,2,0:T(8,128)(2,1)S(1)}, bf16[1,2880,1440]{1,2,0:T(8,128)(2,1)}, u32[]{:S(2)}) copy-start(bf16[1,2880,1440]{1,2,0:T(8,128)(2,1)} %param.30) | copy-start | bytes 24883204
  31.4 14.8 %copy-start.3 = (bf16[1,1440]{1,0:T(2,128)(2,1)S(1)}, bf16[1,1440]{1,0:T(2,128)(2,1)}, u32[]{:S(2)}) copy-start(bf16[1,1440]{1,0:T(2,128)(2,1)} %refs_11_.1) | copy-start | bytes 8644
  31.4 14.8 %copy-start.4 = (bf16[1,1440]{1,0:T(2,128)(2,1)S(1)}, bf16[1,1440]{1,0:T(2,128)(2,1)}, u32[]{:S(2)}) copy-start(bf16[1,1440]{1,0:T(2,128)(2,1)} %refs_12_.1) | copy-start | bytes 8644
  32.7 8.9 %collective-permute-start.5 = (bf16[64,2944]{1,0:T(8,128)(2,1)S(1)}, bf16[64,2944]{1,0:T(8,128)(2,1)S(1)}, u32[]{:S(2)}, u32[]{:S(2)}) collective-permute-start(bf16[64,2944]{1,0:T(8,128)(2,1)S(1)} %constant_dynamic-update-slice_fusion.after_ref.refs_0_), channel_id=1, source_target_pairs={{0,1},{1,0},{2,6},{3,7},{4,5},{5,4},{6,2},{7,3},{8,9},{9,8},{10,14... | collective-permute-start | bytes 1130504 | tf_op jit(solution)/shard_map/ppermute | solution.py:592
  34.3 10.1 %collective-permute-start.6 = (bf16[64,2944]{1,0:T(8,128)(2,1)S(1)}, bf16[64,2944]{1,0:T(8,128)(2,1)S(1)}, u32[]{:S(2)}, u32[]{:S(2)}) collective-permute-start(bf16[64,2944]{1,0:T(8,128)(2,1)S(1)} %collective-permute-done.4.refs_1_), channel_id=1, source_target_pairs={{0,1},{1,0},{2,6},{3,7},{4,5},{5,4},{6,2},{7,3},{8,9},{9,8},{10,14... | collective-permute-start | bytes 1130504 | tf_op jit(solution)/shard_map/ppermute | solution.py:592
  36.3 8.2 %collective-permute-start.7 = (bf16[64,2944]{1,0:T(8,128)(2,1)S(1)}, bf16[64,2944]{1,0:T(8,128)(2,1)S(1)}, u32[]{:S(2)}, u32[]{:S(2)}) collective-permute-start(bf16[64,2944]{1,0:T(8,128)(2,1)S(1)} %constant_dynamic-update-slice_fusion.after_ref.refs_0_), channel_id=1, source_target_pairs={{0,2},{1,3},{2,0},{3,1},{4,6},{5,7},{6,4},{7,5},{8,10},{9,11},{10,... | collective-permute-start | bytes 1130504 | tf_op jit(solution)/shard_map/ppermute | solution.py:581
  36.3 3.4 %copy-start.1 = (bf16[1,1440,2880]{2,1,0:T(8,128)(2,1)S(1)}, bf16[1,1440,2880]{2,1,0:T(8,128)(2,1)}, u32[]{:S(2)}) copy-start(bf16[1,1440,2880]{2,1,0:T(8,128)(2,1)} %param.32) | copy-start | bytes 24883204
  41.0 3.4 %collective-permute-start.8 = (bf16[64,2944]{1,0:T(8,128)(2,1)S(1)}, bf16[64,2944]{1,0:T(8,128)(2,1)S(1)}, u32[]{:S(2)}, u32[]{:S(2)}) collective-permute-start(bf16[64,2944]{1,0:T(8,128)(2,1)S(1)} %collective-permute-done.4.refs_1_), channel_id=1, source_target_pairs={{0,2},{1,3},{2,0},{3,1},{4,6},{5,7},{6,4},{7,5},{8,10},{9,11},{10,... | collective-permute-start | bytes 1130504 | tf_op jit(solution)/shard_map/ppermute | solution.py:581
  41.6 2.8 %collective-permute-start.9 = (bf16[64,2944]{1,0:T(8,128)(2,1)S(1)}, bf16[64,2944]{1,0:T(8,128)(2,1)S(1)}, u32[]{:S(2)}, u32[]{:S(2)}) collective-permute-start(bf16[64,2944]{1,0:T(8,128)(2,1)S(1)} %collective-permute-done.5.refs_2_), channel_id=1, source_target_pairs={{0,2},{1,3},{2,0},{3,1},{4,6},{5,7},{6,4},{7,5},{8,10},{9,11},{10,... | collective-permute-start | bytes 1130504 | tf_op jit(solution)/shard_map/ppermute | solution.py:581
  44.5 1.7 %collective-permute-start.10 = (bf16[64,2944]{1,0:T(8,128)(2,1)S(1)}, bf16[64,2944]{1,0:T(8,128)(2,1)S(1)}, u32[]{:S(2)}, u32[]{:S(2)}) collective-permute-start(bf16[64,2944]{1,0:T(8,128)(2,1)S(1)} %collective-permute-done.6.refs_3_), channel_id=1, source_target_pairs={{0,2},{1,3},{2,0},{3,1},{4,6},{5,7},{6,4},{7,5},{8,10},{9,11},{10,... | collective-permute-start | bytes 1130504 | tf_op jit(solution)/shard_map/ppermute | solution.py:581
  56.0 1.8 %collective-permute-start.12 = (bf16[64,2880]{1,0:T(8,128)(2,1)S(1)}, bf16[64,2880]{1,0:T(8,128)(2,1)S(1)}, u32[]{:S(2)}, u32[]{:S(2)}) collective-permute-start(bf16[64,2880]{1,0:T(8,128)(2,1)S(1)} %get-tuple-element.48), channel_id=1, source_target_pairs={{0,2},{1,3},{2,0},{3,1},{4,6},{5,7},{6,4},{7,5},{8,10},{9,11},{10,... | collective-permute-start | bytes 1105928 | tf_op jit(solution)/shard_map/ppermute | solution.py:581
  56.2 4.9 %collective-permute-start.11 = (bf16[64,2880]{1,0:T(8,128)(2,1)S(1)}, bf16[64,2880]{1,0:T(8,128)(2,1)S(1)}, u32[]{:S(2)}, u32[]{:S(2)}) collective-permute-start(bf16[64,2880]{1,0:T(8,128)(2,1)S(1)} %get-tuple-element.46), channel_id=1, source_target_pairs={{0,2},{1,3},{2,0},{3,1},{4,6},{5,7},{6,4},{7,5},{8,10},{9,11},{10,... | collective-permute-start | bytes 1105928 | tf_op jit(solution)/shard_map/ppermute | solution.py:581
  56.6 9.7 %collective-permute-start.17 = (bf16[64,2880]{1,0:T(8,128)(2,1)S(1)}, bf16[64,2880]{1,0:T(8,128)(2,1)S(1)}, u32[]{:S(2)}, u32[]{:S(2)}) collective-permute-start(bf16[64,2880]{1,0:T(8,128)(2,1)S(1)} %get-tuple-element.50), channel_id=1, source_target_pairs={{0,2},{1,3},{2,0},{3,1},{4,6},{5,7},{6,4},{7,5},{8,10},{9,11},{10,... | collective-permute-start | bytes 1105928 | tf_op jit(solution)/shard_map/ppermute | solution.py:581
  56.7 2.7 %collective-permute-start.18 = (bf16[64,2880]{1,0:T(8,128)(2,1)S(1)}, bf16[64,2880]{1,0:T(8,128)(2,1)S(1)}, u32[]{:S(2)}, u32[]{:S(2)}) collective-permute-start(bf16[64,2880]{1,0:T(8,128)(2,1)S(1)} %get-tuple-element.52), channel_id=1, source_target_pairs={{0,2},{1,3},{2,0},{3,1},{4,6},{5,7},{6,4},{7,5},{8,10},{9,11},{10,... | collective-permute-start | bytes 1105928 | tf_op jit(solution)/shard_map/ppermute | solution.py:581
  57.9 7.7 %collective-permute-start.13 = (bf16[64,2880]{1,0:T(8,128)(2,1)S(1)}, bf16[64,2880]{1,0:T(8,128)(2,1)S(1)}, u32[]{:S(2)}, u32[]{:S(2)}) collective-permute-start(bf16[64,2880]{1,0:T(8,128)(2,1)S(1)} %add_convert_fusion.4), channel_id=1, source_target_pairs={{0,1},{1,0},{2,6},{3,7},{4,5},{5,4},{6,2},{7,3},{8,9},{9,8},{10,14... | collective-permute-start | bytes 1105928 | tf_op jit(solution)/shard_map/ppermute | solution.py:592
  59.5 11.9 %collective-permute-start.19 = (bf16[64,2880]{1,0:T(8,128)(2,1)S(1)}, bf16[64,2880]{1,0:T(8,128)(2,1)S(1)}, u32[]{:S(2)}, u32[]{:S(2)}) collective-permute-start(bf16[64,2880]{1,0:T(8,128)(2,1)S(1)} %add_convert_fusion.1), channel_id=1, source_target_pairs={{0,1},{1,0},{2,6},{3,7},{4,5},{5,4},{6,2},{7,3},{8,9},{9,8},{10,14... | collective-permute-start | bytes 1105928 | tf_op jit(solution)/shard_map/ppermute | solution.py:592
  65.7 6.5 %collective-permute-start.14 = (bf16[32,2880]{1,0:T(8,128)(2,1)S(1)}, bf16[32,2880]{1,0:T(8,128)(2,1)S(1)}, u32[]{:S(2)}, u32[]{:S(2)}) collective-permute-start(bf16[32,2880]{1,0:T(8,128)(2,1)S(1)} %slice.33), channel_id=1, source_target_pairs={{0,4},{1,5},{2,3},{3,2},{4,0},{5,1},{6,7},{7,6},{8,12},{9,13},{10,... | collective-permute-start | bytes 552968 | tf_op jit(solution)/shard_map/ppermute | solution.py:592
  71.6 5.6 %collective-permute-start.20 = (bf16[32,2880]{1,0:T(8,128)(2,1)S(1)}, bf16[32,2880]{1,0:T(8,128)(2,1)S(1)}, u32[]{:S(2)}, u32[]{:S(2)}) collective-permute-start(bf16[32,2880]{1,0:T(8,128)(2,1)S(1)} %slice.37), channel_id=1, source_target_pairs={{0,4},{1,5},{2,3},{3,2},{4,0},{5,1},{6,7},{7,6},{8,12},{9,13},{10,... | collective-permute-start | bytes 552968 | tf_op jit(solution)/shard_map/ppermute | solution.py:592
  72.3 9.4 %collective-permute-start.15 = (bf16[16,2880]{1,0:T(8,128)(2,1)S(1)}, bf16[16,2880]{1,0:T(8,128)(2,1)S(1)}, u32[]{:S(2)}, u32[]{:S(2)}) collective-permute-start(bf16[16,2880]{1,0:T(8,128)(2,1)S(1)} %get-tuple-element.54), channel_id=1, source_target_pairs={{0,16},{1,17},{2,18},{3,19},{4,20},{5,21},{6,22},{7,23},{8,24},{9,... | collective-permute-start | bytes 276488 | tf_op jit(solution)/shard_map/ppermute | solution.py:581
  72.8 8.9 %collective-permute-start.16 = (bf16[16,2880]{1,0:T(8,128)(2,1)S(1)}, bf16[16,2880]{1,0:T(8,128)(2,1)S(1)}, u32[]{:S(2)}, u32[]{:S(2)}) collective-permute-start(bf16[16,2880]{1,0:T(8,128)(2,1)S(1)} %get-tuple-element.55), channel_id=1, source_target_pairs={{0,24},{1,25},{2,26},{3,27},{4,28},{5,29},{6,30},{7,31},{8,16},{9,... | collective-permute-start | bytes 276488 | tf_op jit(solution)/shard_map/ppermute | solution.py:581
  77.3 5.0 %collective-permute-start.21 = (bf16[16,2880]{1,0:T(8,128)(2,1)S(1)}, bf16[16,2880]{1,0:T(8,128)(2,1)S(1)}, u32[]{:S(2)}, u32[]{:S(2)}) collective-permute-start(bf16[16,2880]{1,0:T(8,128)(2,1)S(1)} %slice.39), channel_id=1, source_target_pairs={{0,8},{1,9},{2,10},{3,11},{4,12},{5,13},{6,14},{7,15},{8,0},{9,1},... | collective-permute-start | bytes 276488 | tf_op jit(solution)/shard_map/ppermute | solution.py:581
